TPU v7x, 128 devices: a whole 4x4x4 slice. The times are simulated.
128 devices in a mesh: row: 8 (over x_lo, y), col: 16 (over z, x_hi, core).
Axes of the slice: x: 4 (x_hi: 2, x_lo: 2; x = x_hi * 2 + x_lo), y: 4, z: 4, core: 2. Of those that a mesh axis runs over, the one named last changes fastest.
Arguments:
- child_update_blocks: bfloat16 [8, 16, 128, 16, 8, 128], P('row', None, None, 'col'), may hold values from -4 to 4
- child_pivot_panel: bfloat16 [8, 16, 128, 16, 128], P('row', None, None, 'col'), may hold values from -1 to 1
- child_map: int32 [4, 64], replicated, may hold values from 0 to 127, as said below
- coupled: int32 [120], replicated, may hold values 0 or 1
- parent_front: bfloat16 [8, 16, 128, 16, 8, 128], P('row', None, None, 'col')
Outputs:
- factored: float32 [8, 16, 128, 16, 8, 128], P('row', None, None, 'col')
Inputs may be any that keep to these rules, and one draw needn't show every extreme that they name: `child_map`: the 64 entries of one row are distinct. Each child names exactly 4 parent blocks of each value mod 16; rows 0 and 1 together name every parent block exactly once, and so do rows 2 and 3. For one child and one value of b mod 4, exactly 2 of its blocks b have an entry with each value mod 8; for one child and one value of b mod 8, at most 1 of its blocks b have an entry with one value mod 16, and some value has exactly 1.
All inputs are finite; a program needn't handle non-finite values.
Results may differ from a plain program's by a relative error of at most 0.0015.
The roundings to bfloat16 on the way count: a program that leaves them out, or rounds other values in their place, can miss the bound.
Values may be sent and summed in bfloat16 or wider, within the bound.
A program may use at most 192 MiB of HBM per device.

v0:
```python
import jax
import jax.numpy as jnp
from jax import lax
from jax.sharding import PartitionSpec as P

FRONT_PIVOTS = 1024
BLOCK_ORDER = 128


def from_partner(value, axis, stride):
    mask = 2**stride
    pairs = [(source, source ^ mask) for source in range(lax.axis_size(axis))]
    return lax.ppermute(value, axis, pairs)


def from_root(array, axis, root):
    mine = lax.axis_index(axis) == root
    return lax.psum(jnp.where(mine, array, jnp.zeros_like(array)), axis)


def parent_blocks(child_map, child_index, rank, stride):
    targets = lax.dynamic_index_in_dim(child_map, child_index, 0, keepdims=False)
    grouped = targets.reshape(targets.shape[0] // stride, stride)
    return lax.dynamic_index_in_dim(grouped, rank, 1, keepdims=False)


def slot_match(targets, period, capacity):
    residue = targets % period
    matches = residue[None, :] == jnp.arange(period, dtype=jnp.int32)[:, None]
    ordinal = jnp.cumsum(matches.astype(jnp.int32), axis=1) - 1
    return matches[:, None, :] & (
        ordinal[:, None, :] == jnp.arange(capacity, dtype=jnp.int32)[None, :, None]
    )


def slot_target(targets, period, capacity, owner):
    picked = lax.dynamic_index_in_dim(
        slot_match(targets, period, capacity), owner, 0, keepdims=False
    )
    return jnp.sum(jnp.where(picked, targets[None, :] // period + 1, 0), axis=1) - 1


def arrival_table(
    child_map, grid_rows, grid_cols, cap_rows, cap_cols, my_row, my_col, local_rows, local_cols
):
    half_rows = grid_rows // 2
    half_cols = grid_cols // 2

    def single(source_row, source_col):
        child_index = 2 * (source_row // half_rows) + source_col // half_cols
        row_slots = slot_target(
            parent_blocks(child_map, child_index, source_row % half_rows, half_rows),
            grid_rows,
            cap_rows,
            my_row,
        )
        col_slots = slot_target(
            parent_blocks(child_map, child_index, source_col % half_cols, half_cols),
            grid_cols,
            cap_cols,
            my_col,
        )
        row_hits = row_slots[:, None] == jnp.arange(local_rows, dtype=jnp.int32)[None, :]
        col_hits = col_slots[:, None] == jnp.arange(local_cols, dtype=jnp.int32)[None, :]
        return row_hits[:, None, :, None] & col_hits[None, :, None, :]

    sources_r = jnp.arange(grid_rows, dtype=jnp.int32)
    sources_c = jnp.arange(grid_cols, dtype=jnp.int32)
    arrivals = jax.vmap(
        lambda source_row: jax.vmap(lambda source_col: single(source_row, source_col))(sources_c)
    )(sources_r)
    return arrivals.astype(jnp.bfloat16)


def bit_of(value, position):
    return value // (1 << position) % 2


def join_columns(piece, rank, tree_levels):
    joined = piece
    for position in range(tree_levels):
        partner = from_partner(joined, "col", position)
        joined = jnp.where(
            bit_of(rank, position) == 1,
            jnp.concatenate([partner, joined], axis=1),
            jnp.concatenate([joined, partner], axis=1),
        )
    return joined


def spread_root(chosen, rank, root_rank, tree_levels):
    held = chosen
    for position in reversed(range(tree_levels)):
        half_size = held.shape[0] // 2
        received = from_partner(held[half_size:], "row", position)
        differs = bit_of(rank, position) != bit_of(root_rank, position)
        held = jnp.where(differs, received, held[:half_size])
    for position in range(tree_levels):
        received = from_partner(held, "row", position)
        differs = bit_of(rank, position) != bit_of(root_rank, position)
        held = jnp.where(
            differs,
            jnp.concatenate([received, held], axis=0),
            jnp.concatenate([held, received], axis=0),
        )
    return held


def parity_rows(row_operand, col_rank, row_period, block_width):
    row_count = row_operand.shape[0] // block_width
    grouped = row_operand.reshape(row_count // 2, 2, block_width, row_operand.shape[1])
    return lax.dynamic_index_in_dim(grouped, col_rank // row_period, 1, keepdims=False)


def pivot_factor(pivot_square):
    square = pivot_square.astype(jnp.float32)
    lower_factor = jnp.linalg.cholesky(0.5 * (square + square.T))
    inverse = jax.scipy.linalg.solve_triangular(
        lower_factor, jnp.eye(square.shape[0], dtype=jnp.float32), lower=True
    )
    return (lower_factor, inverse.T.astype(jnp.bfloat16))


def per_device(child_update_blocks, child_pivot_panel, child_map, coupled, parent_front):
    grid_rows = lax.axis_size("row")
    grid_cols = lax.axis_size("col")
    half_rows = grid_rows // 2
    half_cols = grid_cols // 2
    my_row = lax.axis_index("row")
    my_col = lax.axis_index("col")
    row_half = my_row // half_rows
    col_half = my_col // half_cols
    row_rank = my_row % half_rows
    col_rank = my_col % half_cols
    child_index = 2 * row_half + col_half
    local_rows = child_update_blocks.shape[1]
    local_cols = child_update_blocks.shape[4]
    parent_rows = parent_front.shape[1]
    parent_cols = parent_front.shape[4]
    pivot_blocks = FRONT_PIVOTS // BLOCK_ORDER
    update_block = child_update_blocks.reshape(local_rows * BLOCK_ORDER, local_cols * BLOCK_ORDER)
    panel_piece = child_pivot_panel.reshape(local_rows * BLOCK_ORDER, child_pivot_panel.shape[4])
    row_operand = join_columns(panel_piece, col_rank, half_cols.bit_length() - 1)
    chosen = parity_rows(row_operand, col_rank, half_rows, BLOCK_ORDER)
    col_operand = spread_root(chosen, row_rank, col_rank % half_rows, half_rows.bit_length() - 1)
    product = lax.dot_general(
        row_operand,
        col_operand.reshape(local_cols * BLOCK_ORDER, FRONT_PIVOTS),
        (((1,), (1,)), ((), ())),
        preferred_element_type=jnp.float32,
    )
    contribution = (update_block.astype(jnp.float32) - product).astype(jnp.bfloat16)
    cycles = (local_cols + grid_rows - 1) // grid_rows
    cap_rows = 2 * cycles
    cap_cols = (cycles + 1) // 2
    own_rows = parent_blocks(child_map, child_index, row_rank, half_rows)
    own_cols = parent_blocks(child_map, child_index, col_rank, half_cols)
    row_select = slot_match(own_rows, grid_rows, cap_rows).astype(jnp.bfloat16)
    blockwise = contribution.reshape(local_rows, BLOCK_ORDER, local_cols, BLOCK_ORDER)
    by_rows = jnp.einsum(
        "tsa,akbl->tskbl", row_select, blockwise, preferred_element_type=jnp.float32
    ).astype(jnp.bfloat16)
    arrivals = arrival_table(
        child_map,
        grid_rows,
        grid_cols,
        cap_rows,
        cap_cols,
        my_row,
        my_col,
        parent_rows,
        parent_cols,
    )
    col_select = slot_match(own_cols, grid_cols, cap_cols).astype(jnp.bfloat16)
    packed = jnp.einsum(
        "dub,tskbl->tdskul", col_select, by_rows, preferred_element_type=jnp.float32
    ).astype(jnp.bfloat16)
    outgoing = packed.reshape(grid_rows * grid_cols, cap_rows * BLOCK_ORDER, cap_cols * BLOCK_ORDER)
    incoming = lax.all_to_all(outgoing, ("row", "col"), split_axis=0, concat_axis=0, tiled=True)
    arrived = incoming.reshape(grid_rows, grid_cols, cap_rows, BLOCK_ORDER, cap_cols, BLOCK_ORDER)
    summed = jnp.einsum(
        "ycsuab,ycskul->akbl", arrivals, arrived, preferred_element_type=jnp.float32
    )
    assembled = parent_front.reshape(parent_rows * BLOCK_ORDER, parent_cols * BLOCK_ORDER).astype(
        jnp.float32
    ) + summed.reshape(parent_rows * BLOCK_ORDER, parent_cols * BLOCK_ORDER)
    pivot_piece = assembled[:, :BLOCK_ORDER].astype(jnp.bfloat16)
    own_pivot_rows = FRONT_PIVOTS // grid_rows
    pieces = lax.all_gather(pivot_piece[None, :own_pivot_rows], ("row", "col"), axis=0, tiled=True)
    arranged = pieces.reshape(
        grid_rows, grid_cols, own_pivot_rows // BLOCK_ORDER, BLOCK_ORDER, BLOCK_ORDER
    )[:, :pivot_blocks]
    pivot_square = jnp.transpose(arranged, (2, 0, 3, 1, 4)).reshape(FRONT_PIVOTS, FRONT_PIVOTS)
    lower_factor, factor_cols = pivot_factor(pivot_square)
    padded = jnp.concatenate(
        [
            factor_cols,
            jnp.zeros((grid_cols * BLOCK_ORDER - FRONT_PIVOTS, FRONT_PIVOTS), jnp.bfloat16),
        ],
        axis=0,
    )
    running = jnp.zeros((parent_rows * BLOCK_ORDER, FRONT_PIVOTS), jnp.float32)
    portion = lax.all_gather(pivot_piece, "col", axis=1, tiled=True)

    def multiply():
        return jnp.dot(portion, padded, preferred_element_type=jnp.float32)

    raw_below = lax.cond(jnp.int32(0) < FRONT_PIVOTS, multiply, lambda: running)
    block_ids = jnp.arange(parent_rows, dtype=jnp.int32) * grid_rows + my_row
    coupling = jnp.sum(
        jnp.where(
            block_ids[:, None] - pivot_blocks
            == jnp.arange(coupled.shape[0], dtype=jnp.int32)[None, :],
            coupled[None, :],
            0,
        ),
        axis=1,
    )
    kept_rows = jnp.where(block_ids < pivot_blocks, 1.0, coupling.astype(jnp.float32))
    below = (
        raw_below.reshape(parent_rows, BLOCK_ORDER, FRONT_PIVOTS) * kept_rows[:, None, None]
    ).reshape(parent_rows * BLOCK_ORDER, FRONT_PIVOTS)
    below_half = below.astype(jnp.bfloat16)
    parent_chosen = parity_rows(below_half, my_col, grid_rows, BLOCK_ORDER)
    col_panel = from_root(parent_chosen, "row", my_col % grid_rows)
    schur_part = assembled - lax.dot_general(
        below_half,
        col_panel.reshape(parent_cols * BLOCK_ORDER, FRONT_PIVOTS),
        (((1,), (1,)), ((), ())),
        preferred_element_type=jnp.float32,
    )
    blocked = schur_part.reshape(parent_rows, BLOCK_ORDER, parent_cols, BLOCK_ORDER)
    pivot_row = block_ids < pivot_blocks
    blocked = jnp.where(pivot_row[:, None, None, None], 0.0, blocked)
    lower_rows = lax.dynamic_index_in_dim(
        jnp.tril(lower_factor).reshape(
            own_pivot_rows // BLOCK_ORDER, grid_rows, BLOCK_ORDER, FRONT_PIVOTS
        ),
        my_row,
        1,
        keepdims=False,
    )
    safe_col = jnp.minimum(my_col, pivot_blocks - 1)
    top_part = lax.dynamic_slice_in_dim(lower_rows, safe_col * BLOCK_ORDER, BLOCK_ORDER, 2)
    low_part = lax.dynamic_slice_in_dim(
        below.reshape(parent_rows, BLOCK_ORDER, FRONT_PIVOTS),
        safe_col * BLOCK_ORDER,
        BLOCK_ORDER,
        2,
    )[own_pivot_rows // BLOCK_ORDER :]
    pivot_values = jnp.concatenate([top_part, low_part], axis=0)
    first_col = jnp.where(my_col < pivot_blocks, pivot_values, blocked[:, :, 0, :])
    blocked = blocked.at[:, :, 0, :].set(first_col)
    return blocked.reshape(1, parent_rows, BLOCK_ORDER, 1, parent_cols, BLOCK_ORDER)


def solution(mesh):
    in_specs = (
        P("row", None, None, "col", None, None),
        P("row", None, None, "col", None),
        P(),
        P(),
        P("row", None, None, "col", None, None),
    )
    out_specs = P("row", None, None, "col", None, None)
    return jax.shard_map(
        per_device, mesh=mesh, in_specs=in_specs, out_specs=out_specs, check_vma=False
    )
```

profile of v0, /device:TPU:112, one launch (start us, length us, event | category | flops | bytes accessed | tf_op | source)
XLA Modules:
  0.0 1061.2 jit_solution(2380453608947196024)
XLA Ops:
  13.3 23.7 %collective-permute-done.1 = bf16[2048,256]{1,0:T(8,128)(2,1)S(1)} collective-permute-done((bf16[2048,256]{1,0:T(8,128)(2,1)S(1)}, bf16[2048,256]{1,0:T(8,128)(2,1)S(1)}, u32[]{:S(2)}, u32[]{:S(2)}) %collective-permute-start.1) | collective-permute-done | bytes 1048608 | tf_op jit(solution)/shard_map/ppermute | solution.py:13
  40.2 45.7 %collective-permute-done.2 = bf16[2048,512]{1,0:T(8,128)(2,1)} collective-permute-done((bf16[2048,512]{1,0:T(8,128)(2,1)}, bf16[2048,512]{1,0:T(8,128)(2,1)}, u32[]{:S(2)}, u32[]{:S(2)}) %collective-permute-start.2) | collective-permute-done | bytes 2097184 | tf_op jit(solution)/shard_map/ppermute | solution.py:13
  88.7 24.7 %collective-permute-done.3 = bf16[4,128,1024]{2,1,0:T(8,128)(2,1)} collective-permute-done((bf16[4,128,1024]{2,1,0:T(8,128)(2,1)S(1)}, bf16[4,128,1024]{2,1,0:T(8,128)(2,1)}, u32[]{:S(2)}, u32[]{:S(2)}) %collective-permute-start.3) | collective-permute-done | bytes 1048608 | tf_op jit(solution)/shard_map/ppermute | solution.py:13
  116.2 10.7 %collective-permute-done.4 = bf16[2,128,1024]{2,1,0:T(8,128)(2,1)S(1)} collective-permute-done((bf16[2,128,1024]{2,1,0:T(8,128)(2,1)S(1)}, bf16[2,128,1024]{2,1,0:T(8,128)(2,1)S(1)}, u32[]{:S(2)}, u32[]{:S(2)}) %collective-permute-start.4) | collective-permute-done | bytes 524320 | tf_op jit(solution)/shard_map/ppermute | solution.py:13
  140.1 20.3 %collective-permute-done.6 = bf16[4,128,1024]{2,1,0:T(8,128)(2,1)S(1)} collective-permute-done((bf16[4,128,1024]{2,1,0:T(8,128)(2,1)S(1)}, bf16[4,128,1024]{2,1,0:T(8,128)(2,1)S(1)}, u32[]{:S(2)}, u32[]{:S(2)}) %collective-permute-start.6) | collective-permute-done | bytes 1048608 | tf_op jit(solution)/shard_map/ppermute | solution.py:13
  160.7 10.1 fusion.3
  201.8 40.6 %reduce_window_sum.47 = s32[8,16,16,1,8]{4,0,1,3,2:T(8,128)S(1)} reduce-window(s32[8,16,16,1,8]{4,0,1,3,2:T(8,128)S(1)} %get-tuple-element.101, s32[]{:T(128)} %constant.665.clone.1), window={size=1x1x1x1x8 pad=0_0x0_0x0_0x0_0x7_0}, to_apply=%region_4.5 | reduce-window | flops 114688 | bytes 131076 | tf_op jit(solution)/shard_map/vmap(vmap(jit(cumsum)))/reduce_window_sum | solution.py:30
  243.8 21.3 %reduce_window_sum.46 = s32[8,16,8,16]{3,2,1,0:T(8,128)S(1)} reduce-window(s32[8,16,8,16]{3,2,1,0:T(8,128)S(1)} %get-tuple-element.97, s32[]{:T(128)} %constant.665.clone.1), window={size=1x1x1x16 pad=0_0x0_0x0_0x15_0}, to_apply=%region_2.3 | reduce-window | flops 245760 | bytes 131076 | tf_op jit(solution)/shard_map/vmap(vmap(jit(cumsum)))/reduce_window_sum | solution.py:30
  272.3 26.7 %all-to-all-done = bf16[128,256,128]{2,1,0:T(8,128)(2,1)} async-done(((bf16[128,256,128]{2,1,0:T(8,128)(2,1)}), bf16[128,256,128]{2,1,0:T(8,128)(2,1)}, u32[]{:S(2)}, u32[]{:S(2)}) %all-to-all-start) | async-done | bytes 8388640 | tf_op jit(solution)/shard_map/all_to_all | solution.py:179
  299.0 11.5 %fusion.19 = f32[16,128,8,128]{3,0,2,1:T(8,128)} fusion(bf16[8,16,2,128,128,1]{4,3,2,1,0,5:T(8,128)(2,1)} %bitcast.18, pred[8,16,8]{1,0,2:T(8,128)(4,1)S(1)} %iota_compare_fusion.8, pred[8,16,2,16]{1,3,0,2:T(8,128)(4,1)S(1)} %iota_compare_fusion.5), kind=kOutput, calls=%fused_computation.41 | convolution fusion | flops 1073774592 | bytes 16782336 | tf_op jit(solution)/shard_map/ycsuab,ycskul->akbl/dot_general | solution.py:181
  328.1 197.0 %all-gather.6.cloned.1.call-done = bf16[16384,128]{1,0:T(8,128)(2,1)} async-done(((bf16[128,128]{1,0:T(8,128)(2,1)}), bf16[16384,128]{1,0:T(8,128)(2,1)}) %all-gather.6.cloned.1.call-update) | async-done | bytes 4194320 | tf_op jit(solution)/shard_map/all_gather | solution.py:189
  559.9 11.7 %cholesky.223 = f32[128,128]{1,0:T(8,128)S(1)} custom-call(f32[128,128]{1,0:T(8,128)S(1)} %cholesky.580), custom_call_target="Cholesky" | custom-call | tf_op jit(solution)/shard_map/jit(cholesky)/cholesky | solution.py:117
  574.2 9.8 custom-call.63
  587.9 11.9 %cholesky.244 = f32[128,128]{1,0:T(8,128)S(1)} custom-call(f32[128,128]{1,0:T(8,128)S(1)} %cholesky.584), custom_call_target="Cholesky" | custom-call | tf_op jit(solution)/shard_map/jit(cholesky)/cholesky | solution.py:117
  600.4 9.8 custom-call.64
  613.5 11.7 %cholesky.468 = f32[128,128]{1,0:T(8,128)S(1)} custom-call(f32[128,128]{1,0:T(8,128)S(1)} %cholesky.589), custom_call_target="Cholesky" | custom-call | tf_op jit(solution)/shard_map/jit(cholesky)/cholesky | solution.py:117
  625.9 9.8 custom-call.65
  639.2 11.9 %cholesky.487 = f32[128,128]{1,0:T(8,128)S(1)} custom-call(f32[128,128]{1,0:T(8,128)S(1)} %cholesky.594), custom_call_target="Cholesky" | custom-call | tf_op jit(solution)/shard_map/jit(cholesky)/cholesky | solution.py:117
  651.7 9.8 custom-call.66
  665.0 11.7 %cholesky.506 = f32[128,128]{1,0:T(8,128)S(1)} custom-call(f32[128,128]{1,0:T(8,128)S(1)} %cholesky.599), custom_call_target="Cholesky" | custom-call | tf_op jit(solution)/shard_map/jit(cholesky)/cholesky | solution.py:117
  677.3 10.2 custom-call.67
  690.9 11.7 %cholesky.526 = f32[128,128]{1,0:T(8,128)S(1)} custom-call(f32[128,128]{1,0:T(8,128)S(1)} %cholesky.604), custom_call_target="Cholesky" | custom-call | tf_op jit(solution)/shard_map/jit(cholesky)/cholesky | solution.py:117
  703.2 9.8 custom-call.68
  716.0 11.7 %cholesky.546 = f32[128,128]{1,0:T(8,128)S(1)} custom-call(f32[128,128]{1,0:T(8,128)S(1)} %cholesky.609), custom_call_target="Cholesky" | custom-call | tf_op jit(solution)/shard_map/jit(cholesky)/cholesky | solution.py:117
  728.4 9.8 custom-call.69
  740.8 11.7 %cholesky.564 = f32[128,128]{1,0:T(8,128)S(1)} custom-call(f32[128,128]{1,0:T(8,128)S(1)} %convolution_subtract_fusion.11), custom_call_target="Cholesky" | custom-call | tf_op jit(solution)/shard_map/jit(cholesky)/cholesky | solution.py:117
  768.9 28.7 %while.4 = (s32[]{:T(128)}, f32[1024,1024]{1,0:T(8,128)}, s32[8,2]{0,1:T(2,128)S(1)}, f32[8,128,128]{2,1,0:T(8,128)}, s32[]{:T(128)}) while((s32[]{:T(128)}, f32[1024,1024]{1,0:T(8,128)}, s32[8,2]{0,1:T(2,128)S(1)}, f32[8,128,128]{2,1,0:T(8,128)}, s32[]{:T(128)}) %tuple.75), condition=%wide.while_cond.3, body=%wide.while_body.3.sunk | while | flops 2 | bytes 132705 | solution.py:118
  797.6 79.8 %custom-call.70 = f32[8,128,128]{1,2,0:T(8,128)S(1)} custom-call(f32[8,128,128]{2,1,0:T(8,128)} %get-tuple-element.40), custom_call_target="InvertDiagBlocksLowerTriangular" | custom-call | tf_op jit(solution)/shard_map/jit(_solve_triangular)/triangular_solve | solution.py:118
  905.6 13.9 %multiply_convert_fusion = (bf16[2048,1024]{1,0:T(8,128)(2,1)S(1)}, f32[2048,1024]{1,0:T(8,128)}) fusion(f32[2048]{0:T(1024)S(1)} %broadcast_bitcast_fusion, bf16[2048,2048]{1,0:T(8,128)(2,1)} %all-gather.4.cloned.1.call-done, bf16[1024,1024]{0,1:T(8,128)(2,1)} %bitcast.62), kind=kOutput, calls=%fused_computation.12 | convolution fusion | flops 8594128896 | bytes 23076864 | tf_op jit(solution)/shard_map/cond/branch_1_fun/dot_general | solution.py:206
  925.3 78.7 %all-reduce.9.cloned.1.call-done = bf16[1024,1024]{1,0:T(8,128)(2,1)} async-done(((bf16[1024,1024]{1,0:T(8,128)(2,1)}), bf16[1024,1024]{1,0:T(8,128)(2,1)}) %all-reduce.9.cloned.1.call-update) | async-done | bytes 2097168 | tf_op jit(solution)/shard_map/psum | solution.py:18
  1004.0 14.3 %subtract_bitcast_fusion = f32[256,8,8,128]{3,1,2,0:T(8,128)S(1)} fusion(bf16[2048,1024]{1,0:T(8,128)(2,1)} %copy-done.8, bf16[1024,1024]{1,0:T(8,128)(2,1)} %all-reduce.9.cloned.1.call-done, f32[256,8,8,128]{3,2,1,0:T(8,128)} %bitcast.277, f32[256,8,8,128]{3,2,1,0:T(8,128)} %convert.52), kind=kOutput, calls=%fused_computation.11 | convolution fusion | flops 4299161600 | bytes 31457280 | tf_op jit(solution)/shard_map/dot_general | solution.py:226
  1025.6 28.9 %scatter.4 = f32[1,16,128,1,8,128]{5,4,3,2,1,0:T(8,128)} dynamic-update-slice(f32[1,16,128,1,8,128]{5,4,3,2,1,0:T(8,128)} %bitcast_select_fusion, f32[1,16,128,1,1,128]{5,4,3,2,1,0:T(1,128)S(1)} %bitcast.287, s32[]{:T(128)} %constant.665.clone.1, s32[]{:T(128)} %constant.665.clone.1, s32[]{:T(128)} %constant.665.clone.1, s32[]{:T(128)} %constant.665.clone.1, s32[]{:T(128)} %constant.665.clone.1, ...) | dynamic-update-slice | bytes 2097156 | tf_op jit(solution)/shard_map/scatter | solution.py:253
  (210 shorter events, 230.9 us)
Async XLA Ops:
  6.5 32.6 %copy-start.7 = (bf16[1,16,128,1,128]{4,2,3,1,0:T(8,128)(2,1)S(1)}, bf16[1,16,128,1,128]{4,2,3,1,0:T(8,128)(2,1)}, u32[]{:S(2)}) copy-start(bf16[1,16,128,1,128]{4,2,3,1,0:T(8,128)(2,1)} %param.8) | copy-start | bytes 1572868
  6.5 2.1 collective-permute-start
  10.2 26.8 %collective-permute-start.1 = (bf16[2048,256]{1,0:T(8,128)(2,1)S(1)}, bf16[2048,256]{1,0:T(8,128)(2,1)S(1)}, u32[]{:S(2)}, u32[]{:S(2)}) collective-permute-start(bf16[2048,256]{1,0:T(8,128)(2,1)S(1)} %maximum_select_fusion.7), channel_id=1, source_target_pairs={{0,2},{1,3},{2,0},{3,1},{4,6},{5,7},{6,4},{7,5},{8,10},{9,11},{10,... | collective-permute-start | bytes 3145736 | tf_op jit(solution)/shard_map/ppermute | solution.py:13
  38.8 47.2 %collective-permute-start.2 = (bf16[2048,512]{1,0:T(8,128)(2,1)}, bf16[2048,512]{1,0:T(8,128)(2,1)}, u32[]{:S(2)}, u32[]{:S(2)}) collective-permute-start(bf16[2048,512]{1,0:T(8,128)(2,1)} %maximum_select_fusion.4), channel_id=1, source_target_pairs={{0,4},{1,5},{2,6},{3,7},{4,0},{5,1},{6,2},{7,3},{8,12},{9,13},{10,... | collective-permute-start | bytes 6291464 | tf_op jit(solution)/shard_map/ppermute | solution.py:13
  88.3 25.1 %collective-permute-start.3 = (bf16[4,128,1024]{2,1,0:T(8,128)(2,1)S(1)}, bf16[4,128,1024]{2,1,0:T(8,128)(2,1)}, u32[]{:S(2)}, u32[]{:S(2)}) collective-permute-start(bf16[4,128,1024]{2,1,0:T(8,128)(2,1)S(1)} %slice_bitcast_fusion.1), channel_id=1, source_target_pairs={{0,32},{16,48},{32,0},{48,16},{64,96},{80,112},{96,64},{112,80},{1... | collective-permute-start | bytes 3145736 | tf_op jit(solution)/shard_map/ppermute | solution.py:13
  114.8 12.0 %collective-permute-start.4 = (bf16[2,128,1024]{2,1,0:T(8,128)(2,1)S(1)}, bf16[2,128,1024]{2,1,0:T(8,128)(2,1)S(1)}, u32[]{:S(2)}, u32[]{:S(2)}) collective-permute-start(bf16[2,128,1024]{2,1,0:T(8,128)(2,1)S(1)} %slice.382), channel_id=1, source_target_pairs={{0,16},{16,0},{32,48},{48,32},{64,80},{80,64},{96,112},{112,96},{1... | collective-permute-start | bytes 1572872 | tf_op jit(solution)/shard_map/ppermute | solution.py:13
  126.9 11.9 %collective-permute-start.5 = (bf16[2,128,1024]{2,1,0:T(8,128)(2,1)S(1)}, bf16[2,128,1024]{2,1,0:T(8,128)(2,1)S(1)}, u32[]{:S(2)}, u32[]{:S(2)}) collective-permute-start(bf16[2,128,1024]{2,1,0:T(8,128)(2,1)S(1)} %slice_select_fusion), channel_id=1, source_target_pairs={{0,16},{16,0},{32,48},{48,32},{64,80},{80,64},{96,112},{112,96},{1... | collective-permute-start | bytes 1572872 | tf_op jit(solution)/shard_map/ppermute | solution.py:13
  128.3 6.7 copy-start
  139.0 21.4 %collective-permute-start.6 = (bf16[4,128,1024]{2,1,0:T(8,128)(2,1)S(1)}, bf16[4,128,1024]{2,1,0:T(8,128)(2,1)S(1)}, u32[]{:S(2)}, u32[]{:S(2)}) collective-permute-start(bf16[4,128,1024]{2,1,0:T(8,128)(2,1)S(1)} %maximum_select_fusion.9), channel_id=1, source_target_pairs={{0,32},{16,48},{32,0},{48,16},{64,96},{80,112},{96,64},{112,80},{1... | collective-permute-start | bytes 3145736 | tf_op jit(solution)/shard_map/ppermute | solution.py:13
  189.3 109.7 %all-to-all-start = ((bf16[128,256,128]{2,1,0:T(8,128)(2,1)}), bf16[128,256,128]{2,1,0:T(8,128)(2,1)}, u32[]{:S(2)}, u32[]{:S(2)}) async-start(bf16[128,256,128]{2,1,0:T(8,128)(2,1)} %bitcast.278), calls=%async_computation | async-start | bytes 16777216 | tf_op jit(solution)/shard_map/all_to_all | solution.py:179
  198.9 326.3 %all-gather.6.cloned.1.call-start = ((), (), s32[]{:S(2)}) async-start(), calls=%async_computation.3 | async-start | bytes 4227072 | tf_op jit(solution)/shard_map/all_gather | solution.py:189
  310.5 6.2 copy-start.2
  316.7 3.7 copy-start.3
  316.7 6.4 copy-start.9
  320.4 2.0 copy-start.6
  323.0 582.5 %all-gather.4.cloned.1.call-start = ((), (), s32[]{:S(2)}) async-start(), calls=%async_computation.1 | async-start | bytes 8912896 | tf_op jit(solution)/shard_map/all_gather | solution.py:203
  328.0 676.0 %all-reduce.9.cloned.1.call-start = ((), (), s32[]{:S(2)}) async-start(), calls=%async_computation.2 | async-start | bytes 4194304 | tf_op jit(solution)/shard_map/psum | solution.py:18
  531.8 3.4 copy-start.1
  558.0 1.9 copy-start.5
  877.4 4.6 copy-start.4
  919.5 1.9 copy-start.8
Sparse Core Ops, SparseCore 0:
  323.1 201.9 all-gather.5
  527.5 75.8 all-gather.3
  923.1 80.9 all-reduce.8
where the time goes:
time: 1070 us; the launch traced here: 1060 us
  waiting for transfers between devices  433 us (40%)
  other arithmetic  368 us (34%)
  local copies, waits for them, and re-layouts  116 us (11%)
  matrix products  108 us (10%)
  between operations  19.4 us (2%)
  starting transfers between devices  16.9 us (2%)
    all_gather x1, waiting for transfers between devices, per_device(): lax.all_gather(pivot_piece[None, :own_pivot_rows], ('row', 'col'), axis=0...  197 us
    another operation x31, other arithmetic, pivot_factor(): lower_factor = jnp.linalg.cholesky(0.5 * (square + square.T))  173 us
    ppermute x7, waiting for transfers between devices, from_partner(): return lax.ppermute(value, axis, pairs)  131 us
    another operation x3, other arithmetic, pivot_factor(): jax.scipy.linalg.solve_triangular(lower_factor, jnp.eye(square.shape[0],...  84.6 us
    psum x1, waiting for transfers between devices, from_root(): return lax.psum(jnp.where(mine, array, jnp.zeros_like(array)), axis)  78.7 us
    another operation x4, other arithmetic, slot_match(): ordinal = jnp.cumsum(matches.astype(jnp.int32), axis=1) - 1  62.1 us
    scatter x1, local copies, waits for them, and re-layouts, per_device(): blocked = blocked.at[:, :, 0, :].set(first_col)  28.9 us
    another operation x24, local copies, waits for them, and re-layouts  28.7 us
  transfers between devices with their start and end apart: 11, of which 10 were waited for; matrix products, arithmetic and copies ran while one was open for 44% of the time, Pallas kernels for 0%

commit v1 on v0

v1 whole, which is shorter than its diff:
```python
import functools

import jax
import jax.numpy as jnp
from jax import lax
from jax.experimental import pallas as pl
from jax.experimental.pallas import tpu as pltpu
from jax.sharding import PartitionSpec as P

B = 128
NB = 8
N = NB * B
F32 = jnp.float32
BF = jnp.bfloat16
MESH = pl.DeviceIdType.MESH
ANY = pl.BlockSpec(memory_space=pl.ANY)
VM = pl.BlockSpec(memory_space=pltpu.VMEM)
SM = pl.BlockSpec(memory_space=pltpu.SMEM)
LIMIT = 56 * 1024 * 1024


def params(**kw):
    return pltpu.CompilerParams(vmem_limit_bytes=LIMIT, **kw)


N_TAB = 128
AT_ROW, AT_COL, AT_RSRC, AT_RCH, AT_CSRC, AT_CCH = 0, 16, 32, 64, 96, 112


def tables_kernel(map_ref, tab_ref, count):
    my_row, my_col = lax.axis_index("row"), lax.axis_index("col")
    row_rank, col_rank = my_row % 4, my_col % 8
    child = 2 * (my_row // 4) + my_col // 8

    def clear(i, _):
        count[i] = 0
        return 0

    lax.fori_loop(0, 24, clear, 0)

    def out_row(l, _):
        owner = map_ref[child, l * 4 + row_rank] % 8
        tab_ref[AT_ROW + owner * 2 + count[owner]] = l
        count[owner] = count[owner] + 1
        return 0

    lax.fori_loop(0, 16, out_row, 0)

    def out_col(m, _):
        tab_ref[AT_COL + m] = map_ref[child, m * 8 + col_rank] % 16
        return 0

    lax.fori_loop(0, 8, out_col, 0)

    def arrive(q, _):
        h, g = q // 2, q % 2

        def one(b, _):
            target = map_ref[q, b]

            @pl.when(target % 8 == my_row)
            def _():
                slot = 8 + q * 4 + b % 4
                at = h * 16 + target // 8
                tab_ref[AT_RSRC + at] = (h * 4 + b % 4) * 32 + count[slot]
                tab_ref[AT_RCH + at] = g
                count[slot] = count[slot] + 1

            @pl.when(target % 16 == my_col)
            def _():
                at = h * 8 + target // 16
                tab_ref[AT_CSRC + at] = (g * 8 + b % 8) * 2
                tab_ref[AT_CCH + at] = g

            return 0

        lax.fori_loop(0, 64, one, 0)
        return 0

    lax.fori_loop(0, 4, arrive, 0)


def tables(child_map):
    return pl.pallas_call(
        tables_kernel,
        out_shape=jax.ShapeDtypeStruct((N_TAB,), jnp.int32),
        in_specs=[SM],
        out_specs=SM,
        scratch_shapes=[pltpu.SMEM((24,), jnp.int32)],
    )(child_map)


def place(row, col):
    return row // 4, row % 4, col // 4, col // 2 % 2, col % 2


def panel_gather_kernel(p_ref, row_ref, col_ref, local, send, rrow, rcol):
    my_row, my_col = lax.axis_index("row"), lax.axis_index("col")
    half_row, y = my_row // 4 * 4, my_row % 4
    half_col, cc = my_col // 8 * 8, my_col % 8
    core, pair = cc % 2, cc // 2
    sibling = half_col + pair * 2 + 1 - core
    barrier = pltpu.get_barrier_semaphore()

    def greet(row, col):
        pl.semaphore_signal(barrier, inc=1, device_id=(row, col), device_id_type=MESH)

    others = [half_col + (pair + d) % 4 * 2 + core for d in (1, 2, 3)]
    for col in others:
        greet(my_row, col)
    greet(my_row, sibling)
    source_row = half_row + cc % 4
    own = y == cc % 4
    for j in range(8):

        @pl.when(jnp.logical_not(own & (cc == j)))
        def _():
            greet(source_row, half_col + j)

    pl.semaphore_wait(barrier, jnp.where(own, 11, 12))

    def remote(src, dst, s, r, row, col):
        return pltpu.make_async_remote_copy(
            src_ref=src, dst_ref=dst, send_sem=s, recv_sem=r, device_id=(row, col), device_id_type=MESH
        )

    mine = pltpu.make_async_copy(p_ref, row_ref.at[cc], local.at[0])
    mine.start()
    copies = []
    for i, col in enumerate(others):
        copies.append(remote(p_ref, row_ref.at[cc], send.at[i], rrow.at[cc], my_row, col))
        copies[-1].start()
    for d in range(4):
        for parity in range(2):
            row, col = half_row + (y + d) % 4, half_col + parity * 4 + y
            i = 4 + d * 2 + parity
            c = remote(p_ref.at[:, parity], col_ref.at[cc], send.at[i], rcol.at[cc], row, col)
            if d:
                c.start()
            else:
                self_copy = pltpu.make_async_copy(p_ref.at[:, parity], col_ref.at[cc], local.at[1])
                is_self = cc == parity * 4 + y

                @pl.when(is_self)
                def _():
                    self_copy.start()

                @pl.when(jnp.logical_not(is_self))
                def _():
                    c.start()

    sib = remote(p_ref, row_ref.at[cc], send.at[3], rrow.at[cc], my_row, sibling)
    sib.start()
    forwards = []
    for i in range(3):
        k = (pair + 3 - i) % 4 * 2 + core
        remote(p_ref, row_ref.at[k], send.at[0], rrow.at[k], my_row, sibling).wait_recv()
        f = remote(row_ref.at[k], row_ref.at[k], send.at[12 + i], rrow.at[k], my_row, sibling)
        f.start()
        forwards.append(f)
    for c in copies + forwards + [sib]:
        c.wait_send()
    for d in range(4):
        for parity in range(2):
            c = remote(p_ref.at[:, parity], col_ref.at[cc], send.at[4 + d * 2 + parity], rcol.at[cc], my_row, my_col)
            if d:
                c.wait_send()
            else:
                is_self = cc == parity * 4 + y

                @pl.when(is_self)
                def _():
                    pltpu.make_async_copy(p_ref.at[:, parity], col_ref.at[cc], local.at[1]).wait()

                @pl.when(jnp.logical_not(is_self))
                def _():
                    c.wait_send()

    mine.wait()
    for i in range(4):
        k = i * 2 + 1 - core
        remote(p_ref, row_ref.at[k], send.at[0], rrow.at[k], my_row, sibling).wait_recv()
    for j in range(8):

        @pl.when(jnp.logical_not(own & (cc == j)))
        def _():
            remote(p_ref.at[:, 0], col_ref.at[j], send.at[0], rcol.at[j], my_row, sibling).wait_recv()


def panel_gather(piece):
    return pl.pallas_call(
        panel_gather_kernel,
        out_shape=(
            jax.ShapeDtypeStruct((8, 8, 2, B, B), BF),
            jax.ShapeDtypeStruct((8, 8, B, B), BF),
        ),
        in_specs=[ANY],
        out_specs=(ANY, ANY),
        scratch_shapes=[
            pltpu.SemaphoreType.DMA((2,)),
            pltpu.SemaphoreType.DMA((15,)),
            pltpu.SemaphoreType.DMA((8,)),
            pltpu.SemaphoreType.DMA((8,)),
        ],
        compiler_params=params(collective_id=1, has_side_effects=True),
    )(piece)


def contribution_kernel(tab, u0, u1, row_ref, col_ref, out_ref, wide):
    owner = pl.program_id(0)
    left = []
    for s, u in enumerate((u0, u1)):
        wide[s] = u[0].astype(F32)
        l = tab[AT_ROW + owner * 2 + s]
        left.append(jnp.concatenate([row_ref[k, l] for k in range(8)], axis=1))
    left = jnp.concatenate(left, axis=0)
    for m in range(0, 8, 2):
        right = jnp.concatenate(
            [jnp.concatenate([col_ref[k, m + t] for k in range(8)], axis=1) for t in range(2)], axis=0
        )
        product = lax.dot_general(left, right, (((1,), (1,)), ((), ())), preferred_element_type=F32)
        for t in range(2):
            c = tab[AT_COL + m + t]
            for s in range(2):
                value = wide[s, :, m + t, :] - product[s * B : (s + 1) * B, t * B : (t + 1) * B]
                out_ref[c, s * B : (s + 1) * B, :] = value.astype(BF)


def contributions(tab, update, row_op, col_op):
    full = lambda shape: pl.BlockSpec(shape, lambda i, t: (0,) * len(shape))
    u_spec = lambda s: pl.BlockSpec((1, B, 8, B), lambda i, t: (t[AT_ROW + 2 * i + s], 0, 0, 0))
    return pl.pallas_call(
        contribution_kernel,
        out_shape=jax.ShapeDtypeStruct((128, 2 * B, B), BF),
        grid_spec=pltpu.PrefetchScalarGridSpec(
            num_scalar_prefetch=1,
            grid=(8,),
            in_specs=[u_spec(0), u_spec(1), full((8, 16, B, B)), full((8, 8, B, B))],
            out_specs=pl.BlockSpec((16, 2 * B, B), lambda i, t: (i, 0, 0)),
            scratch_shapes=[pltpu.VMEM((2, B, 8, B), F32)],
        ),
        compiler_params=params(),
    )(tab, update, update, row_op, col_op)


def pivot_kernel(tab, c0, c1, front, out_ref):
    l = pl.program_id(0)
    value = front[0].astype(F32)
    for h, c in enumerate((c0, c1)):
        valid = tab[AT_RCH + h * 16 + l] == tab[AT_CCH + h * 8]
        value = value + jnp.where(valid, c[0].astype(F32), 0.0)
    out_ref[0] = value.astype(BF)


def pivot_columns(tab, arrived, front):
    def spec(h):
        return pl.BlockSpec((1, B, B), lambda l, t: (t[AT_RSRC + h * 16 + l] + t[AT_CSRC + h * 8], 0, 0))

    one = pl.BlockSpec((1, B, B), lambda l, t: (l, 0, 0))
    return pl.pallas_call(
        pivot_kernel,
        out_shape=jax.ShapeDtypeStruct((16, B, B), BF),
        grid_spec=pltpu.PrefetchScalarGridSpec(
            num_scalar_prefetch=1, grid=(16,), in_specs=[spec(0), spec(1), one], out_specs=one
        ),
        compiler_params=params(),
    )(tab, arrived, arrived, front)


def remote(src, dst, s, r, row, col):
    return pltpu.make_async_remote_copy(
        src_ref=src, dst_ref=dst, send_sem=s, recv_sem=r, device_id=(row, col), device_id_type=MESH
    )


class Gather:
    def __init__(self, p_ref, sq_ref, por_ref, cols_ref, local, s_row, s_sq, s_por, s_cols, s_fsq, s_fpor, r_row, r_sq, r_por, r_cols):
        self.__dict__.update(locals())
        self.row, self.col = lax.axis_index("row"), lax.axis_index("col")
        self.core, self.chip = self.col % 2, self.col // 2
        self.sibling = self.chip * 2 + 1 - self.core
        self.owner = self.col < 8
        self.diagonal = self.row == self.col

    def chips(self):
        return [(self.chip + d) % 8 * 2 + self.core for d in (4, 1, 7, 2, 6, 3, 5)]

    def enter(self):
        barrier = pltpu.get_barrier_semaphore()

        def greet(row, col):
            pl.semaphore_signal(barrier, inc=1, device_id=(row, col), device_id_type=MESH)

        greet(self.row, self.sibling)

        @pl.when(self.owner)
        def _():
            for d in range(1, 8):
                greet((self.row + d) % 8, self.col)

        for i in range(4):
            j = 2 * i + self.core

            @pl.when(j != self.col)
            def _():
                greet(self.row, j)

        for j in range(8):
            source = self.col % 8

            @pl.when(jnp.logical_not((source == self.row) & (self.col == j)))
            def _():
                greet(source, j)

        pl.semaphore_wait(barrier, jnp.where(self.owner, jnp.where(self.diagonal, 30, 31), 1))

    def row_sends(self):
        out = []
        for d in range(1, 8):
            dst = self.sq_ref.at[self.col, self.row]
            out.append(remote(self.p_ref.at[0, 0], dst, self.s_row.at[d - 1], self.r_row.at[self.row], (self.row + d) % 8, self.col))
        return out

    def sq_sends(self):
        return [
            remote(self.sq_ref.at[self.col], self.sq_ref.at[self.col], self.s_sq.at[i], self.r_sq.at[self.col], self.row, c)
            for i, c in enumerate(self.chips())
        ]

    def por_sends(self):
        return [
            remote(self.p_ref, self.por_ref.at[self.col], self.s_por.at[i], self.r_por.at[self.col], self.row, c)
            for i, c in enumerate(self.chips())
        ]

    def cols_sends(self):
        out = []
        for d in (4, 1, 3, 5, 7, 2, 6, 0):
            for half in range(2):
                c = remote(
                    self.p_ref.at[:, half], self.cols_ref.at[self.col], self.s_cols.at[d * 2 + half], self.r_cols.at[self.col],
                    (self.row + d) % 8, self.row + 8 * half,
                )
                out.append((c, d == 0 and half == 0))
        return out

    def local_copies(self):
        a = pltpu.make_async_copy(self.p_ref.at[0, 0], self.sq_ref.at[self.col, self.row], self.local.at[0])
        b = pltpu.make_async_copy(self.p_ref, self.por_ref.at[self.col], self.local.at[1])
        c = pltpu.make_async_copy(self.p_ref.at[:, 0], self.cols_ref.at[self.col], self.local.at[2])
        return a, b, c

    def start(self):
        @pl.when(self.owner)
        def _():
            a, b, c = self.local_copies()
            a.start()
            for s in self.row_sends():
                s.start()
            b.start()

            @pl.when(self.diagonal)
            def _():
                c.start()

            a.wait()
            for d in range(1, 8):
                i = (self.row + d) % 8
                remote(self.p_ref.at[0, 0], self.sq_ref.at[self.col, i], self.s_row.at[0], self.r_row.at[i], self.row, self.sibling).wait_recv()
            for s in self.sq_sends():
                s.start()
            for s in self.por_sends():
                s.start()
            for s, maybe_self in self.cols_sends():
                if maybe_self:

                    @pl.when(jnp.logical_not(self.diagonal))
                    def _():
                        s.start()

                else:
                    s.start()
            b.wait()

            @pl.when(self.diagonal)
            def _():
                c.wait()

    def share(self, ref, send, recv):
        for i in range(4):
            j = 2 * i + self.core

            @pl.when(j != self.col)
            def _():
                remote(ref.at[j], ref.at[j], send.at[i], recv.at[j], self.row, self.sibling).wait_recv()

            remote(ref.at[j], ref.at[j], send.at[i], recv.at[j], self.row, self.sibling).start()

    def shared(self, ref, send, recv):
        for i in range(4):
            j = 2 * i + 1 - self.core
            remote(ref.at[j], ref.at[j], send.at[i], recv.at[j], self.row, self.sibling).wait_recv()

    def share_square(self):
        self.share(self.sq_ref, self.s_fsq, self.r_sq)

    def wait_square(self):
        self.shared(self.sq_ref, self.s_fsq, self.r_sq)

    def share_portion(self):
        self.share(self.por_ref, self.s_fpor, self.r_por)

    def wait_rest(self):
        self.shared(self.por_ref, self.s_fpor, self.r_por)
        for j in range(8):

            @pl.when(jnp.logical_not(self.diagonal & (self.col == j)))
            def _():
                remote(self.cols_ref.at[j], self.cols_ref.at[j], self.s_cols.at[0], self.r_cols.at[j], self.row, self.sibling).wait_recv()

    def finish(self):
        for ref, send, recv in ((self.sq_ref, self.s_fsq, self.r_sq), (self.por_ref, self.s_fpor, self.r_por)):
            for i in range(4):
                j = 2 * i + self.core
                remote(ref.at[j], ref.at[j], send.at[i], recv.at[j], self.row, self.sibling).wait_send()

        @pl.when(self.owner)
        def _():
            for s in self.row_sends() + self.sq_sends() + self.por_sends():
                s.wait_send()
            for s, maybe_self in self.cols_sends():
                if maybe_self:

                    @pl.when(jnp.logical_not(self.diagonal))
                    def _():
                        s.wait_send()

                else:
                    s.wait_send()


GATHER_SEMS = (3, 7, 7, 7, 16, 4, 4, 8, 8, 8, 8)


def pivot_gather_kernel(p_ref, sq_ref, por_ref, cols_ref, *sems):
    g = Gather(p_ref, sq_ref, por_ref, cols_ref, *sems)
    g.enter()
    g.start()
    g.share_square()
    g.wait_square()
    g.share_portion()
    g.wait_rest()
    g.finish()


def pivot_gather(piece):
    return pl.pallas_call(
        pivot_gather_kernel,
        out_shape=(
            jax.ShapeDtypeStruct((8, 8, B, B), BF),
            jax.ShapeDtypeStruct((8, 8, 2, B, B), BF),
            jax.ShapeDtypeStruct((8, 8, B, B), BF),
        ),
        in_specs=[ANY],
        out_specs=(ANY, ANY, ANY),
        scratch_shapes=[pltpu.SemaphoreType.DMA((n,)) for n in GATHER_SEMS],
        compiler_params=params(collective_id=2, has_side_effects=True),
    )(piece)


def splits(a):
    parts = []
    for i in range(3):
        h = a.astype(BF)
        parts.append(h)
        if i < 2:
            a = a - h.astype(F32)
    return parts


LEFT = (0, 0, 1, 1, 0, 2)
RIGHT = (0, 1, 0, 1, 2, 0)


def dot_f32(a, b, dims):
    sa, sb = splits(a), splits(b)
    left = jnp.concatenate([sa[i] for i in LEFT], axis=dims[0][0])
    right = jnp.concatenate([sb[i] for i in RIGHT], axis=dims[1][0])
    return lax.dot_general(left, right, (dims, ((), ())), preferred_element_type=F32)


def diagonal_factor(square):
    group = 16
    lane = lax.broadcasted_iota(jnp.int32, (8, B), 1)
    sub = lax.broadcasted_iota(jnp.int32, (8, B), 0)
    spread = lambda x, s: jnp.broadcast_to(x[s : s + 1, :], (8, B))
    rest, upper, lower = square, [], []
    for g in range(B // group):
        r0 = group * g
        p = [rest[8 * v : 8 * v + 8, :] for v in range(2)]
        column = [[jnp.broadcast_to(p[v][:, r0 + j : r0 + j + 1], (8, B)) for v in range(2)] for j in range(group)]
        root = [jnp.zeros((8, B), F32) for _ in range(2)]
        for k in range(group):
            at, s = divmod(k, 8)
            r = lax.rsqrt(spread(column[k][at], s))
            root[at] = jnp.where(sub == s, r, root[at])
            if k == group - 1:
                break
            here = lane == r0 + k
            row = jnp.where(here, 1.0, spread(p[at], s))
            for v in range(at, 2):
                if v == at and s == 7:
                    continue
                factor = column[k][v] * (r * r)
                if v == at:
                    factor = jnp.where(sub > s, factor, 0.0)
                    p[v] = jnp.where(here & (sub > s), 0.0, p[v]) - factor * row
                else:
                    p[v] = jnp.where(here, 0.0, p[v]) - factor * row
                for j in range(k + 1, group):
                    column[j][v] = column[j][v] - factor * spread(column[j][at], s)
        panel = jnp.concatenate([p[v] * root[v] for v in range(2)], axis=0)
        roots = jnp.concatenate(root, axis=0)
        ln = lax.broadcasted_iota(jnp.int32, (group, B), 1) - r0
        sb = lax.broadcasted_iota(jnp.int32, (group, B), 0)
        eliminated = jnp.where(ln == sb, roots, jnp.where((ln > sb) & (ln < group), 0.0, panel))
        upper.append(panel)
        lower.append(jnp.where(ln > sb, 0.0, eliminated))
        if g < B // group - 1:
            change = dot_f32(jnp.where(ln >= group, panel, 0.0), eliminated, ((0,), (0,)))
            lt = lax.broadcasted_iota(jnp.int32, (B - r0 - group, B), 1)
            rest = jnp.where((lt >= r0) & (lt < r0 + group), 0.0, rest[group:, :]) - change[r0 + group :, :]
    return jnp.concatenate(upper, axis=0), jnp.concatenate(lower, axis=0)


def factor_start(sq_ref, lower_ref, work):
    for i in range(NB):
        for j in range(NB):
            at = (slice(i * B, (i + 1) * B), slice(j * B, (j + 1) * B))
            if j < i:
                work[at] = jnp.zeros((B, B), F32)
            else:
                work[at] = 0.5 * (sq_ref[j, i].astype(F32) + sq_ref[i, j].astype(F32).T)
    lower_ref[...] = jnp.zeros((B, B), F32)


def factor_step(kb, my_row, my_col, inv_ref, lower_ref, work, left, right):
    lane = lax.broadcasted_iota(jnp.int32, (B, B), 1)
    sub = lax.broadcasted_iota(jnp.int32, (B, B), 0)
    d0 = pl.multiple_of(kb * B, B)
    upper, lower = diagonal_factor(work[pl.ds(d0, B), pl.ds(d0, B)])
    work[pl.ds(d0, B), pl.ds(d0, B)] = jnp.where(lane == sub, 1.0, 0.0)
    panel = dot_f32(lower, work[pl.ds(d0, B), :], ((1,), (0,)))
    col = lax.broadcasted_iota(jnp.int32, (B, N), 1)
    inv_ref[pl.ds(d0, B), :] = jnp.where(col < d0 + B, panel, 0.0).astype(BF)

    @pl.when(kb == my_col)
    def _():
        @pl.when(kb == my_row)
        def _():
            lower_ref[...] = jnp.where(lane >= sub, upper, 0.0).T

        @pl.when(kb < my_row)
        def _():
            work[pl.ds(d0, B), :] = panel
            lower_ref[...] = work[pl.ds(d0, B), pl.ds(pl.multiple_of(my_row * B, B), B)].T

    parts = splits(panel)
    for t in range(6):
        left[t * B : (t + 1) * B, :] = parts[LEFT[t]]
        right[t * B : (t + 1) * B, :] = parts[RIGHT[t]]

    def trailing(i, _):
        i0 = pl.multiple_of(i * B, B)
        work[pl.ds(i0, B), pl.ds(d0, B)] = jnp.zeros((B, B), F32)
        work[pl.ds(i0, B), :] = work[pl.ds(i0, B), :] - lax.dot_general(
            left[:, pl.ds(i0, B)], right[...], (((0,), (0,)), ((), ())), preferred_element_type=F32
        )
        return 0

    lax.fori_loop(kb + 1, NB, trailing, 0)


def below_rows(por_ref, cols_ref, inv_ref, lower_ref, keep_ref, my_col, below_ref, panel_ref, first_ref):
    safe = jnp.minimum(my_col, NB - 1)
    dims = (((1,), (1,)), ((), ()))

    def rows(i, _):
        for t in range(2):
            l = 2 * i + t
            a = jnp.concatenate([por_ref[k, l] for k in range(8)], axis=1)
            out = lax.dot_general(a, inv_ref[...], dims, preferred_element_type=F32) * keep_ref[l]
            below_ref[pl.ds(pl.multiple_of(l * B, B), B), :] = out.astype(BF)
            mine = inv_ref[pl.ds(pl.multiple_of(safe * B, B), B), :]
            first_ref[l] = lax.dot_general(a, mine, dims, preferred_element_type=F32) * keep_ref[l]
        return 0

    lax.fori_loop(0, 8, rows, 0)
    first_ref[0] = lower_ref[...]

    def cols(m, _):
        a = jnp.concatenate([cols_ref[k, m] for k in range(8)], axis=1)
        out = lax.dot_general(a, inv_ref[...], dims, preferred_element_type=F32) * keep_ref[16 + m]
        panel_ref[pl.ds(pl.multiple_of(m * B, B), B), :] = out.astype(BF)
        return 0

    lax.fori_loop(0, 8, cols, 0)


def factor_kernel(sq_ref, por_ref, cols_ref, keep_ref, below_ref, panel_ref, first_ref, inv_ref, lower_ref, work, left, right):
    my_row, my_col = lax.axis_index("row"), lax.axis_index("col")
    factor_start(sq_ref, lower_ref, work)

    def step(kb, _):
        factor_step(kb, my_row, my_col, inv_ref, lower_ref, work, left, right)
        return 0

    lax.fori_loop(0, NB, step, 0)
    below_rows(por_ref, cols_ref, inv_ref, lower_ref, keep_ref, my_col, below_ref, panel_ref, first_ref)


FACTOR_OUT = (
    jax.ShapeDtypeStruct((16 * B, N), BF),
    jax.ShapeDtypeStruct((8 * B, N), BF),
    jax.ShapeDtypeStruct((16, B, B), F32),
)
FACTOR_SCRATCH = (
    ((N, N), BF),
    ((B, B), F32),
    ((N, N), F32),
    ((6 * B, N), BF),
    ((6 * B, N), BF),
)


def factor(square, portion, cols, keep):
    return pl.pallas_call(
        factor_kernel,
        out_shape=FACTOR_OUT,
        in_specs=[VM, VM, VM, SM],
        out_specs=(VM, VM, VM),
        scratch_shapes=[pltpu.VMEM(s, d) for s, d in FACTOR_SCRATCH],
        compiler_params=params(),
    )(square, portion, cols, keep)


def schur_kernel(tab, front, arrived, below, panel, first, out_ref, wide):
    i = pl.program_id(0)
    my_col = lax.axis_index("col")
    product = lax.dot_general(below[...], panel[...], (((1,), (1,)), ((), ())), preferred_element_type=F32)
    for s in range(2):
        l = 2 * i + s
        wide[...] = front[s].astype(F32)
        for m in range(8):
            value = wide[:, m, :]
            for h in range(2):
                valid = tab[AT_RCH + h * 16 + l] == tab[AT_CCH + h * 8 + m]
                at = jnp.where(valid, tab[AT_RSRC + h * 16 + l] + tab[AT_CSRC + h * 8 + m], 0)
                value = value + jnp.where(valid, arrived[at].astype(F32), 0.0)
            value = value - product[s * B : (s + 1) * B, m * B : (m + 1) * B]
            if s == 0:
                value = jnp.where(l == 0, 0.0, value)
            if m == 0:
                value = jnp.where(my_col < NB, first[s], value)
            out_ref[s, :, m, :] = value


def schur(tab, front, arrived, below, panel, first):
    full = lambda shape: pl.BlockSpec(shape, lambda i, t: (0,) * len(shape))
    return pl.pallas_call(
        schur_kernel,
        out_shape=jax.ShapeDtypeStruct((16, B, 8, B), F32),
        grid_spec=pltpu.PrefetchScalarGridSpec(
            num_scalar_prefetch=1,
            grid=(8,),
            in_specs=[
                pl.BlockSpec((2, B, 8, B), lambda i, t: (i, 0, 0, 0)),
                full((256, B, B)),
                pl.BlockSpec((2 * B, N), lambda i, t: (i, 0)),
                full((N, N)),
                pl.BlockSpec((2, B, B), lambda i, t: (i, 0, 0)),
            ],
            out_specs=pl.BlockSpec((2, B, 8, B), lambda i, t: (i, 0, 0, 0)),
            scratch_shapes=[pltpu.VMEM((B, 8, B), F32)],
        ),
        compiler_params=params(),
    )(tab, front, arrived, below, panel, first)


def per_device(child_update_blocks, child_pivot_panel, child_map, coupled, parent_front):
    my_row, my_col = lax.axis_index("row"), lax.axis_index("col")
    front = parent_front.reshape(16, B, 8, B)
    tab = tables(child_map)
    row_op, col_op = panel_gather(child_pivot_panel.reshape(8, 2, B, B))
    outgoing = contributions(tab, child_update_blocks.reshape(16, B, 8, B), row_op.reshape(8, 16, B, B), col_op)
    incoming = lax.all_to_all(outgoing, ("row", "col"), split_axis=0, concat_axis=0, tiled=True)
    arrived = incoming.reshape(256, B, B)
    kept = jnp.concatenate([jnp.ones((NB,), F32), coupled.astype(F32)])
    keep = jnp.concatenate(
        [
            lax.dynamic_index_in_dim(kept.reshape(16, 8), my_row, 1, keepdims=False),
            lax.dynamic_index_in_dim(kept.reshape(8, 16), my_col, 1, keepdims=False),
        ]
    )
    pivots = pivot_columns(tab, arrived, front[:, :, 0, :])
    square, portion, cols = pivot_gather(pivots.reshape(8, 2, B, B))
    below, panel, first = factor(square, portion.reshape(8, 16, B, B), cols, keep)
    out = schur(tab, front, arrived, below, panel, first)
    return out.reshape(1, 16, B, 1, 8, B)


def solution(mesh):
    in_specs = (
        P("row", None, None, "col", None, None),
        P("row", None, None, "col", None),
        P(),
        P(),
        P("row", None, None, "col", None, None),
    )
    out_specs = P("row", None, None, "col", None, None)
    return jax.shard_map(per_device, mesh=mesh, in_specs=in_specs, out_specs=out_specs, check_vma=False)
```

time: 1070 us -> 518 us (0.48)
  Pallas kernels: 0 us -> 401 us
  other arithmetic: 368 us -> 0.66 us
  waiting for transfers between devices: 433 us -> 94.8 us
  local copies, waits for them, and re-layouts: 116 us -> 4.64 us
  matrix products: 108 us -> 0 us
  between operations: 19.4 us -> 0.07 us
    pallas_call x0 -> x7, Pallas kernels: none -> 401 us  [the longest x1 198 us: pivot_gather(): pl.pallas_call(pivot_gather_kernel, out_shape=(jax.ShapeDtypeStruct((8, 8...]
    another operation x39 -> x0, other arithmetic: 323 us -> none  [the longest x31 173 us: pivot_factor(): lower_factor = jnp.linalg.cholesky(0.5 * (square + square.T))]
    all_gather x2 -> x0, waiting for transfers between devices: 197 us -> none  [the longest x1 197 us: per_device(): lax.all_gather(pivot_piece[None, :own_pivot_rows], ('row', 'col'), axis=0...]
    ppermute x7 -> x0, waiting for transfers between devices: 131 us -> none  [from_partner(): return lax.ppermute(value, axis, pairs)]
    psum x1 -> x0, waiting for transfers between devices: 78.7 us -> none  [from_root(): return lax.psum(jnp.where(mine, array, jnp.zeros_like(array)), axis)]
    all_to_all x1, waiting for transfers between devices: 26.7 us -> 94.8 us  [per_device(): lax.all_to_all(outgoing, ('row', 'col'), split_axis=0, concat_axis=0, til...]
    dot_general x6 -> x0, matrix products: 58.3 us -> none  [the longest x1 14.3 us: per_device(): lax.dot_general(below_half, col_panel.reshape(parent_cols * BLOCK_ORDER,...]
    another operation x29 -> x0, matrix products: 50 us -> none  [the longest x15 27 us: pivot_factor(): jax.scipy.linalg.solve_triangular(lower_factor, jnp.eye(square.shape[0],...]
  transfers between devices with their start and end apart: 11 -> 1, of which waited for: 10 -> 1; matrix products, arithmetic and copies ran while one was open for 44% -> 1% of each run, Pallas kernels for 0% -> 0%
where the time goes in v1:
time: 518 us; the launch traced here: 515 us
  Pallas kernels  401 us (77%)
  waiting for transfers between devices  94.8 us (18%)
  starting transfers between devices  13.8 us (3%)
    pallas_call x1, Pallas kernels, pivot_gather(): pl.pallas_call(pivot_gather_kernel, out_shape=(jax.ShapeDtypeStruct((8, 8...  198 us
    all_to_all x1, waiting for transfers between devices, per_device(): lax.all_to_all(outgoing, ('row', 'col'), split_axis=0, concat_axis=0, til...  94.8 us
    pallas_call x1, Pallas kernels, panel_gather(): pl.pallas_call(panel_gather_kernel, out_shape=(jax.ShapeDtypeStruct((8, 8...  76.3 us
    pallas_call x1, Pallas kernels, factor(): pl.pallas_call(factor_kernel, out_shape=FACTOR_OUT, in_specs=[VM, VM, VM,...  70.7 us
    pallas_call x1, Pallas kernels, schur(): pl.pallas_call(schur_kernel, out_shape=jax.ShapeDtypeStruct((16, B, 8, B)...  22.6 us
    pallas_call x1, Pallas kernels, contributions(): pl.pallas_call(contribution_kernel, out_shape=jax.ShapeDtypeStruct((128,...  14.6 us
    all_to_all x1, starting transfers between devices, per_device(): lax.all_to_all(outgoing, ('row', 'col'), split_axis=0, concat_axis=0, til...  13.8 us
  transfers between devices with their start and end apart: 1, of which 1 were waited for; matrix products, arithmetic and copies ran while one was open for 1% of the time, Pallas kernels for 0%

profile of v1, /device:TPU:112, one launch (start us, length us, event | category | flops | bytes accessed | tf_op | source)
XLA Modules:
  0.0 514.6 jit_solution(17276920724739146895)
XLA Ops:
  0.0 9.2 %shard_map.55.tab = s32[128]{0:T(128)} custom-call(s32[4,64]{1,0:T(4,128)} %map_ref.1), custom_call_target="tpu_custom_call" | custom-call | tf_op jit(solution)/shard_map/pallas_call | solution.py:84
  9.2 76.3 %shard_map.56 = (bf16[8,8,2,128,128]{4,3,2,1,0:T(8,128)(2,1)}, bf16[8,8,128,128]{3,2,1,0:T(8,128)(2,1)}) custom-call(bf16[8,2,128,128]{3,2,1,0:T(8,128)(2,1)} %bitcast.21), custom_call_target="tpu_custom_call" | custom-call | tf_op jit(solution)/shard_map/pallas_call | solution.py:191
  85.5 14.6 %shard_map.57 = bf16[128,256,128]{2,1,0:T(8,128)(2,1)} custom-call(s32[128]{0:T(128)} %shard_map.55.tab, bf16[16,128,8,128]{3,2,1,0:T(8,128)(2,1)} %bitcast.13, bf16[16,128,8,128]{3,2,1,0:T(8,128)(2,1)} %bitcast.14, bf16[8,16,128,128]{3,2,1,0:T(8,128)(2,1)} %bitcast.17, bf16[8,8,128,128]{3,2,1,0:T(8,128)(2,1)} %get-tuple-element.14.col_ref), custom_call_target="tpu_custom_call" | custom-call | tf_op jit(solution)/shard_map/pallas_call | solution.py:232
  100.1 0.0 copy-start
  100.1 13.8 %all-to-all-start = ((bf16[128,256,128]{2,1,0:T(8,128)(2,1)}), bf16[128,256,128]{2,1,0:T(8,128)(2,1)}, u32[]{:S(2)}, u32[]{:S(2)}) async-start(bf16[128,256,128]{2,1,0:T(8,128)(2,1)} %shard_map.57), calls=%async_computation | async-start | bytes 16777216 | tf_op jit(solution)/shard_map/all_to_all | solution.py:696
  114.0 0.0 copy-done
  114.0 0.1 concatenate.6
  114.0 0.1 reshape.38
  114.1 0.1 reshape.37
  114.2 3.1 slice.4
  117.3 0.9 copy.10
  118.3 0.2 dynamic-slice_reduce_fusion.1
  118.4 0.2 dynamic-slice_reduce_fusion
  118.6 0.7 pad_maximum_fusion.keep_ref
  119.3 94.8 %all-to-all-done = bf16[128,256,128]{2,1,0:T(8,128)(2,1)} async-done(((bf16[128,256,128]{2,1,0:T(8,128)(2,1)}), bf16[128,256,128]{2,1,0:T(8,128)(2,1)}, u32[]{:S(2)}, u32[]{:S(2)}) %all-to-all-start) | async-done | bytes 8388640 | tf_op jit(solution)/shard_map/all_to_all | solution.py:696
  214.1 9.3 %shard_map.58 = bf16[16,128,128]{2,1,0:T(8,128)(2,1)} custom-call(s32[128]{0:T(128)} %shard_map.55.tab, bf16[256,128,128]{2,1,0:T(8,128)(2,1)} %bitcast.4.c0.c1.arrived, bf16[256,128,128]{2,1,0:T(8,128)(2,1)} %bitcast.4.c0.c1.arrived, bf16[16,128,128]{2,1,0:T(8,128)(2,1)} %bitcast.19), custom_call_target="tpu_custom_call" | custom-call | tf_op jit(solution)/shard_map/pallas_call | solution.py:260
  223.3 198.0 %shard_map.59 = (bf16[8,8,128,128]{3,2,1,0:T(8,128)(2,1)}, bf16[8,8,2,128,128]{4,3,2,1,0:T(8,128)(2,1)}, bf16[8,8,128,128]{3,2,1,0:T(8,128)(2,1)}) custom-call(bf16[8,2,128,128]{3,2,1,0:T(8,128)(2,1)} %bitcast.20), custom_call_target="tpu_custom_call" | custom-call | tf_op jit(solution)/shard_map/pallas_call | solution.py:457
  421.4 70.7 %shard_map.60 = (bf16[2048,1024]{1,0:T(8,128)(2,1)}, bf16[1024,1024]{1,0:T(8,128)(2,1)}, f32[16,128,128]{2,1,0:T(8,128)}) custom-call(bf16[8,8,128,128]{3,2,1,0:T(8,128)(2,1)} %get-tuple-element.15.sq_ref, bf16[8,16,128,128]{3,2,1,0:T(8,128)(2,1)} %bitcast.18, bf16[8,8,128,128]{3,2,1,0:T(8,128)(2,1)} %get-tuple-element.17.cols_ref, f32[24]{0:T(128)} %pad_maximum_fusion.keep_ref), custom_call_target="tpu_custom_call" | custom-call | tf_op jit(solution)/shard_map/pallas_call | solution.py:637
  492.0 22.6 %shard_map.61 = f32[16,128,8,128]{3,2,1,0:T(8,128)} custom-call(s32[128]{0:T(128)} %shard_map.55.tab, bf16[16,128,8,128]{3,2,1,0:T(8,128)(2,1)} %bitcast.16, bf16[256,128,128]{2,1,0:T(8,128)(2,1)} %bitcast.4.c0.c1.arrived, bf16[2048,1024]{1,0:T(8,128)(2,1)} %get-tuple-element.18.below, bf16[1024,1024]{1,0:T(8,128)(2,1)} %get-tuple-element.19.panel, ...), custom_call_target="tpu_custom_call" | custom-call | tf_op jit(solution)/shard_map/pallas_call | solution.py:670
  (1 shorter events, 0.0 us)
Async XLA Ops:
  100.1 13.9 %copy-start = (s32[120]{0:T(128)S(1)}, s32[120]{0:T(128)}, u32[]{:S(2)}) copy-start(s32[120]{0:T(128)} %param.8) | copy-start | bytes 1444
  100.1 114.0 %all-to-all-start = ((bf16[128,256,128]{2,1,0:T(8,128)(2,1)}), bf16[128,256,128]{2,1,0:T(8,128)(2,1)}, u32[]{:S(2)}, u32[]{:S(2)}) async-start(bf16[128,256,128]{2,1,0:T(8,128)(2,1)} %shard_map.57), calls=%async_computation | async-start | bytes 16777216 | tf_op jit(solution)/shard_map/all_to_all | solution.py:696

commit v2 on v1

v2 whole, which is shorter than its diff:
```python
import functools

import jax
import jax.numpy as jnp
from jax import lax
from jax.experimental import pallas as pl
from jax.experimental.pallas import tpu as pltpu
from jax.sharding import PartitionSpec as P

B = 128
NB = 8
N = NB * B
F32 = jnp.float32
BF = jnp.bfloat16
MESH = pl.DeviceIdType.MESH
ANY = pl.BlockSpec(memory_space=pl.ANY)
VM = pl.BlockSpec(memory_space=pltpu.VMEM)
SM = pl.BlockSpec(memory_space=pltpu.SMEM)
LIMIT = 56 * 1024 * 1024


def params(**kw):
    return pltpu.CompilerParams(vmem_limit_bytes=LIMIT, **kw)


OUT_ROW, OUT_COL = 0, 16
AT_RSRC, AT_RCH, AT_CSRC, AT_CCH = 0, 32, 64, 80


def clear(count):
    def one(i, _):
        count[i] = 0
        return 0

    lax.fori_loop(0, 16, one, 0)


def outgoing_kernel(map_ref, tab_ref, count):
    my_row, my_col = lax.axis_index("row"), lax.axis_index("col")
    row_rank, col_rank = my_row % 4, my_col % 8
    child = 2 * (my_row // 4) + my_col // 8
    clear(count)
    for l in range(16):
        owner = map_ref[child, l * 4 + row_rank] % 8
        tab_ref[OUT_ROW + owner * 2 + count[owner]] = l
        count[owner] = count[owner] + 1
    for m in range(8):
        tab_ref[OUT_COL + m] = map_ref[child, m * 8 + col_rank] % 16


def incoming_kernel(map_ref, tab_ref, count):
    my_row, my_col = lax.axis_index("row"), lax.axis_index("col")
    clear(count)

    def arrive(q, _):
        h, g = q // 2, q % 2

        def one(b, _):
            target = map_ref[q, b]

            @pl.when(target % 8 == my_row)
            def _():
                slot = q * 4 + b % 4
                at = h * 16 + target // 8
                tab_ref[AT_RSRC + at] = (h * 4 + b % 4) * 32 + count[slot]
                tab_ref[AT_RCH + at] = g
                count[slot] = count[slot] + 1

            @pl.when(target % 16 == my_col)
            def _():
                at = h * 8 + target // 16
                tab_ref[AT_CSRC + at] = (g * 8 + b % 8) * 2
                tab_ref[AT_CCH + at] = g

            return 0

        lax.fori_loop(0, 64, one, 0)
        return 0

    lax.fori_loop(0, 4, arrive, 0)


def table(kernel, size, child_map):
    return pl.pallas_call(
        kernel,
        out_shape=jax.ShapeDtypeStruct((size,), jnp.int32),
        in_specs=[SM],
        out_specs=SM,
        scratch_shapes=[pltpu.SMEM((16,), jnp.int32)],
        cost_estimate=pl.CostEstimate(flops=20000, bytes_accessed=2048, transcendentals=0),
    )(child_map)


def remote(src, dst, s, r, row, col):
    return pltpu.make_async_remote_copy(
        src_ref=src, dst_ref=dst, send_sem=s, recv_sem=r, device_id=(row, col), device_id_type=MESH
    )


def panel_gather_kernel(p_ref, row_ref, col_ref, local, s_chip, s_sib, s_col, r_row, r_col):
    my_row, my_col = lax.axis_index("row"), lax.axis_index("col")
    base, y = my_row // 4 * 4, my_row % 4
    half, cc = my_col // 8 * 8, my_col % 8
    core, pair, parity = cc % 2, cc // 2, cc // 4
    sibling = half + pair * 2 + 1 - core
    y0 = cc % 4
    step = jnp.where(y0 % 2 == 0, 3, 1)
    outer = (y0 + step) % 4
    inner = y0 + 1 - 2 * (y0 % 2)
    last = outer + 1 - 2 * (outer % 2)
    is_source, is_relay = y == y0, y == outer
    barrier = pltpu.get_barrier_semaphore()

    def greet(row, col):
        pl.semaphore_signal(barrier, inc=1, device_id=(row, col), device_id_type=MESH)

    others = [half + (pair + d) % 4 * 2 + core for d in (2, 1, 3)]
    for col in others:
        greet(my_row, col)
    greet(my_row, sibling)

    @pl.when(jnp.logical_not(is_source))
    def _():
        greet(base + jnp.where(y == last, outer, y0), my_col)

    pl.semaphore_wait(barrier, 4 + jnp.where(is_source, 2, jnp.where(is_relay, 1, 0)))

    order = [cc, pair * 2 + 1 - core] + [(pair + d) % 4 * 2 + core for d in (2, 1, 3)]
    order += [(pair + d) % 4 * 2 + 1 - core for d in (2, 1, 3)]

    def own():
        return pltpu.make_async_copy(p_ref, row_ref.at[cc], local.at[8])

    def chip_send(i):
        return remote(p_ref, row_ref.at[cc], s_chip.at[i], r_row.at[cc], my_row, others[i])

    def sib_send(e):
        src = p_ref if e == 0 else row_ref.at[order[e]]
        return remote(src, row_ref.at[order[e]], s_sib.at[max(e - 1, 0)], r_row.at[order[e]], my_row, sibling)

    def part(e):
        return p_ref.at[:, parity] if e == 0 else row_ref.at[order[e], :, parity]

    def keep(e):
        return pltpu.make_async_copy(part(e), col_ref.at[order[e]], local.at[e])

    def col_send(e, t):
        return remote(part(e), col_ref.at[order[e]], s_col.at[e, t], r_col.at[order[e]], base + (outer, inner)[t], my_col)

    def pass_on(e):
        j = order[e]
        return remote(col_ref.at[j], col_ref.at[j], s_col.at[e, 0], r_col.at[j], base + last, my_col)

    own().start()
    for i in range(3):
        chip_send(i).start()
    sib_send(0).start()
    for e in range(9):
        if e < 8:
            if e:
                remote(p_ref, row_ref.at[order[e]], s_sib.at[0], r_row.at[order[e]], my_row, sibling).wait_recv()
            if 2 <= e < 5:
                sib_send(e).start()

            @pl.when(is_source)
            def _():
                col_send(e, 0).start()
                col_send(e, 1).start()
                keep(e).start()

        if e:

            @pl.when(is_relay)
            def _():
                pass_on(e - 1).wait_recv()
                pass_on(e - 1).start()

    @pl.when(jnp.logical_not(is_source | is_relay))
    def _():
        for e in range(8):
            pass_on(e).wait_recv()

    own().wait()
    for i in range(3):
        chip_send(i).wait_send()
    for e in (0, 2, 3, 4):
        sib_send(e).wait_send()

    @pl.when(is_source)
    def _():
        for e in range(8):
            keep(e).wait()
            col_send(e, 0).wait_send()
            col_send(e, 1).wait_send()

    @pl.when(is_relay)
    def _():
        for e in range(8):
            pass_on(e).wait_send()


def panel_gather(piece):
    return pl.pallas_call(
        panel_gather_kernel,
        out_shape=(
            jax.ShapeDtypeStruct((8, 8, 2, B, B), BF),
            jax.ShapeDtypeStruct((8, 8, B, B), BF),
        ),
        in_specs=[ANY],
        out_specs=(ANY, ANY),
        scratch_shapes=[
            pltpu.SemaphoreType.DMA((9,)),
            pltpu.SemaphoreType.DMA((3,)),
            pltpu.SemaphoreType.DMA((4,)),
            pltpu.SemaphoreType.DMA((8, 2)),
            pltpu.SemaphoreType.DMA((8,)),
            pltpu.SemaphoreType.DMA((8,)),
        ],
        compiler_params=params(collective_id=1, has_side_effects=True),
    )(piece)


def contribution_kernel(tab, u0, u1, row_ref, col_ref, out_ref, right):
    owner = pl.program_id(0)

    @pl.when(owner == 0)
    def _():
        for k in range(8):
            for m in range(8):
                right[m * B : (m + 1) * B, k * B : (k + 1) * B] = col_ref[k, m]

    left = []
    for s in range(2):
        l = tab[OUT_ROW + owner * 2 + s]
        left.append(jnp.concatenate([row_ref[k, l] for k in range(8)], axis=1))
    left = jnp.concatenate(left, axis=0)
    product = lax.dot_general(left, right[...], (((1,), (1,)), ((), ())), preferred_element_type=F32)
    for s, u in enumerate((u0, u1)):
        update = jnp.swapaxes(u[0], 0, 1)
        for m in range(8):
            value = update[m].astype(F32) - product[s * B : (s + 1) * B, m * B : (m + 1) * B]
            out_ref[tab[OUT_COL + m], s * B : (s + 1) * B, :] = value.astype(BF)


def contributions(tab, update, row_op, col_op):
    full = lambda shape: pl.BlockSpec(shape, lambda i, t: (0,) * len(shape))
    u_spec = lambda s: pl.BlockSpec((1, B, 8, B), lambda i, t: (t[OUT_ROW + 2 * i + s], 0, 0, 0))
    return pl.pallas_call(
        contribution_kernel,
        out_shape=jax.ShapeDtypeStruct((128, 2 * B, B), BF),
        grid_spec=pltpu.PrefetchScalarGridSpec(
            num_scalar_prefetch=1,
            grid=(8,),
            in_specs=[u_spec(0), u_spec(1), full((8, 16, B, B)), full((8, 8, B, B))],
            out_specs=pl.BlockSpec((16, 2 * B, B), lambda i, t: (i, 0, 0)),
            scratch_shapes=[pltpu.VMEM((N, N), BF)],
        ),
        compiler_params=params(),
    )(tab, update, update, row_op, col_op)


def pivot_kernel(tab, arrived, front, out_ref, block, sem):
    def fits(l, h):
        return tab[AT_RCH + h * 16 + l] == tab[AT_CCH + h * 8]

    def fetch(l, h):
        at = jnp.where(fits(l, h), tab[AT_RSRC + h * 16 + l] + tab[AT_CSRC + h * 8], 0)
        return pltpu.make_async_copy(arrived.at[at], block.at[h, l], sem.at[h, l])

    for l in range(16):
        for h in range(2):
            fetch(l, h).start()
    for l in range(16):
        value = front[l].astype(F32)
        for h in range(2):
            valid = fits(l, h)
            fetch(l, h).wait()
            value = value + jnp.where(valid, block[h, l].astype(F32), 0.0)
        out_ref[l] = value.astype(BF)


def pivot_columns(tab, arrived, front):
    return pl.pallas_call(
        pivot_kernel,
        out_shape=jax.ShapeDtypeStruct((16, B, B), BF),
        in_specs=[SM, ANY, VM],
        out_specs=VM,
        scratch_shapes=[pltpu.VMEM((2, 16, B, B), BF), pltpu.SemaphoreType.DMA((2, 16))],
        compiler_params=params(),
    )(tab, arrived, front)


class Gather:
    SEMS = (2, 7, 7, 4, 3, 2, 4, 8, 8, 8, 8, 8)

    def __init__(self, piece, sq, portion, cols, sems):
        self.piece, self.sq, self.portion, self.cols = piece, sq, portion, cols
        (self.local, self.s_row, self.s_sq, self.s_sqf, self.s_z, self.s_x, self.s_sib, self.s_cols) = sems[:8]
        self.r_row, self.r_sq, self.r_por, self.r_cols = sems[8:]
        self.row, self.col = lax.axis_index("row"), lax.axis_index("col")
        col = self.col
        self.z, self.xh, self.core = col // 4, col // 2 % 2, col % 2
        self.zh = self.z // 2
        self.chip = col // 2
        self.sibling = self.chip * 2 + 1 - self.core
        self.across = self.z * 4 + (1 - self.xh) * 2 + self.core
        self.owner = col < 8
        self.same = col % 8 == self.row

    def chips(self):
        return [(self.chip + d) % 8 * 2 + self.core for d in (4, 1, 7, 2, 6, 3, 5)]

    def enter(self):
        barrier = pltpu.get_barrier_semaphore()

        def greet(row, col):
            pl.semaphore_signal(barrier, inc=1, device_id=(row, col), device_id_type=MESH)

        greet(self.row, self.sibling)
        greet(self.row, self.across)

        @pl.when(self.owner)
        def _():
            for d in range(1, 8):
                greet((self.row + d) % 8, self.col)

        for i in range(4):
            j = 2 * i + self.core

            @pl.when(j != self.col)
            def _():
                greet(self.row, j)

        for d in range(8):
            j = (self.col + d) % 8
            if d:
                greet(self.col % 8, self.zh * 8 + j)
            else:

                @pl.when(jnp.logical_not(self.same))
                def _():
                    greet(self.col % 8, self.zh * 8 + j)

        pl.semaphore_wait(barrier, 10 + jnp.where(self.owner, 14, 0) - jnp.where(self.same, 1, 0))

    def row_sends(self):
        dst = self.sq.at[self.col, self.row]
        return [
            remote(self.piece.at[0, 0], dst, self.s_row.at[d - 1], self.r_row.at[self.row], (self.row + d) % 8, self.col)
            for d in range(1, 8)
        ]

    def sq_sends(self):
        c = self.sq.at[self.col]
        return [
            remote(c, c, self.s_sq.at[i], self.r_sq.at[self.col], self.row, t) for i, t in enumerate(self.chips())
        ]

    def z_sends(self):
        c = self.portion.at[self.col]
        return [
            remote(self.piece, c, self.s_z.at[d - 1], self.r_por.at[self.col], self.row, (self.col + 4 * d) % 16)
            for d in (2, 1, 3)
        ]

    def x_sends(self):
        out = []
        for zp in range(2):
            j = zp * 4 + self.xh * 2 + self.core
            out.append(remote(self.portion.at[j], self.portion.at[j], self.s_x.at[zp], self.r_por.at[j], self.row, self.across))
        return out

    def sib_sends(self):
        out = []
        for i in range(4):
            j = 2 * i + self.core
            out.append(remote(self.portion.at[j], self.portion.at[j], self.s_sib.at[i], self.r_por.at[j], self.row, self.sibling))
        return out

    def cols_send(self, d):
        j = self.col % 8
        src = self.portion.at[j, :, self.zh]
        return remote(
            src, self.cols.at[j], self.s_cols.at[d], self.r_cols.at[j], (self.row + d) % 8, self.row + 8 * self.zh
        )

    def cols_sends(self):
        return [self.cols_send(d) for d in (4, 1, 3, 5, 7, 2, 6)]

    def arrived(self, ref, sem):
        remote(ref, ref, self.s_row.at[0], sem, self.row, self.sibling).wait_recv()

    def square(self):
        @pl.when(self.owner)
        def _():
            first = pltpu.make_async_copy(self.piece.at[0, 0], self.sq.at[self.col, self.row], self.local.at[0])
            whole = pltpu.make_async_copy(self.piece, self.portion.at[self.col], self.local.at[1])
            first.start()
            for s in self.row_sends():
                s.start()
            whole.start()
            first.wait()
            for d in range(1, 8):
                i = (self.row + d) % 8
                self.arrived(self.sq.at[self.col, i], self.r_row.at[i])
            for s in self.sq_sends():
                s.start()
            whole.wait()

        for i in range(4):
            j = 2 * i + self.core

            @pl.when(j != self.col)
            def _():
                self.arrived(self.sq.at[j], self.r_sq.at[j])

            c = self.sq.at[j]
            remote(c, c, self.s_sqf.at[i], self.r_sq.at[j], self.row, self.sibling).start()
        for i in range(4):
            j = 2 * i + 1 - self.core
            self.arrived(self.sq.at[j], self.r_sq.at[j])

    def cols_start(self):
        for s in self.cols_sends():
            s.start()

        @pl.when(jnp.logical_not(self.same))
        def _():
            self.cols_send(0).start()

    def keep_cols(self):
        j = self.col % 8
        return pltpu.make_async_copy(self.portion.at[j, :, self.zh], self.cols.at[j], self.local.at[0])

    def first(self):
        @pl.when(self.owner)
        def _():
            for s in self.z_sends():
                s.start()
            self.cols_start()

    def second(self):
        for zp in range(2):
            j = zp * 4 + self.xh * 2 + self.core

            @pl.when(j != self.col)
            def _():
                self.arrived(self.portion.at[j], self.r_por.at[j])

        for s in self.x_sends():
            s.start()

        @pl.when(jnp.logical_not(self.owner))
        def _():
            self.cols_start()

        @pl.when(self.same)
        def _():
            self.keep_cols().start()

    def third(self):
        for zp in range(2):
            j = zp * 4 + (1 - self.xh) * 2 + self.core
            self.arrived(self.portion.at[j], self.r_por.at[j])
        for s in self.sib_sends():
            s.start()

    def last(self):
        for i in range(4):
            j = 2 * i + 1 - self.core
            self.arrived(self.portion.at[j], self.r_por.at[j])
        for d in range(1, 8):
            j = (self.col + d) % 8
            self.arrived(self.cols.at[j], self.r_cols.at[j])

        @pl.when(self.same)
        def _():
            self.keep_cols().wait()

        @pl.when(jnp.logical_not(self.same))
        def _():
            j = self.col % 8
            self.arrived(self.cols.at[j], self.r_cols.at[j])

    def finish(self):
        for i in range(4):
            c = self.sq.at[2 * i + self.core]
            remote(c, c, self.s_sqf.at[i], self.r_sq.at[0], self.row, self.sibling).wait_send()
        for s in self.x_sends() + self.sib_sends() + self.cols_sends():
            s.wait_send()

        @pl.when(jnp.logical_not(self.same))
        def _():
            self.cols_send(0).wait_send()

        @pl.when(self.owner)
        def _():
            for s in self.row_sends() + self.sq_sends() + self.z_sends():
                s.wait_send()


def splits(a):
    parts = []
    for i in range(3):
        h = a.astype(BF)
        parts.append(h)
        if i < 2:
            a = a - h.astype(F32)
    return parts


LEFT = (0, 0, 1, 1, 0, 2)
RIGHT = (0, 1, 0, 1, 2, 0)


def dot_f32(a, b, dims):
    sa, sb = splits(a), splits(b)
    left = jnp.concatenate([sa[i] for i in LEFT], axis=dims[0][0])
    right = jnp.concatenate([sb[i] for i in RIGHT], axis=dims[1][0])
    return lax.dot_general(left, right, (dims, ((), ())), preferred_element_type=F32)


def diagonal_factor(square):
    group = 16
    lane = lax.broadcasted_iota(jnp.int32, (8, B), 1)
    sub = lax.broadcasted_iota(jnp.int32, (8, B), 0)
    spread = lambda x, s: jnp.broadcast_to(x[s : s + 1, :], (8, B))
    rest, upper, lower = square, [], []
    for g in range(B // group):
        r0 = group * g
        p = [rest[8 * v : 8 * v + 8, :] for v in range(2)]
        column = [[jnp.broadcast_to(p[v][:, r0 + j : r0 + j + 1], (8, B)) for v in range(2)] for j in range(group)]
        root = [jnp.zeros((8, B), F32) for _ in range(2)]
        for k in range(group):
            at, s = divmod(k, 8)
            r = lax.rsqrt(spread(column[k][at], s))
            root[at] = jnp.where(sub == s, r, root[at])
            if k == group - 1:
                break
            here = lane == r0 + k
            row = jnp.where(here, 1.0, spread(p[at], s))
            for v in range(at, 2):
                if v == at and s == 7:
                    continue
                factor = column[k][v] * (r * r)
                if v == at:
                    factor = jnp.where(sub > s, factor, 0.0)
                    p[v] = jnp.where(here & (sub > s), 0.0, p[v]) - factor * row
                else:
                    p[v] = jnp.where(here, 0.0, p[v]) - factor * row
                for j in range(k + 1, group):
                    column[j][v] = column[j][v] - factor * spread(column[j][at], s)
        panel = jnp.concatenate([p[v] * root[v] for v in range(2)], axis=0)
        roots = jnp.concatenate(root, axis=0)
        ln = lax.broadcasted_iota(jnp.int32, (group, B), 1) - r0
        sb = lax.broadcasted_iota(jnp.int32, (group, B), 0)
        eliminated = jnp.where(ln == sb, roots, jnp.where((ln > sb) & (ln < group), 0.0, panel))
        upper.append(panel)
        lower.append(jnp.where(ln > sb, 0.0, eliminated))
        if g < B // group - 1:
            change = dot_f32(jnp.where(ln >= group, panel, 0.0), eliminated, ((0,), (0,)))
            lt = lax.broadcasted_iota(jnp.int32, (B - r0 - group, B), 1)
            rest = jnp.where((lt >= r0) & (lt < r0 + group), 0.0, rest[group:, :]) - change[r0 + group :, :]
    return jnp.concatenate(upper, axis=0), jnp.concatenate(lower, axis=0)


def factor_start(sq_ref, lower_ref, work):
    for i in range(NB):
        for j in range(NB):
            at = (slice(i * B, (i + 1) * B), slice(j * B, (j + 1) * B))
            if j < i:
                work[at] = jnp.zeros((B, B), F32)
            else:
                work[at] = 0.5 * (sq_ref[j, i].astype(F32) + sq_ref[i, j].astype(F32).T)
    lower_ref[...] = jnp.zeros((B, B), F32)


def factor_step(kb, my_row, my_col, inv_ref, lower_ref, work, left, right):
    lane = lax.broadcasted_iota(jnp.int32, (B, B), 1)
    sub = lax.broadcasted_iota(jnp.int32, (B, B), 0)
    d0 = pl.multiple_of(kb * B, B)
    upper, lower = diagonal_factor(work[pl.ds(d0, B), pl.ds(d0, B)])
    work[pl.ds(d0, B), pl.ds(d0, B)] = jnp.where(lane == sub, 1.0, 0.0)
    panel = dot_f32(lower, work[pl.ds(d0, B), :], ((1,), (0,)))
    col = lax.broadcasted_iota(jnp.int32, (B, N), 1)
    inv_ref[pl.ds(d0, B), :] = jnp.where(col < d0 + B, panel, 0.0).astype(BF)

    @pl.when(kb == my_col)
    def _():
        @pl.when(kb == my_row)
        def _():
            lower_ref[...] = jnp.where(lane >= sub, upper, 0.0).T

        @pl.when(kb < my_row)
        def _():
            work[pl.ds(d0, B), :] = panel
            lower_ref[...] = work[pl.ds(d0, B), pl.ds(pl.multiple_of(my_row * B, B), B)].T

    parts = splits(panel)
    for t in range(6):
        left[t * B : (t + 1) * B, :] = parts[LEFT[t]]
        right[t * B : (t + 1) * B, :] = parts[RIGHT[t]]

    def trailing(i, _):
        i0 = pl.multiple_of(i * B, B)
        work[pl.ds(i0, B), pl.ds(d0, B)] = jnp.zeros((B, B), F32)
        work[pl.ds(i0, B), :] = work[pl.ds(i0, B), :] - lax.dot_general(
            left[:, pl.ds(i0, B)], right[...], (((0,), (0,)), ((), ())), preferred_element_type=F32
        )
        return 0

    lax.fori_loop(kb + 1, NB, trailing, 0)


def below_rows(portion, cols, inv_ref, lower_ref, keep_ref, my_col, below_ref, panel_ref, first_ref, wide):
    safe = jnp.minimum(my_col, NB - 1)
    dims = (((1,), (1,)), ((), ()))

    def rows(i, _):
        a = jnp.concatenate(
            [jnp.concatenate([portion[k, 2 * i + t // 2, t % 2] for k in range(8)], axis=1) for t in range(4)], axis=0
        )
        out = lax.dot_general(a, inv_ref[...], dims, preferred_element_type=F32)
        for t in range(4):
            l = 4 * i + t
            kept = out[t * B : (t + 1) * B, :] * keep_ref[l]
            wide[t * B : (t + 1) * B, :] = kept
            below_ref[pl.ds(pl.multiple_of(l * B, B), B), :] = kept.astype(BF)
        for t in range(4):
            first_ref[4 * i + t] = wide[t * B : (t + 1) * B, pl.ds(pl.multiple_of(safe * B, B), B)]
        return 0

    lax.fori_loop(0, 4, rows, 0)
    first_ref[0] = lower_ref[...]

    def more(i, _):
        a = jnp.concatenate(
            [jnp.concatenate([cols[k, 4 * i + t] for k in range(8)], axis=1) for t in range(4)], axis=0
        )
        out = lax.dot_general(a, inv_ref[...], dims, preferred_element_type=F32)
        for t in range(4):
            m = 4 * i + t
            kept = out[t * B : (t + 1) * B, :] * keep_ref[16 + m]
            panel_ref[pl.ds(pl.multiple_of(m * B, B), B), :] = kept.astype(BF)
        return 0

    lax.fori_loop(0, 2, more, 0)


def factor_kernel(piece, keep_ref, below_ref, panel_ref, first_ref, sq, portion, cols, inv_ref, lower_ref, work, left, right, wide, *sems):
    my_row, my_col = lax.axis_index("row"), lax.axis_index("col")
    gather = Gather(piece, sq, portion, cols, sems)
    gather.enter()
    gather.square()
    gather.first()
    factor_start(sq, lower_ref, work)

    def step(kb, _):
        @pl.when(kb == 3)
        def _():
            gather.second()

        @pl.when(kb == 7)
        def _():
            gather.third()

        factor_step(kb, my_row, my_col, inv_ref, lower_ref, work, left, right)
        return 0

    lax.fori_loop(0, NB, step, 0)
    gather.last()
    below_rows(portion, cols, inv_ref, lower_ref, keep_ref, my_col, below_ref, panel_ref, first_ref, wide)
    gather.finish()


FACTOR_OUT = (
    jax.ShapeDtypeStruct((16 * B, N), BF),
    jax.ShapeDtypeStruct((8 * B, N), BF),
    jax.ShapeDtypeStruct((16, B, B), F32),
)
FACTOR_SCRATCH = (
    ((8, 8, B, B), BF),
    ((8, 8, 2, B, B), BF),
    ((8, 8, B, B), BF),
    ((N, N), BF),
    ((B, B), F32),
    ((N, N), F32),
    ((6 * B, N), BF),
    ((6 * B, N), BF),
    ((4 * B, N), F32),
)


def factor(piece, keep):
    return pl.pallas_call(
        factor_kernel,
        out_shape=FACTOR_OUT,
        in_specs=[ANY, SM],
        out_specs=(VM, VM, VM),
        scratch_shapes=[pltpu.VMEM(s, d) for s, d in FACTOR_SCRATCH]
        + [pltpu.SemaphoreType.DMA((n,)) for n in Gather.SEMS],
        compiler_params=params(collective_id=2, has_side_effects=True),
    )(piece, keep)


def schur_kernel(tab, front, arrived, below, panel, first, out_ref):
    i = pl.program_id(0)
    my_col = lax.axis_index("col")
    product = lax.dot_general(below[...], panel[...], (((1,), (1,)), ((), ())), preferred_element_type=F32)
    for s in range(2):
        l = 2 * i + s
        initial = jnp.swapaxes(front[s], 0, 1)
        values = []
        for m in range(8):
            value = initial[m].astype(F32)
            for h in range(2):
                valid = tab[AT_RCH + h * 16 + l] == tab[AT_CCH + h * 8 + m]
                at = jnp.where(valid, tab[AT_RSRC + h * 16 + l] + tab[AT_CSRC + h * 8 + m], 0)
                value = value + jnp.where(valid, arrived[at].astype(F32), 0.0)
            value = value - product[s * B : (s + 1) * B, m * B : (m + 1) * B]
            if s == 0:
                value = jnp.where(l == 0, 0.0, value)
            if m == 0:
                value = jnp.where(my_col < NB, first[s], value)
            values.append(value)
        out_ref[s] = jnp.swapaxes(jnp.stack(values), 0, 1)


def schur(tab, front, arrived, below, panel, first):
    full = lambda shape: pl.BlockSpec(shape, lambda i, t: (0,) * len(shape))
    return pl.pallas_call(
        schur_kernel,
        out_shape=jax.ShapeDtypeStruct((16, B, 8, B), F32),
        grid_spec=pltpu.PrefetchScalarGridSpec(
            num_scalar_prefetch=1,
            grid=(8,),
            in_specs=[
                pl.BlockSpec((2, B, 8, B), lambda i, t: (i, 0, 0, 0)),
                full((256, B, B)),
                pl.BlockSpec((2 * B, N), lambda i, t: (i, 0)),
                full((N, N)),
                pl.BlockSpec((2, B, B), lambda i, t: (i, 0, 0)),
            ],
            out_specs=pl.BlockSpec((2, B, 8, B), lambda i, t: (i, 0, 0, 0)),
        ),
        compiler_params=params(),
    )(tab, front, arrived, below, panel, first)


def per_device(child_update_blocks, child_pivot_panel, child_map, coupled, parent_front):
    my_row, my_col = lax.axis_index("row"), lax.axis_index("col")
    front = parent_front.reshape(16, B, 8, B)
    out_tab = table(outgoing_kernel, 24, child_map)
    row_op, col_op = panel_gather(child_pivot_panel.reshape(8, 2, B, B))
    outgoing = contributions(out_tab, child_update_blocks.reshape(16, B, 8, B), row_op.reshape(8, 16, B, B), col_op)
    incoming = lax.all_to_all(outgoing, ("row", "col"), split_axis=0, concat_axis=0, tiled=True)
    arrived = incoming.reshape(256, B, B)
    later_map, later_coupled, _ = lax.optimization_barrier((child_map, coupled, outgoing))
    in_tab = table(incoming_kernel, 96, later_map)
    kept = jnp.concatenate([jnp.ones((NB,), F32), later_coupled.astype(F32)])
    keep = jnp.concatenate(
        [
            lax.dynamic_index_in_dim(kept.reshape(16, 8), my_row, 1, keepdims=False),
            lax.dynamic_index_in_dim(kept.reshape(8, 16), my_col, 1, keepdims=False),
        ]
    )
    pivots = pivot_columns(in_tab, arrived, front[:, :, 0, :])
    below, panel, first = factor(pivots.reshape(8, 2, B, B), keep)
    out = schur(in_tab, front, arrived, below, panel, first)
    return out.reshape(1, 16, B, 1, 8, B)


def solution(mesh):
    in_specs = (
        P("row", None, None, "col", None, None),
        P("row", None, None, "col", None),
        P(),
        P(),
        P("row", None, None, "col", None, None),
    )
    out_specs = P("row", None, None, "col", None, None)
    return jax.shard_map(per_device, mesh=mesh, in_specs=in_specs, out_specs=out_specs, check_vma=False)
```

time: 518 us -> 387 us (0.75)
  Pallas kernels: 401 us -> 254 us
  starting transfers between devices: 13.8 us -> 40.2 us
  waiting for transfers between devices: 94.8 us -> 86.2 us
    pallas_call x3, Pallas kernels: 278 us -> 167 us  [the longest x1 156 us: factor(): pl.pallas_call(factor_kernel, out_shape=FACTOR_OUT, in_specs=[ANY, SM], o...]
    all_to_all x1, starting transfers between devices: 13.8 us -> 40.2 us  [per_device(): lax.all_to_all(outgoing, ('row', 'col'), split_axis=0, concat_axis=0, til...]
    pallas_call x1, Pallas kernels: 76.3 us -> 53.1 us  [panel_gather(): pl.pallas_call(panel_gather_kernel, out_shape=(jax.ShapeDtypeStruct((8, 8...]
    all_to_all x1, waiting for transfers between devices: 94.8 us -> 86.2 us  [per_device(): lax.all_to_all(outgoing, ('row', 'col'), split_axis=0, concat_axis=0, til...]
    pallas_call x1, Pallas kernels: 9.27 us -> 3.58 us  [pivot_columns(): pl.pallas_call(pivot_kernel, out_shape=jax.ShapeDtypeStruct((16, B, B), B...]
    pallas_call x1, Pallas kernels: 22.6 us -> 17.2 us  [schur(): pl.pallas_call(schur_kernel, out_shape=jax.ShapeDtypeStruct((16, B, 8, B)...]
  transfers between devices with their start and end apart: 1 -> 1, of which waited for: 1 -> 1; matrix products, arithmetic and copies ran while one was open for 1% -> 1% of each run, Pallas kernels for 0% -> 2%
where the time goes in v2:
time: 387 us; the launch traced here: 386 us
  Pallas kernels  254 us (66%)
  waiting for transfers between devices  86.2 us (22%)
  starting transfers between devices  40.2 us (10%)
  local copies, waits for them, and re-layouts  4.64 us (1%)
    pallas_call x1, Pallas kernels, factor(): pl.pallas_call(factor_kernel, out_shape=FACTOR_OUT, in_specs=[ANY, SM], o...  156 us
    all_to_all x1, waiting for transfers between devices, per_device(): lax.all_to_all(outgoing, ('row', 'col'), split_axis=0, concat_axis=0, til...  86.2 us
    pallas_call x1, Pallas kernels, panel_gather(): pl.pallas_call(panel_gather_kernel, out_shape=(jax.ShapeDtypeStruct((8, 8...  53.1 us
    all_to_all x1, starting transfers between devices, per_device(): lax.all_to_all(outgoing, ('row', 'col'), split_axis=0, concat_axis=0, til...  40.2 us
    pallas_call x1, Pallas kernels, schur(): pl.pallas_call(schur_kernel, out_shape=jax.ShapeDtypeStruct((16, B, 8, B)...  17.2 us
    pallas_call x1, Pallas kernels, contributions(): pl.pallas_call(contribution_kernel, out_shape=jax.ShapeDtypeStruct((128,...  13.6 us
    pallas_call x2, Pallas kernels, table(): pl.pallas_call(kernel, out_shape=jax.ShapeDtypeStruct((size,), jnp.int32)...  10.1 us
  transfers between devices with their start and end apart: 1, of which 1 were waited for; matrix products, arithmetic and copies ran while one was open for 1% of the time, Pallas kernels for 2%

profile of v2, /device:TPU:112, one launch (start us, length us, event | category | flops | bytes accessed | tf_op | source)
XLA Modules:
  0.0 385.9 jit_solution(1342492106317614846)
XLA Ops:
  0.0 1.5 shard_map.55.tab
  1.5 53.1 %shard_map.56 = (bf16[8,8,2,128,128]{4,3,2,1,0:T(8,128)(2,1)}, bf16[8,8,128,128]{3,2,1,0:T(8,128)(2,1)}) custom-call(bf16[8,2,128,128]{3,2,1,0:T(8,128)(2,1)} %bitcast.19), custom_call_target="tpu_custom_call" | custom-call | tf_op jit(solution)/shard_map/pallas_call | solution.py:203
  54.6 13.6 %shard_map.57 = bf16[128,256,128]{2,1,0:T(8,128)(2,1)} custom-call(s32[24]{0:T(128)} %shard_map.55.tab, bf16[16,128,8,128]{3,2,1,0:T(8,128)(2,1)} %bitcast.12, bf16[16,128,8,128]{3,2,1,0:T(8,128)(2,1)} %bitcast.13, bf16[8,16,128,128]{3,2,1,0:T(8,128)(2,1)} %bitcast.16, bf16[8,8,128,128]{3,2,1,0:T(8,128)(2,1)} %get-tuple-element.13.col_ref), custom_call_target="tpu_custom_call" | custom-call | tf_op jit(solution)/shard_map/pallas_call | solution.py:248
  68.2 0.0 copy-start
  68.2 40.2 %all-to-all-start = ((bf16[128,256,128]{2,1,0:T(8,128)(2,1)}), bf16[128,256,128]{2,1,0:T(8,128)(2,1)}, u32[]{:S(2)}, u32[]{:S(2)}) async-start(bf16[128,256,128]{2,1,0:T(8,128)(2,1)} %shard_map.57), calls=%async_computation | async-start | bytes 16777216 | tf_op jit(solution)/shard_map/all_to_all | solution.py:756
  108.4 8.6 %shard_map.58.tab = s32[96]{0:T(128)} custom-call(s32[4,64]{1,0:T(4,128)} %map_ref.2), custom_call_target="tpu_custom_call" | custom-call | flops 20000 | bytes 2048 | tf_op jit(solution)/shard_map/pallas_call | solution.py:84
  117.1 0.0 copy-done
  117.1 0.1 concatenate.6
  117.2 0.1 reshape.34
  117.2 0.1 reshape.33
  117.3 3.1 slice.4
  120.4 0.9 copy.10
  121.4 0.2 dynamic-slice_reduce_fusion.1
  121.5 0.2 dynamic-slice_reduce_fusion
  121.7 0.7 pad_maximum_fusion.keep_ref
  122.4 86.2 %all-to-all-done = bf16[128,256,128]{2,1,0:T(8,128)(2,1)} async-done(((bf16[128,256,128]{2,1,0:T(8,128)(2,1)}), bf16[128,256,128]{2,1,0:T(8,128)(2,1)}, u32[]{:S(2)}, u32[]{:S(2)}) %all-to-all-start) | async-done | bytes 8388640 | tf_op jit(solution)/shard_map/all_to_all | solution.py:756
  208.6 3.6 shard_map.59
  212.1 156.5 %shard_map.60 = (bf16[2048,1024]{1,0:T(8,128)(2,1)}, bf16[1024,1024]{1,0:T(8,128)(2,1)}, f32[16,128,128]{2,1,0:T(8,128)}) custom-call(bf16[8,2,128,128]{3,2,1,0:T(8,128)(2,1)} %bitcast.18, f32[24]{0:T(128)} %pad_maximum_fusion.keep_ref), custom_call_target="tpu_custom_call" | custom-call | tf_op jit(solution)/shard_map/pallas_call | solution.py:695
  368.6 17.2 %shard_map.61 = f32[16,128,8,128]{3,2,1,0:T(8,128)} custom-call(s32[96]{0:T(128)} %shard_map.58.tab, bf16[16,128,8,128]{3,2,1,0:T(8,128)(2,1)} %bitcast.15, bf16[256,128,128]{2,1,0:T(8,128)(2,1)} %bitcast.4.arrived, bf16[2048,1024]{1,0:T(8,128)(2,1)} %get-tuple-element.16.below, bf16[1024,1024]{1,0:T(8,128)(2,1)} %get-tuple-element.17.panel, ...), custom_call_target="tpu_custom_call" | custom-call | tf_op jit(solution)/shard_map/pallas_call | solution.py:731
  (1 shorter events, 0.0 us)
Async XLA Ops:
  68.2 48.9 %copy-start = (s32[120]{0:T(128)S(1)}, s32[120]{0:T(128)}, u32[]{:S(2)}) copy-start(s32[120]{0:T(128)} %param.8) | copy-start | bytes 1444
  68.2 140.3 %all-to-all-start = ((bf16[128,256,128]{2,1,0:T(8,128)(2,1)}), bf16[128,256,128]{2,1,0:T(8,128)(2,1)}, u32[]{:S(2)}, u32[]{:S(2)}) async-start(bf16[128,256,128]{2,1,0:T(8,128)(2,1)} %shard_map.57), calls=%async_computation | async-start | bytes 16777216 | tf_op jit(solution)/shard_map/all_to_all | solution.py:756

commit v3 on v2

--- a/solution.py
+++ b/solution.py
@@ -44,8 +44,10 @@
         owner = map_ref[child, l * 4 + row_rank] % 8
         tab_ref[OUT_ROW + owner * 2 + count[owner]] = l
         count[owner] = count[owner] + 1
+    for c in range(16):
+        tab_ref[OUT_COL + c] = 0
     for m in range(8):
-        tab_ref[OUT_COL + m] = map_ref[child, m * 8 + col_rank] % 16
+        tab_ref[OUT_COL + map_ref[child, m * 8 + col_rank] % 16] = m
 
 
 def incoming_kernel(map_ref, tab_ref, count):
@@ -97,7 +99,7 @@
     )
 
 
-def panel_gather_kernel(p_ref, row_ref, col_ref, local, s_chip, s_sib, s_col, r_row, r_col):
+def contribution_kernel(tab, p_ref, u_hbm, out_hbm, row_ref, col_ref, total, u_ref, block, slots, local, s_chip, s_sib, s_col, r_row, r_col):
     my_row, my_col = lax.axis_index("row"), lax.axis_index("col")
     base, y = my_row // 4 * 4, my_row % 4
     half, cc = my_col // 8 * 8, my_col % 8
@@ -109,6 +111,8 @@
     inner = y0 + 1 - 2 * (y0 % 2)
     last = outer + 1 - 2 * (outer % 2)
     is_source, is_relay = y == y0, y == outer
+    fetch = pltpu.make_async_copy(u_hbm, u_ref, local.at[2])
+    fetch.start()
     barrier = pltpu.get_barrier_semaphore()
 
     def greet(row, col):
@@ -128,9 +132,6 @@
     order = [cc, pair * 2 + 1 - core] + [(pair + d) % 4 * 2 + core for d in (2, 1, 3)]
     order += [(pair + d) % 4 * 2 + 1 - core for d in (2, 1, 3)]
 
-    def own():
-        return pltpu.make_async_copy(p_ref, row_ref.at[cc], local.at[8])
-
     def chip_send(i):
         return remote(p_ref, row_ref.at[cc], s_chip.at[i], r_row.at[cc], my_row, others[i])
 
@@ -138,27 +139,29 @@
         src = p_ref if e == 0 else row_ref.at[order[e]]
         return remote(src, row_ref.at[order[e]], s_sib.at[max(e - 1, 0)], r_row.at[order[e]], my_row, sibling)
 
-    def part(e):
-        return p_ref.at[:, parity] if e == 0 else row_ref.at[order[e], :, parity]
-
-    def keep(e):
-        return pltpu.make_async_copy(part(e), col_ref.at[order[e]], local.at[e])
-
     def col_send(e, t):
-        return remote(part(e), col_ref.at[order[e]], s_col.at[e, t], r_col.at[order[e]], base + (outer, inner)[t], my_col)
+        src = p_ref.at[:, parity] if e == 0 else row_ref.at[order[e], :, parity]
+        return remote(src, col_ref.at[order[e]], s_col.at[e, t], r_col.at[order[e]], base + (outer, inner)[t], my_col)
 
     def pass_on(e):
         j = order[e]
         return remote(col_ref.at[j], col_ref.at[j], s_col.at[e, 0], r_col.at[j], base + last, my_col)
 
-    own().start()
     for i in range(3):
         chip_send(i).start()
     sib_send(0).start()
-    for e in range(9):
-        if e < 8:
-            if e:
-                remote(p_ref, row_ref.at[order[e]], s_sib.at[0], r_row.at[order[e]], my_row, sibling).wait_recv()
+
+    @pl.when(is_source)
+    def _():
+        col_send(0, 0).start()
+        col_send(0, 1).start()
+
+    row_ref[cc] = p_ref[...]
+
+    for e in range(8):
+        j = order[e]
+        if e:
+            remote(p_ref, row_ref.at[j], s_sib.at[0], r_row.at[j], my_row, sibling).wait_recv()
             if 2 <= e < 5:
                 sib_send(e).start()
 
@@ -166,21 +169,64 @@
             def _():
                 col_send(e, 0).start()
                 col_send(e, 1).start()
-                keep(e).start()
-
-        if e:
-
-            @pl.when(is_relay)
-            def _():
-                pass_on(e - 1).wait_recv()
-                pass_on(e - 1).start()
-
-    @pl.when(jnp.logical_not(is_source | is_relay))
-    def _():
-        for e in range(8):
-            pass_on(e).wait_recv()
-
-    own().wait()
+
+        if e % 2 == 0:
+            continue
+
+        @pl.when(is_source)
+        def _():
+            for i in (order[e - 1], j):
+                col_ref[i] = row_ref[i, :, parity]
+
+        @pl.when(jnp.logical_not(is_source))
+        def _():
+            for f in (e - 1, e):
+                pass_on(f).wait_recv()
+
+                @pl.when(is_relay)
+                def _():
+                    pass_on(f).start()
+
+        def product(i, _):
+            left = [row_ref[f, pl.ds(2 * i, 2)].reshape(4 * B, B) for f in (order[e - 1], j)]
+            right = [col_ref[f].reshape(8 * B, B) for f in (order[e - 1], j)]
+            more = lax.dot_general(
+                jnp.concatenate(left, axis=1), jnp.concatenate(right, axis=1), (((1,), (1,)), ((), ())),
+                preferred_element_type=F32,
+            )
+            for m in range(8):
+                part = more[:, m * B : (m + 1) * B].reshape(4, B, B)
+                at = pl.ds(4 * i, 4)
+                total[m, at] = part if e == 1 else total[m, at] + part
+            return 0
+
+        lax.fori_loop(0, 4, product, 0)
+
+    fetch.wait()
+
+    def emit(owner, slot):
+        return pltpu.make_async_copy(slots.at[slot], out_hbm.at[pl.ds(owner * 16, 16)], local.at[slot])
+
+    def lay_out(owner, _):
+        slot = owner % 2
+
+        @pl.when(owner >= 2)
+        def _():
+            emit(owner - 2, slot).wait()
+
+        for s in range(2):
+            l = tab[OUT_ROW + owner * 2 + s]
+            update = jnp.swapaxes(u_ref[l], 0, 1)
+            for m in range(8):
+                block[m] = (update[m].astype(F32) - total[m, l]).astype(BF)
+            for c in range(16):
+                slots[slot, c, s * B : (s + 1) * B, :] = block[tab[OUT_COL + c]]
+        emit(owner, slot).start()
+        return 0
+
+    lax.fori_loop(0, 8, lay_out, 0)
+    for slot in range(2):
+        emit(6 + slot, slot).wait()
     for i in range(3):
         chip_send(i).wait_send()
     for e in (0, 2, 3, 4):
@@ -189,7 +235,6 @@
     @pl.when(is_source)
     def _():
         for e in range(8):
-            keep(e).wait()
             col_send(e, 0).wait_send()
             col_send(e, 1).wait_send()
 
@@ -199,64 +244,29 @@
             pass_on(e).wait_send()
 
 
-def panel_gather(piece):
-    return pl.pallas_call(
-        panel_gather_kernel,
-        out_shape=(
-            jax.ShapeDtypeStruct((8, 8, 2, B, B), BF),
-            jax.ShapeDtypeStruct((8, 8, B, B), BF),
-        ),
-        in_specs=[ANY],
-        out_specs=(ANY, ANY),
-        scratch_shapes=[
-            pltpu.SemaphoreType.DMA((9,)),
-            pltpu.SemaphoreType.DMA((3,)),
-            pltpu.SemaphoreType.DMA((4,)),
-            pltpu.SemaphoreType.DMA((8, 2)),
-            pltpu.SemaphoreType.DMA((8,)),
-            pltpu.SemaphoreType.DMA((8,)),
-        ],
-        compiler_params=params(collective_id=1, has_side_effects=True),
-    )(piece)
-
-
-def contribution_kernel(tab, u0, u1, row_ref, col_ref, out_ref, right):
-    owner = pl.program_id(0)
-
-    @pl.when(owner == 0)
-    def _():
-        for k in range(8):
-            for m in range(8):
-                right[m * B : (m + 1) * B, k * B : (k + 1) * B] = col_ref[k, m]
-
-    left = []
-    for s in range(2):
-        l = tab[OUT_ROW + owner * 2 + s]
-        left.append(jnp.concatenate([row_ref[k, l] for k in range(8)], axis=1))
-    left = jnp.concatenate(left, axis=0)
-    product = lax.dot_general(left, right[...], (((1,), (1,)), ((), ())), preferred_element_type=F32)
-    for s, u in enumerate((u0, u1)):
-        update = jnp.swapaxes(u[0], 0, 1)
-        for m in range(8):
-            value = update[m].astype(F32) - product[s * B : (s + 1) * B, m * B : (m + 1) * B]
-            out_ref[tab[OUT_COL + m], s * B : (s + 1) * B, :] = value.astype(BF)
-
-
-def contributions(tab, update, row_op, col_op):
-    full = lambda shape: pl.BlockSpec(shape, lambda i, t: (0,) * len(shape))
-    u_spec = lambda s: pl.BlockSpec((1, B, 8, B), lambda i, t: (t[OUT_ROW + 2 * i + s], 0, 0, 0))
+def contributions(tab, piece, update):
+    dma = pltpu.SemaphoreType.DMA
     return pl.pallas_call(
         contribution_kernel,
         out_shape=jax.ShapeDtypeStruct((128, 2 * B, B), BF),
-        grid_spec=pltpu.PrefetchScalarGridSpec(
-            num_scalar_prefetch=1,
-            grid=(8,),
-            in_specs=[u_spec(0), u_spec(1), full((8, 16, B, B)), full((8, 8, B, B))],
-            out_specs=pl.BlockSpec((16, 2 * B, B), lambda i, t: (i, 0, 0)),
-            scratch_shapes=[pltpu.VMEM((N, N), BF)],
-        ),
-        compiler_params=params(),
-    )(tab, update, update, row_op, col_op)
+        in_specs=[SM, VM, ANY],
+        out_specs=ANY,
+        scratch_shapes=[
+            pltpu.VMEM((8, 8, 2, B, B), BF),
+            pltpu.VMEM((8, 8, B, B), BF),
+            pltpu.VMEM((8, 16, B, B), F32),
+            pltpu.VMEM((16, B, 8, B), BF),
+            pltpu.VMEM((8, B, B), BF),
+            pltpu.VMEM((2, 16, 2 * B, B), BF),
+            dma((3,)),
+            dma((3,)),
+            dma((4,)),
+            dma((8, 2)),
+            dma((8,)),
+            dma((8,)),
+        ],
+        compiler_params=params(collective_id=1, has_side_effects=True),
+    )(tab, piece, update)
 
 
 def pivot_kernel(tab, arrived, front, out_ref, block, sem):
@@ -406,6 +416,8 @@
             for s in self.sq_sends():
                 s.start()
             whole.wait()
+            for s in self.z_sends():
+                s.start()
 
         for i in range(4):
             j = 2 * i + self.core
@@ -428,17 +440,6 @@
         def _():
             self.cols_send(0).start()
 
-    def keep_cols(self):
-        j = self.col % 8
-        return pltpu.make_async_copy(self.portion.at[j, :, self.zh], self.cols.at[j], self.local.at[0])
-
-    def first(self):
-        @pl.when(self.owner)
-        def _():
-            for s in self.z_sends():
-                s.start()
-            self.cols_start()
-
     def second(self):
         for zp in range(2):
             j = zp * 4 + self.xh * 2 + self.core
@@ -449,14 +450,11 @@
 
         for s in self.x_sends():
             s.start()
-
-        @pl.when(jnp.logical_not(self.owner))
-        def _():
-            self.cols_start()
+        self.cols_start()
 
         @pl.when(self.same)
         def _():
-            self.keep_cols().start()
+            self.cols[self.col % 8] = self.portion[self.col % 8, :, self.zh]
 
     def third(self):
         for zp in range(2):
@@ -472,10 +470,6 @@
         for d in range(1, 8):
             j = (self.col + d) % 8
             self.arrived(self.cols.at[j], self.r_cols.at[j])
-
-        @pl.when(self.same)
-        def _():
-            self.keep_cols().wait()
 
         @pl.when(jnp.logical_not(self.same))
         def _():
@@ -652,15 +646,11 @@
     gather = Gather(piece, sq, portion, cols, sems)
     gather.enter()
     gather.square()
-    gather.first()
+    gather.second()
     factor_start(sq, lower_ref, work)
 
     def step(kb, _):
-        @pl.when(kb == 3)
-        def _():
-            gather.second()
-
-        @pl.when(kb == 7)
+        @pl.when(kb == 6)
         def _():
             gather.third()
 
@@ -750,9 +740,8 @@
 def per_device(child_update_blocks, child_pivot_panel, child_map, coupled, parent_front):
     my_row, my_col = lax.axis_index("row"), lax.axis_index("col")
     front = parent_front.reshape(16, B, 8, B)
-    out_tab = table(outgoing_kernel, 24, child_map)
-    row_op, col_op = panel_gather(child_pivot_panel.reshape(8, 2, B, B))
-    outgoing = contributions(out_tab, child_update_blocks.reshape(16, B, 8, B), row_op.reshape(8, 16, B, B), col_op)
+    out_tab = table(outgoing_kernel, 32, child_map)
+    outgoing = contributions(out_tab, child_pivot_panel.reshape(8, 2, B, B), child_update_blocks.reshape(16, B, 8, B))
     incoming = lax.all_to_all(outgoing, ("row", "col"), split_axis=0, concat_axis=0, tiled=True)
     arrived = incoming.reshape(256, B, B)
     later_map, later_coupled, _ = lax.optimization_barrier((child_map, coupled, outgoing))

time: 387 us -> 340 us (0.88)
  starting transfers between devices: 40.2 us -> 7.8 us
  Pallas kernels: 254 us -> 238 us
    pallas_call x1 -> x0, Pallas kernels: 53.1 us -> none  [panel_gather(): pl.pallas_call(panel_gather_kernel, out_shape=(jax.ShapeDtypeStruct((8, 8...]
    pallas_call x1, Pallas kernels: 13.6 us -> 61 us  [contributions(): pl.pallas_call(contribution_kernel, out_shape=jax.ShapeDtypeStruct((128,...]
    all_to_all x1, starting transfers between devices: 40.2 us -> 7.8 us  [per_device(): lax.all_to_all(outgoing, ('row', 'col'), split_axis=0, concat_axis=0, til...]
    pallas_call x1, Pallas kernels: 156 us -> 146 us  [factor(): pl.pallas_call(factor_kernel, out_shape=FACTOR_OUT, in_specs=[ANY, SM], o...]
  transfers between devices with their start and end apart: 1 -> 1, of which waited for: 1 -> 1; matrix products, arithmetic and copies ran while one was open for 1% -> 2% of each run, Pallas kernels for 2% -> 3%
where the time goes in v3:
time: 340 us; the launch traced here: 337 us
  Pallas kernels  238 us (70%)
  waiting for transfers between devices  86.2 us (25%)
  starting transfers between devices  7.8 us (2%)
  local copies, waits for them, and re-layouts  4.59 us (1%)
    pallas_call x1, Pallas kernels, factor(): pl.pallas_call(factor_kernel, out_shape=FACTOR_OUT, in_specs=[ANY, SM], o...  146 us
    all_to_all x1, waiting for transfers between devices, per_device(): lax.all_to_all(outgoing, ('row', 'col'), split_axis=0, concat_axis=0, til...  86.2 us
    pallas_call x1, Pallas kernels, contributions(): pl.pallas_call(contribution_kernel, out_shape=jax.ShapeDtypeStruct((128,...  61 us
    pallas_call x1, Pallas kernels, schur(): pl.pallas_call(schur_kernel, out_shape=jax.ShapeDtypeStruct((16, B, 8, B)...  17.2 us
    pallas_call x2, Pallas kernels, table(): pl.pallas_call(kernel, out_shape=jax.ShapeDtypeStruct((size,), jnp.int32)...  10.1 us
    all_to_all x1, starting transfers between devices, per_device(): lax.all_to_all(outgoing, ('row', 'col'), split_axis=0, concat_axis=0, til...  7.8 us
  transfers between devices with their start and end apart: 1, of which 1 were waited for; matrix products, arithmetic and copies ran while one was open for 2% of the time, Pallas kernels for 3%

profile of v3, /device:TPU:112, one launch (start us, length us, event | category | flops | bytes accessed | tf_op | source)
XLA Modules:
  0.0 337.0 jit_solution(1506572997500962969)
XLA Ops:
  0.0 1.5 shard_map.55.tab
  1.5 61.0 %shard_map.56 = bf16[128,256,128]{2,1,0:T(8,128)(2,1)} custom-call(s32[32]{0:T(128)} %shard_map.55.tab, bf16[8,2,128,128]{3,2,1,0:T(8,128)(2,1)} %bitcast.16, bf16[16,128,8,128]{3,2,1,0:T(8,128)(2,1)} %bitcast.13), custom_call_target="tpu_custom_call" | custom-call | tf_op jit(solution)/shard_map/pallas_call | solution.py:249
  62.5 0.0 copy-start
  62.5 7.8 %all-to-all-start = ((bf16[128,256,128]{2,1,0:T(8,128)(2,1)}), bf16[128,256,128]{2,1,0:T(8,128)(2,1)}, u32[]{:S(2)}, u32[]{:S(2)}) async-start(bf16[128,256,128]{2,1,0:T(8,128)(2,1)} %shard_map.56), calls=%async_computation | async-start | bytes 16777216 | tf_op jit(solution)/shard_map/all_to_all | solution.py:745
  70.3 8.6 %shard_map.57.tab = s32[96]{0:T(128)} custom-call(s32[4,64]{1,0:T(4,128)} %map_ref.2), custom_call_target="tpu_custom_call" | custom-call | flops 20000 | bytes 2048 | tf_op jit(solution)/shard_map/pallas_call | solution.py:86
  79.0 0.0 copy-done
  79.0 0.1 concatenate.6
  79.1 0.1 reshape.30
  79.1 0.1 reshape.29
  79.2 3.1 slice.4
  82.3 0.9 copy.10
  83.2 0.2 dynamic-slice_reduce_fusion.1
  83.4 0.2 dynamic-slice_reduce_fusion
  83.6 0.7 pad_maximum_fusion.keep_ref
  84.2 86.2 %all-to-all-done = bf16[128,256,128]{2,1,0:T(8,128)(2,1)} async-done(((bf16[128,256,128]{2,1,0:T(8,128)(2,1)}), bf16[128,256,128]{2,1,0:T(8,128)(2,1)}, u32[]{:S(2)}, u32[]{:S(2)}) %all-to-all-start) | async-done | bytes 8388640 | tf_op jit(solution)/shard_map/all_to_all | solution.py:745
  170.4 3.6 %shard_map.58 = bf16[16,128,128]{2,1,0:T(8,128)(2,1)} custom-call(s32[96]{0:T(128)} %shard_map.57.tab, bf16[256,128,128]{2,1,0:T(8,128)(2,1)} %bitcast.3.arrived, bf16[16,128,128]{2,1,0:T(8,128)(2,1)} %bitcast.14), custom_call_target="tpu_custom_call" | custom-call | tf_op jit(solution)/shard_map/pallas_call | solution.py:293
  174.0 145.8 %shard_map.59 = (bf16[2048,1024]{1,0:T(8,128)(2,1)}, bf16[1024,1024]{1,0:T(8,128)(2,1)}, f32[16,128,128]{2,1,0:T(8,128)}) custom-call(bf16[8,2,128,128]{3,2,1,0:T(8,128)(2,1)} %bitcast.15, f32[24]{0:T(128)} %pad_maximum_fusion.keep_ref), custom_call_target="tpu_custom_call" | custom-call | tf_op jit(solution)/shard_map/pallas_call | solution.py:685
  319.8 17.2 %shard_map.60 = f32[16,128,8,128]{3,2,1,0:T(8,128)} custom-call(s32[96]{0:T(128)} %shard_map.57.tab, bf16[16,128,8,128]{3,2,1,0:T(8,128)(2,1)} %bitcast.12, bf16[256,128,128]{2,1,0:T(8,128)(2,1)} %bitcast.3.arrived, bf16[2048,1024]{1,0:T(8,128)(2,1)} %get-tuple-element.12.below, bf16[1024,1024]{1,0:T(8,128)(2,1)} %get-tuple-element.13.panel, ...), custom_call_target="tpu_custom_call" | custom-call | tf_op jit(solution)/shard_map/pallas_call | solution.py:721
  (1 shorter events, 0.0 us)
Async XLA Ops:
  62.5 16.4 %copy-start = (s32[120]{0:T(128)S(1)}, s32[120]{0:T(128)}, u32[]{:S(2)}) copy-start(s32[120]{0:T(128)} %param.8) | copy-start | bytes 1444
  62.5 107.9 %all-to-all-start = ((bf16[128,256,128]{2,1,0:T(8,128)(2,1)}), bf16[128,256,128]{2,1,0:T(8,128)(2,1)}, u32[]{:S(2)}, u32[]{:S(2)}) async-start(bf16[128,256,128]{2,1,0:T(8,128)(2,1)} %shard_map.56), calls=%async_computation | async-start | bytes 16777216 | tf_op jit(solution)/shard_map/all_to_all | solution.py:745

commit v4 on v3

v4 whole, which is shorter than its diff:
```python
import functools

import jax
import jax.numpy as jnp
from jax import lax
from jax.experimental import pallas as pl
from jax.experimental.pallas import tpu as pltpu
from jax.sharding import PartitionSpec as P

B = 128
NB = 8
N = NB * B
F32 = jnp.float32
BF = jnp.bfloat16
MESH = pl.DeviceIdType.MESH
ANY = pl.BlockSpec(memory_space=pl.ANY)
VM = pl.BlockSpec(memory_space=pltpu.VMEM)
SM = pl.BlockSpec(memory_space=pltpu.SMEM)
MIB = 1024 * 1024


def params(mib, **kw):
    return pltpu.CompilerParams(vmem_limit_bytes=mib * MIB, **kw)


OUT_ROW, OUT_COL = 0, 16
AT_RSRC, AT_RCH, AT_CSRC, AT_CCH = 0, 32, 64, 80


def clear(count):
    def one(i, _):
        count[i] = 0
        return 0

    lax.fori_loop(0, 16, one, 0)


def outgoing_kernel(map_ref, tab_ref, count):
    my_row, my_col = lax.axis_index("row"), lax.axis_index("col")
    row_rank, col_rank = my_row % 4, my_col % 8
    child = 2 * (my_row // 4) + my_col // 8
    clear(count)
    for l in range(16):
        owner = map_ref[child, l * 4 + row_rank] % 8
        tab_ref[OUT_ROW + owner * 2 + count[owner]] = l
        count[owner] = count[owner] + 1
    for c in range(16):
        tab_ref[OUT_COL + c] = 0
    for m in range(8):
        tab_ref[OUT_COL + map_ref[child, m * 8 + col_rank] % 16] = m


def incoming_kernel(map_ref, tab_ref, count):
    my_row, my_col = lax.axis_index("row"), lax.axis_index("col")
    clear(count)

    def arrive(q, _):
        h, g = q // 2, q % 2

        def one(b, _):
            target = map_ref[q, b]

            @pl.when(target % 8 == my_row)
            def _():
                slot = q * 4 + b % 4
                at = h * 16 + target // 8
                tab_ref[AT_RSRC + at] = (h * 4 + b % 4) * 32 + count[slot]
                tab_ref[AT_RCH + at] = g
                count[slot] = count[slot] + 1

            @pl.when(target % 16 == my_col)
            def _():
                at = h * 8 + target // 16
                tab_ref[AT_CSRC + at] = (g * 8 + b % 8) * 2
                tab_ref[AT_CCH + at] = g

            return 0

        lax.fori_loop(0, 64, one, 0)
        return 0

    lax.fori_loop(0, 4, arrive, 0)


def table(kernel, size, child_map):
    return pl.pallas_call(
        kernel,
        out_shape=jax.ShapeDtypeStruct((size,), jnp.int32),
        in_specs=[SM],
        out_specs=SM,
        scratch_shapes=[pltpu.SMEM((16,), jnp.int32)],
        cost_estimate=pl.CostEstimate(flops=20000, bytes_accessed=2048, transcendentals=0),
    )(child_map)


def remote(src, dst, s, r, row, col):
    return pltpu.make_async_remote_copy(
        src_ref=src, dst_ref=dst, send_sem=s, recv_sem=r, device_id=(row, col), device_id_type=MESH
    )


def contribution_kernel(tab, p_ref, u_hbm, out_hbm, row_ref, col_ref, total, u_ref, block, slots, local, s_chip, s_sib, s_col, r_row, r_col):
    my_row, my_col = lax.axis_index("row"), lax.axis_index("col")
    base, y = my_row // 4 * 4, my_row % 4
    half, cc = my_col // 8 * 8, my_col % 8
    core, pair, parity = cc % 2, cc // 2, cc // 4
    sibling = half + pair * 2 + 1 - core
    y0 = cc % 4
    step = jnp.where(y0 % 2 == 0, 3, 1)
    outer = (y0 + step) % 4
    inner = y0 + 1 - 2 * (y0 % 2)
    last = outer + 1 - 2 * (outer % 2)
    is_source, is_relay = y == y0, y == outer
    fetch = pltpu.make_async_copy(u_hbm, u_ref, local.at[2])
    fetch.start()
    barrier = pltpu.get_barrier_semaphore()

    def greet(row, col):
        pl.semaphore_signal(barrier, inc=1, device_id=(row, col), device_id_type=MESH)

    others = [half + (pair + d) % 4 * 2 + core for d in (2, 1, 3)]
    for col in others:
        greet(my_row, col)
    greet(my_row, sibling)

    @pl.when(jnp.logical_not(is_source))
    def _():
        greet(base + jnp.where(y == last, outer, y0), my_col)

    pl.semaphore_wait(barrier, 4 + jnp.where(is_source, 2, jnp.where(is_relay, 1, 0)))

    order = [cc, pair * 2 + 1 - core] + [(pair + d) % 4 * 2 + core for d in (2, 1, 3)]
    order += [(pair + d) % 4 * 2 + 1 - core for d in (2, 1, 3)]


    def chip_send(i, late):
        col = others[i]
        p = (col % 8 // 4 + late) % 2
        return remote(p_ref.at[:, p], row_ref.at[cc, :, p], s_chip.at[i, late], r_row.at[cc, late], my_row, col)

    def sib_send(e, late):
        p, j = (parity + late) % 2, order[e]
        src = p_ref.at[:, p] if e == 0 else row_ref.at[j, :, p]
        return remote(src, row_ref.at[j, :, p], s_sib.at[max(e - 1, 0), late], r_row.at[j, late], my_row, sibling)

    def row_wait(e, late):
        p, j = (parity + late) % 2, order[e]
        remote(p_ref.at[:, p], row_ref.at[j, :, p], s_sib.at[0, 0], r_row.at[j, late], my_row, sibling).wait_recv()

    def col_send(e, t):
        src = p_ref.at[:, parity] if e == 0 else row_ref.at[order[e], :, parity]
        return remote(src, col_ref.at[order[e]], s_col.at[e, t], r_col.at[order[e]], base + (outer, inner)[t], my_col)

    def pass_on(e):
        j = order[e]
        return remote(col_ref.at[j], col_ref.at[j], s_col.at[e, 0], r_col.at[j], base + last, my_col)

    def relay(*events):
        @pl.when(is_relay)
        def _():
            for e in events:
                pass_on(e).wait_recv()
                pass_on(e).start()

    def product(t):
        pairs = (order[2 * t], order[2 * t + 1])

        @pl.when(is_source)
        def _():
            for i in pairs:
                col_ref[i] = row_ref[i, :, parity]

        @pl.when(jnp.logical_not(is_source | is_relay))
        def _():
            pass_on(2 * t).wait_recv()
            pass_on(2 * t + 1).wait_recv()

        def some(i, _):
            left = [row_ref[f, pl.ds(2 * i, 2)].reshape(4 * B, B) for f in pairs]
            right = [col_ref[f].reshape(8 * B, B) for f in pairs]
            more = lax.dot_general(
                jnp.concatenate(left, axis=1), jnp.concatenate(right, axis=1), (((1,), (1,)), ((), ())),
                preferred_element_type=F32,
            )
            at = pl.ds(4 * i, 4)
            if t == 0:
                update = [jnp.swapaxes(u_ref[4 * i + r], 0, 1) for r in range(4)]
            for m in range(8):
                part = more[:, m * B : (m + 1) * B].reshape(4, B, B)
                if t == 0:
                    for r in range(4):
                        total[m, 4 * i + r] = update[r][m].astype(F32) - part[r]
                elif t < 3:
                    total[m, at] = total[m, at] - part
                else:
                    block[m, at] = (total[m, at] - part).astype(BF)
            return 0

        lax.fori_loop(0, 4, some, 0)

    for late in range(2):
        for i in range(3):
            chip_send(i, late).start()
        sib_send(0, late).start()
        if late == 0:

            @pl.when(is_source)
            def _():
                col_send(0, 0).start()
                col_send(0, 1).start()

    row_ref[cc] = p_ref[...]
    for e in range(1, 8):
        row_wait(e, 0)
        if 2 <= e < 5:
            sib_send(e, 0).start()

        @pl.when(is_source)
        def _():
            col_send(e, 0).start()
            col_send(e, 1).start()

        if e == 1:
            row_wait(1, 1)
            relay(0, 1)
            fetch.wait()
            product(0)
    relay(2, 3, 4)
    for e in (2, 3, 4):
        row_wait(e, 1)
        sib_send(e, 1).start()
    relay(5)
    product(1)
    relay(6, 7)
    for e in (5, 6, 7):
        row_wait(e, 1)
    product(2)
    product(3)

    def emit(owner, slot):
        return pltpu.make_async_copy(slots.at[slot], out_hbm.at[pl.ds(owner * 16, 16)], local.at[slot])

    def lay_out(owner, _):
        slot = owner % 2

        @pl.when(owner >= 2)
        def _():
            emit(owner - 2, slot).wait()

        for s in range(2):
            l = tab[OUT_ROW + owner * 2 + s]
            for c in range(16):
                slots[slot, c, s * B : (s + 1) * B, :] = block[tab[OUT_COL + c], l]
        emit(owner, slot).start()
        return 0

    lax.fori_loop(0, 8, lay_out, 0)
    for slot in range(2):
        emit(6 + slot, slot).wait()
    for late in range(2):
        for i in range(3):
            chip_send(i, late).wait_send()
        for e in (0, 2, 3, 4):
            sib_send(e, late).wait_send()

    @pl.when(is_source)
    def _():
        for e in range(8):
            col_send(e, 0).wait_send()
            col_send(e, 1).wait_send()

    @pl.when(is_relay)
    def _():
        for e in range(8):
            pass_on(e).wait_send()


def contributions(tab, piece, update):
    dma = pltpu.SemaphoreType.DMA
    return pl.pallas_call(
        contribution_kernel,
        out_shape=jax.ShapeDtypeStruct((128, 2 * B, B), BF),
        in_specs=[SM, VM, ANY],
        out_specs=ANY,
        scratch_shapes=[
            pltpu.VMEM((8, 8, 2, B, B), BF),
            pltpu.VMEM((8, 8, B, B), BF),
            pltpu.VMEM((8, 16, B, B), F32),
            pltpu.VMEM((16, B, 8, B), BF),
            pltpu.VMEM((8, 16, B, B), BF),
            pltpu.VMEM((2, 16, 2 * B, B), BF),
            dma((3,)),
            dma((3, 2)),
            dma((4, 2)),
            dma((8, 2)),
            dma((8, 2)),
            dma((8,)),
        ],
        compiler_params=params(56, collective_id=1, has_side_effects=True),
    )(tab, piece, update)


def pivot_kernel(tab, arrived, front, out_ref, block, sem):
    def fits(l, h):
        return tab[AT_RCH + h * 16 + l] == tab[AT_CCH + h * 8]

    def fetch(l, h):
        at = jnp.where(fits(l, h), tab[AT_RSRC + h * 16 + l] + tab[AT_CSRC + h * 8], 0)
        return pltpu.make_async_copy(arrived.at[at], block.at[h, l], sem.at[h, l])

    for l in range(16):
        for h in range(2):
            fetch(l, h).start()
    for l in range(16):
        value = front[l].astype(F32)
        for h in range(2):
            valid = fits(l, h)
            fetch(l, h).wait()
            value = value + jnp.where(valid, block[h, l].astype(F32), 0.0)
        out_ref[l] = value.astype(BF)


def pivot_columns(tab, arrived, front):
    return pl.pallas_call(
        pivot_kernel,
        out_shape=jax.ShapeDtypeStruct((16, B, B), BF),
        in_specs=[SM, ANY, VM],
        out_specs=VM,
        scratch_shapes=[pltpu.VMEM((2, 16, B, B), BF), pltpu.SemaphoreType.DMA((2, 16))],
        compiler_params=params(8),
    )(tab, arrived, front)


class Gather:
    SEMS = (3, 3, 3, 3, 3, 3, 4, 4, 1, 2, 1, 8, 2, 2, 4, 4, 4, 4, 4, 4, 1, 2, 4, 4)

    def __init__(self, piece, sq, portion, cols, sems):
        self.piece, self.sq, self.portion, self.cols = piece, sq, portion, cols
        (self.s_zq, self.s_zp, self.s_y2, self.s_x2, self.s_x3, self.s_y3, self.s_bx, self.s_by) = sems[:8]
        (self.s_px, self.s_ps, self.s_f, self.s_c) = sems[8:12]
        (self.r_zq, self.r_zp, self.r_y2, self.r_x2, self.r_x3, self.r_y3, self.r_bx, self.r_by) = sems[12:20]
        (self.r_px, self.r_ps, self.r_f, self.r_c) = sems[20:]
        row, col = lax.axis_index("row"), lax.axis_index("col")
        self.xl, self.y, self.z, self.xh, self.k = row // 4, row % 4, col // 4, col // 2 % 2, col % 2
        self.x = self.xh * 2 + self.xl
        self.zh, self.zl = self.z // 2, self.z % 2
        self.owner = self.z < 2
        y0 = self.xh * 2 + self.k
        outer = (y0 + jnp.where(y0 % 2 == 0, 3, 1)) % 4
        self.y0, self.outer, self.inner = y0, outer, y0 + 1 - 2 * (y0 % 2)
        self.last_y = outer + 1 - 2 * (outer % 2)
        self.is_source, self.is_relay = self.y == y0, self.y == outer
        self.straight = self.xl == self.zl
        self.groups = [(self.xh, self.k), (self.xh, 1 - self.k), (1 - self.xh, self.k), (1 - self.xh, 1 - self.k)]

    def at(self, xl=None, y=None, z=None, xh=None, k=None):
        pick = lambda new, old: old if new is None else new
        return pick(xl, self.xl) * 4 + pick(y, self.y), pick(z, self.z) * 4 + pick(xh, self.xh) * 2 + pick(k, self.k)

    def xs(self):
        return [((self.x + d) % 4 % 2, (self.x + d) % 4 // 2) for d in (1, 3, 2)]

    def ys(self):
        return [(self.y + d) % 4 for d in (1, 3, 2)]

    def zs(self):
        return [(self.z + d) % 4 for d in (1, 3, 2)]

    def send(self, src, dst, s, r, to):
        return remote(src, dst, s, r, to[0], to[1])

    def arrived(self, ref, sem):
        to = self.at(k=1 - self.k)
        remote(ref, ref, self.s_zq.at[0], sem, to[0], to[1]).wait_recv()

    def enter(self):
        barrier = pltpu.get_barrier_semaphore()

        def greet(to):
            pl.semaphore_signal(barrier, inc=1, device_id=to, device_id_type=MESH)

        for z in self.zs():
            greet(self.at(z=z))
        for y in self.ys():
            greet(self.at(y=y))
        for xl, xh in self.xs():
            greet(self.at(xl=xl, xh=xh))
        greet(self.at(k=1 - self.k))

        @pl.when(self.is_source & jnp.logical_not(self.straight))
        def _():
            for xh, k in self.groups:
                greet(self.at(xl=self.zl, xh=xh, k=k))

        pl.semaphore_wait(barrier, 10 + jnp.where(self.straight, 1, 0))


    def mine(self, zp):
        return self.sq.at[zp, self.xh, self.k, self.xl, self.y]

    def zq_sends(self):
        src = self.piece.at[0, 0]
        return [
            self.send(src, self.mine(self.z), self.s_zq.at[i], self.r_zq.at[self.z], self.at(z=z))
            for i, z in enumerate(self.zs())
        ]

    def zp_sends(self):
        dst = self.portion.at[self.z, self.xh, self.k]
        return [
            self.send(self.piece, dst, self.s_zp.at[i], self.r_zp.at[self.z], self.at(z=z)) for i, z in enumerate(self.zs())
        ]

    def y2_sends(self):
        c = self.mine(0)
        return [self.send(c, c, self.s_y2.at[i], self.r_y2.at[self.y], self.at(y=y)) for i, y in enumerate(self.ys())]

    def x2_sends(self):
        c = self.mine(1)
        return [
            self.send(c, c, self.s_x2.at[i], self.r_x2.at[self.x], self.at(xl=xl, xh=xh))
            for i, (xl, xh) in enumerate(self.xs())
        ]

    def along_y(self, xl, xh, k):
        return self.sq.at[0, xh, k, xl]

    def along_x(self, y, k):
        return self.sq.at[1, :, k, :, y]

    def x3_sends(self):
        c = self.along_y(self.xl, self.xh, self.k)
        return [
            self.send(c, c, self.s_x3.at[i], self.r_x3.at[self.x], self.at(xl=xl, xh=xh))
            for i, (xl, xh) in enumerate(self.xs())
        ]

    def y3_sends(self):
        c = self.along_x(self.y, self.k)
        return [self.send(c, c, self.s_y3.at[i], self.r_y3.at[self.y], self.at(y=y)) for i, y in enumerate(self.ys())]

    def bx_send(self, xl, xh):
        c, x = self.along_y(xl, xh, self.k), xh * 2 + xl
        return self.send(c, c, self.s_bx.at[x], self.r_bx.at[x], self.at(k=1 - self.k))

    def by_send(self, y):
        c = self.along_x(y, self.k)
        return self.send(c, c, self.s_by.at[y], self.r_by.at[y], self.at(k=1 - self.k))

    def square(self):
        @pl.when(self.owner)
        def _():
            for s in self.zq_sends() + self.zp_sends():
                s.start()
            self.sq[self.z, self.xh, self.k, self.xl, self.y] = self.piece[0, 0]
            self.portion[self.z, self.xh, self.k] = self.piece[...]

        for zp, sends in ((0, self.y2_sends), (1, self.x2_sends)):

            @pl.when(self.z != zp)
            def _():
                self.arrived(self.mine(zp), self.r_zq.at[zp])

            for s in sends():
                s.start()
        for y in self.ys():
            self.arrived(self.sq.at[0, self.xh, self.k, self.xl, y], self.r_y2.at[y])
        for s in self.x3_sends():
            s.start()
        self.bx_send(self.xl, self.xh).start()
        for xl, xh in self.xs():
            self.arrived(self.sq.at[1, xh, self.k, xl, self.y], self.r_x2.at[xh * 2 + xl])
        for s in self.y3_sends():
            s.start()
        self.by_send(self.y).start()
        for (xl, xh), y in zip(self.xs(), self.ys()):
            self.arrived(self.along_y(xl, xh, self.k), self.r_x3.at[xh * 2 + xl])
            self.bx_send(xl, xh).start()
            self.arrived(self.along_x(y, self.k), self.r_y3.at[y])
            self.by_send(y).start()
        for i in range(4):
            self.arrived(self.along_y(i % 2, i // 2, 1 - self.k), self.r_bx.at[i])
            self.arrived(self.along_x(i, 1 - self.k), self.r_by.at[i])


    def two(self, xh, k):
        return self.portion.at[:, xh, k]

    def px_send(self):
        c = self.two(self.xh, self.k)
        return self.send(c, c, self.s_px.at[0], self.r_px.at[0], self.at(xh=1 - self.xh))

    def ps_send(self, i):
        c = self.two(self.xh if i == 0 else 1 - self.xh, self.k)
        return self.send(c, c, self.s_ps.at[i], self.r_ps.at[i], self.at(k=1 - self.k))

    def f_send(self):
        src = self.portion.at[:, self.xh, self.k, :, self.zh]
        dst = self.cols.at[:, self.xh, self.k]
        to = self.at(xl=1 - self.xl, xh=self.y // 2, k=self.y % 2)
        return self.send(src, dst, self.s_f.at[0], self.r_f.at[self.xh * 2 + self.k], to)

    def group(self, i):
        xh, k = self.groups[i]
        return self.cols.at[:, xh, k]

    def c_send(self, i, t):
        c = self.group(i)
        return self.send(c, c, self.s_c.at[2 * i + t], self.r_c.at[i], self.at(y=(self.outer, self.inner)[t]))

    def pass_send(self, i):
        c = self.group(i)
        return self.send(c, c, self.s_c.at[2 * i], self.r_c.at[i], self.at(y=self.last_y))

    def spread(self, i):
        @pl.when(self.is_source & self.straight)
        def _():
            xh, k = self.groups[i]
            for zp in range(2):
                self.cols[zp, xh, k] = self.portion[zp, xh, k, :, self.zh]
            self.c_send(i, 0).start()
            self.c_send(i, 1).start()

    def turn(self, i):
        @pl.when(self.is_source & jnp.logical_not(self.straight))
        def _():
            xh, k = self.groups[i]
            self.arrived(self.group(i), self.r_f.at[xh * 2 + k])
            self.c_send(i, 0).start()
            self.c_send(i, 1).start()

    def relay(self, i):
        @pl.when(self.is_relay)
        def _():
            self.arrived(self.group(i), self.r_c.at[i])
            self.pass_send(i).start()

    def begin(self):
        for zp in range(2):

            @pl.when(self.z != zp)
            def _():
                self.arrived(self.portion.at[zp, self.xh, self.k], self.r_zp.at[zp])

        @pl.when(self.straight)
        def _():
            self.f_send().start()

        self.ps_send(0).start()
        self.spread(0)

    def during(self, kb):
        straight, turned = self.straight, jnp.logical_not(self.straight)

        @pl.when(kb == 1)
        def _():
            self.arrived(self.two(self.xh, 1 - self.k), self.r_ps.at[0])
            self.spread(1)

        @pl.when(kb == 2)
        def _():
            self.px_send().start()

        for step, i in ((3, 0), (3, 1), (3, 2), (3, 3)):

            @pl.when(kb == step)
            def _():
                self.turn(i)

        for step, i in ((4, 0), (5, 1), (6, 2), (7, 3)):

            @pl.when((kb == step) & turned)
            def _():
                self.relay(i)

        for step, i in ((2, 0), (3, 1), (7, 2)):

            @pl.when((kb == step) & straight)
            def _():
                self.relay(i)

        @pl.when(kb == 6)
        def _():
            self.arrived(self.two(1 - self.xh, self.k), self.r_px.at[0])
            self.ps_send(1).start()
            self.spread(2)

        @pl.when(kb == 7)
        def _():
            self.arrived(self.two(1 - self.xh, 1 - self.k), self.r_ps.at[1])
            self.spread(3)

    def after(self):
        @pl.when(self.straight)
        def _():
            self.relay(3)

    def end(self):
        @pl.when(jnp.logical_not(self.is_source | self.is_relay))
        def _():
            for i in range(4):
                self.arrived(self.group(i), self.r_c.at[i])

    def finish(self):
        @pl.when(self.owner)
        def _():
            for s in self.zq_sends() + self.zp_sends():
                s.wait_send()

        for s in self.y2_sends() + self.x2_sends() + self.x3_sends() + self.y3_sends():
            s.wait_send()
        for i in range(4):
            self.bx_send(i % 2, i // 2).wait_send()
            self.by_send(i).wait_send()
        self.px_send().wait_send()
        self.ps_send(0).wait_send()
        self.ps_send(1).wait_send()

        @pl.when(self.straight)
        def _():
            self.f_send().wait_send()

        @pl.when(self.is_source)
        def _():
            for i in range(4):
                self.c_send(i, 0).wait_send()
                self.c_send(i, 1).wait_send()

        @pl.when(self.is_relay)
        def _():
            for i in range(4):
                self.pass_send(i).wait_send()


def splits(a, n):
    parts = []
    for i in range(n):
        h = a.astype(BF)
        parts.append(h)
        if i < n - 1:
            a = a - h.astype(F32)
    return parts


LEFT = {2: (0, 0, 1), 3: (0, 0, 1, 1, 0, 2)}
RIGHT = {2: (0, 1, 0), 3: (0, 1, 0, 1, 2, 0)}


def dot_f32(a, b, dims, n=3):
    sa, sb = splits(a, n), splits(b, n)
    left = jnp.concatenate([sa[i] for i in LEFT[n]], axis=dims[0][0])
    right = jnp.concatenate([sb[i] for i in RIGHT[n]], axis=dims[1][0])
    return lax.dot_general(left, right, (dims, ((), ())), preferred_element_type=F32)


def diagonal_factor(square):
    group = 16
    lane = lax.broadcasted_iota(jnp.int32, (8, B), 1)
    sub = lax.broadcasted_iota(jnp.int32, (8, B), 0)
    spread = lambda x, s: jnp.broadcast_to(x[s : s + 1, :], (8, B))
    rest, upper, lower = square, [], []
    for g in range(B // group):
        r0 = group * g
        p = [rest[8 * v : 8 * v + 8, :] for v in range(2)]
        column = [[jnp.broadcast_to(p[v][:, r0 + j : r0 + j + 1], (8, B)) for v in range(2)] for j in range(group)]
        root = [jnp.zeros((8, B), F32) for _ in range(2)]
        for k in range(group):
            at, s = divmod(k, 8)
            r = lax.rsqrt(spread(column[k][at], s))
            root[at] = jnp.where(sub == s, r, root[at])
            if k == group - 1:
                break
            here = lane == r0 + k
            row = jnp.where(here, 1.0, spread(p[at], s))
            for v in range(at, 2):
                if v == at and s == 7:
                    continue
                factor = column[k][v] * (r * r)
                if v == at:
                    factor = jnp.where(sub > s, factor, 0.0)
                    p[v] = jnp.where(here & (sub > s), 0.0, p[v]) - factor * row
                else:
                    p[v] = jnp.where(here, 0.0, p[v]) - factor * row
                for j in range(k + 1, group):
                    column[j][v] = column[j][v] - factor * spread(column[j][at], s)
        panel = jnp.concatenate([p[v] * root[v] for v in range(2)], axis=0)
        roots = jnp.concatenate(root, axis=0)
        ln = lax.broadcasted_iota(jnp.int32, (group, B), 1) - r0
        sb = lax.broadcasted_iota(jnp.int32, (group, B), 0)
        eliminated = jnp.where(ln == sb, roots, jnp.where((ln > sb) & (ln < group), 0.0, panel))
        upper.append(panel)
        lower.append(jnp.where(ln > sb, 0.0, eliminated))
        if g < B // group - 1:
            change = dot_f32(jnp.where(ln >= group, panel, 0.0), eliminated, ((0,), (0,)))
            lt = lax.broadcasted_iota(jnp.int32, (B - r0 - group, B), 1)
            rest = jnp.where((lt >= r0) & (lt < r0 + group), 0.0, rest[group:, :]) - change[r0 + group :, :]
    return jnp.concatenate(upper, axis=0), jnp.concatenate(lower, axis=0)


def factor_start(sq_ref, lower_ref, work):
    for i in range(NB):
        for j in range(NB):
            at = (slice(i * B, (i + 1) * B), slice(j * B, (j + 1) * B))
            if j < i:
                work[at] = jnp.zeros((B, B), F32)
            else:
                block = lambda r, c: sq_ref[c // 4, c // 2 % 2, c % 2, r // 4, r % 4].astype(F32)
                work[at] = 0.5 * (block(i, j) + block(j, i).T)
    lower_ref[...] = jnp.zeros((B, B), F32)


def factor_step(kb, my_row, my_col, inv_ref, lower_ref, work, left, right):
    lane = lax.broadcasted_iota(jnp.int32, (B, B), 1)
    sub = lax.broadcasted_iota(jnp.int32, (B, B), 0)
    d0 = pl.multiple_of(kb * B, B)
    upper, lower = diagonal_factor(work[pl.ds(d0, B), pl.ds(d0, B)])
    work[pl.ds(d0, B), pl.ds(d0, B)] = jnp.where(lane == sub, 1.0, 0.0)
    panel = dot_f32(lower, work[pl.ds(d0, B), :], ((1,), (0,)), 2)
    col = lax.broadcasted_iota(jnp.int32, (B, N), 1)
    inv_ref[pl.ds(d0, B), :] = jnp.where(col < d0 + B, panel, 0.0).astype(BF)

    @pl.when(kb == my_col)
    def _():
        @pl.when(kb == my_row)
        def _():
            lower_ref[...] = jnp.where(lane >= sub, upper, 0.0).T

        @pl.when(kb < my_row)
        def _():
            work[pl.ds(d0, B), :] = panel
            lower_ref[...] = work[pl.ds(d0, B), pl.ds(pl.multiple_of(my_row * B, B), B)].T

    parts = splits(panel, 2)
    for t in range(3):
        left[t * B : (t + 1) * B, :] = parts[LEFT[2][t]]
        right[t * B : (t + 1) * B, :] = parts[RIGHT[2][t]]

    def trailing(i, _):
        i0 = pl.multiple_of(i * B, B)
        work[pl.ds(i0, B), pl.ds(d0, B)] = jnp.zeros((B, B), F32)
        work[pl.ds(i0, B), :] = work[pl.ds(i0, B), :] - lax.dot_general(
            left[:, pl.ds(i0, B)], right[...], (((0,), (0,)), ((), ())), preferred_element_type=F32
        )
        return 0

    lax.fori_loop(kb + 1, NB, trailing, 0)


def below_rows(portion, inv_ref, lower_ref, keep_ref, my_col, below_ref, first_ref, wide, write):
    safe = jnp.minimum(my_col, NB - 1)

    def rows(i, _):
        a = jnp.concatenate(
            [
                jnp.concatenate([portion[k // 4, k // 2 % 2, k % 2, 2 * i + t // 2, t % 2] for k in range(8)], axis=1)
                for t in range(4)
            ],
            axis=0,
        )
        out = lax.dot_general(a, inv_ref[...], (((1,), (1,)), ((), ())), preferred_element_type=F32)
        for t in range(4):
            l = 4 * i + t
            kept = out[t * B : (t + 1) * B, :] * keep_ref[l]
            wide[t * B : (t + 1) * B, :] = kept
            below_ref[pl.ds(pl.multiple_of(l * B, B), B), :] = kept.astype(BF)
        for t in range(4):
            first_ref[4 * i + t] = wide[t * B : (t + 1) * B, pl.ds(pl.multiple_of(safe * B, B), B)]
        write(i).start()
        return 0

    lax.fori_loop(0, 4, rows, 0)
    first_ref[0] = lower_ref[...]


def below_columns(cols, inv_ref, keep_ref, panel_ref, write):
    def some(i, _):
        a = jnp.concatenate(
            [
                jnp.concatenate([cols[k // 4, k // 2 % 2, k % 2, 4 * i + t] for k in range(8)], axis=1)
                for t in range(4)
            ],
            axis=0,
        )
        out = lax.dot_general(a, inv_ref[...], (((1,), (1,)), ((), ())), preferred_element_type=F32)
        for t in range(4):
            m = 4 * i + t
            kept = out[t * B : (t + 1) * B, :] * keep_ref[16 + m]
            panel_ref[pl.ds(pl.multiple_of(m * B, B), B), :] = kept.astype(BF)
        write(i).start()
        return 0

    lax.fori_loop(0, 2, some, 0)


def factor_kernel(piece, keep_ref, below_hbm, panel_hbm, first_hbm, sq, portion, cols, inv_ref, lower_ref, work, left, right, wide, below_ref, panel_ref, first_ref, out_sem, *sems):
    my_row, my_col = lax.axis_index("row"), lax.axis_index("col")

    def write(i):
        rows = pl.ds(4 * B * i, 4 * B)
        return pltpu.make_async_copy(below_ref.at[rows], below_hbm.at[rows], out_sem.at[i])

    def write_first():
        return pltpu.make_async_copy(first_ref, first_hbm, out_sem.at[4])

    def write_panel(i):
        rows = pl.ds(4 * B * i, 4 * B)
        return pltpu.make_async_copy(panel_ref.at[rows], panel_hbm.at[rows], out_sem.at[5 + i])

    gather = Gather(piece, sq, portion, cols, sems)
    gather.enter()
    gather.square()
    gather.begin()
    factor_start(sq, lower_ref, work)

    def step(kb, _):
        gather.during(kb)
        factor_step(kb, my_row, my_col, inv_ref, lower_ref, work, left, right)
        return 0

    lax.fori_loop(0, NB, step, 0)
    gather.after()
    below_rows(portion, inv_ref, lower_ref, keep_ref, my_col, below_ref, first_ref, wide, write)
    write_first().start()
    gather.end()
    below_columns(cols, inv_ref, keep_ref, panel_ref, write_panel)
    gather.finish()
    for i in range(4):
        write(i).wait()
    write_first().wait()
    for i in range(2):
        write_panel(i).wait()


FACTOR_OUT = (
    jax.ShapeDtypeStruct((16 * B, N), BF),
    jax.ShapeDtypeStruct((8 * B, N), BF),
    jax.ShapeDtypeStruct((16, B, B), F32),
)
FACTOR_SCRATCH = (
    ((2, 2, 2, 2, 4, B, B), BF),
    ((2, 2, 2, 8, 2, B, B), BF),
    ((2, 2, 2, 8, B, B), BF),
    ((N, N), BF),
    ((B, B), F32),
    ((N, N), F32),
    ((3 * B, N), BF),
    ((3 * B, N), BF),
    ((4 * B, N), F32),
)


def factor(piece, keep):
    return pl.pallas_call(
        factor_kernel,
        out_shape=FACTOR_OUT,
        in_specs=[VM, SM],
        out_specs=(ANY, ANY, ANY),
        scratch_shapes=[pltpu.VMEM(s, d) for s, d in FACTOR_SCRATCH]
        + [pltpu.VMEM(o.shape, o.dtype) for o in FACTOR_OUT]
        + [pltpu.SemaphoreType.DMA((7,))]
        + [pltpu.SemaphoreType.DMA((n,)) for n in Gather.SEMS],
        compiler_params=params(32, collective_id=2, has_side_effects=True),
    )(piece, keep)


def schur_kernel(tab, front, arrived, below, panel, first, out_ref):
    i = pl.program_id(0)
    my_col = lax.axis_index("col")
    product = lax.dot_general(below[...], panel[...], (((1,), (1,)), ((), ())), preferred_element_type=F32)
    sub = lax.broadcasted_iota(jnp.int32, (B, 8, B), 1)
    taken = (sub == 0) & (my_col < NB)
    for s in range(2):
        l = 2 * i + s
        values = []
        for m in range(8):
            value = -product[s * B : (s + 1) * B, m * B : (m + 1) * B]
            for h in range(2):
                valid = tab[AT_RCH + h * 16 + l] == tab[AT_CCH + h * 8 + m]
                at = jnp.where(valid, tab[AT_RSRC + h * 16 + l] + tab[AT_CSRC + h * 8 + m], 0)
                value = value + jnp.where(valid, arrived[at].astype(F32), 0.0)
            if s == 0:
                value = jnp.where(l == 0, 0.0, value)
            if m == 0:
                value = jnp.where(my_col < NB, first[s], value)
            values.append(value)
        drop = taken | (l == 0) if s == 0 else taken
        out_ref[s] = jnp.swapaxes(jnp.stack(values), 0, 1) + jnp.where(drop, 0.0, front[s].astype(F32))


def schur(tab, front, arrived, below, panel, first):
    full = lambda shape: pl.BlockSpec(shape, lambda i, t: (0,) * len(shape))
    return pl.pallas_call(
        schur_kernel,
        out_shape=jax.ShapeDtypeStruct((16, B, 8, B), F32),
        grid_spec=pltpu.PrefetchScalarGridSpec(
            num_scalar_prefetch=1,
            grid=(8,),
            in_specs=[
                pl.BlockSpec((2, B, 8, B), lambda i, t: (i, 0, 0, 0)),
                full((256, B, B)),
                pl.BlockSpec((2 * B, N), lambda i, t: (i, 0)),
                full((N, N)),
                pl.BlockSpec((2, B, B), lambda i, t: (i, 0, 0)),
            ],
            out_specs=pl.BlockSpec((2, B, 8, B), lambda i, t: (i, 0, 0, 0)),
        ),
        compiler_params=params(28),
    )(tab, front, arrived, below, panel, first)


def per_device(child_update_blocks, child_pivot_panel, child_map, coupled, parent_front):
    my_row, my_col = lax.axis_index("row"), lax.axis_index("col")
    front = parent_front.reshape(16, B, 8, B)
    out_tab = table(outgoing_kernel, 32, child_map)
    outgoing = contributions(out_tab, child_pivot_panel.reshape(8, 2, B, B), child_update_blocks.reshape(16, B, 8, B))
    incoming = lax.all_to_all(outgoing, ("row", "col"), split_axis=0, concat_axis=0, tiled=True)
    arrived = incoming.reshape(256, B, B)
    later_map, later_coupled, _ = lax.optimization_barrier((child_map, coupled, outgoing))
    in_tab = table(incoming_kernel, 96, later_map)
    kept = jnp.concatenate([jnp.ones((NB,), F32), later_coupled.astype(F32)])
    keep = jnp.concatenate(
        [
            lax.dynamic_index_in_dim(kept.reshape(16, 8), my_row, 1, keepdims=False),
            lax.dynamic_index_in_dim(kept.reshape(8, 16), my_col, 1, keepdims=False),
        ]
    )
    pivots = pivot_columns(in_tab, arrived, front[:, :, 0, :])
    below, panel, first = factor(pivots.reshape(8, 2, B, B), keep)
    out = schur(in_tab, front, arrived, below, panel, first)
    return out.reshape(1, 16, B, 1, 8, B)


def solution(mesh):
    in_specs = (
        P("row", None, None, "col", None, None),
        P("row", None, None, "col", None),
        P(),
        P(),
        P("row", None, None, "col", None, None),
    )
    out_specs = P("row", None, None, "col", None, None)
    return jax.shard_map(per_device, mesh=mesh, in_specs=in_specs, out_specs=out_specs, check_vma=False)
```

time: 340 us -> 280 us (0.82)
  the two profiles are of different devices: /device:TPU:112 before, /device:TPU:114 now
where the time goes in v4:
time: 280 us; the launch traced here: 279 us
  Pallas kernels  176 us (63%)
  waiting for transfers between devices  86.4 us (31%)
  starting transfers between devices  12.5 us (4%)
  local copies, waits for them, and re-layouts  4.46 us (2%)
    pallas_call x1, Pallas kernels, factor(): pl.pallas_call(factor_kernel, out_shape=FACTOR_OUT, in_specs=[VM, SM], ou...  99.4 us
    all_to_all x1, waiting for transfers between devices, per_device(): lax.all_to_all(outgoing, ('row', 'col'), split_axis=0, concat_axis=0, til...  86.4 us
    pallas_call x1, Pallas kernels, contributions(): pl.pallas_call(contribution_kernel, out_shape=jax.ShapeDtypeStruct((128,...  49.8 us
    pallas_call x1, Pallas kernels, schur(): pl.pallas_call(schur_kernel, out_shape=jax.ShapeDtypeStruct((16, B, 8, B)...  14 us
    all_to_all x1, starting transfers between devices, per_device(): lax.all_to_all(outgoing, ('row', 'col'), split_axis=0, concat_axis=0, til...  12.5 us
    pallas_call x2, Pallas kernels, table(): pl.pallas_call(kernel, out_shape=jax.ShapeDtypeStruct((size,), jnp.int32)...  10.1 us
  transfers between devices with their start and end apart: 1, of which 1 were waited for; matrix products, arithmetic and copies ran while one was open for 1% of the time, Pallas kernels for 3%

profile of v4, /device:TPU:114, one launch (start us, length us, event | category | flops | bytes accessed | tf_op | source)
XLA Modules:
  0.0 279.2 jit_solution(17419298047401814023)
XLA Ops:
  0.0 1.5 shard_map.55.tab
  1.5 49.8 %shard_map.56 = bf16[128,256,128]{2,1,0:T(8,128)(2,1)} custom-call(s32[32]{0:T(128)} %shard_map.55.tab, bf16[8,2,128,128]{3,2,1,0:T(8,128)(2,1)} %bitcast.16, bf16[16,128,8,128]{3,2,1,0:T(8,128)(2,1)} %bitcast.15), custom_call_target="tpu_custom_call" | custom-call | tf_op jit(solution)/shard_map/pallas_call | solution.py:280
  51.3 0.0 copy-start.3
  51.4 12.5 %all-to-all-start = ((bf16[128,256,128]{2,1,0:T(8,128)(2,1)}), bf16[128,256,128]{2,1,0:T(8,128)(2,1)}, u32[]{:S(2)}, u32[]{:S(2)}) async-start(bf16[128,256,128]{2,1,0:T(8,128)(2,1)} %shard_map.56), calls=%async_computation | async-start | bytes 16777216 | tf_op jit(solution)/shard_map/all_to_all | solution.py:916
  63.9 8.6 %shard_map.57.tab = s32[96]{0:T(128)} custom-call(s32[4,64]{1,0:T(4,128)} %map_ref.2), custom_call_target="tpu_custom_call" | custom-call | flops 20000 | bytes 2048 | tf_op jit(solution)/shard_map/pallas_call | solution.py:86
  72.5 0.0 copy-done.3
  72.5 0.1 concatenate.6
  72.6 0.1 reshape.30
  72.7 0.1 reshape.29
  72.8 3.1 %slice.4 = bf16[16,128,1,128]{3,2,1,0:T(2,128)(2,1)S(1)} slice(bf16[16,128,8,128]{3,2,1,0:T(8,128)(2,1)} %bitcast.11), slice={[0:16], [0:128], [0:1], [0:128]} | slice | bytes 1048576 | tf_op jit(solution)/shard_map/slice | solution.py:927
  75.9 0.1 copy.10
  76.0 0.2 dynamic-slice_reduce_fusion.1
  76.2 0.2 dynamic-slice_reduce_fusion
  76.3 0.1 pad_maximum_fusion.keep_ref
  76.4 86.4 %all-to-all-done = bf16[128,256,128]{2,1,0:T(8,128)(2,1)} async-done(((bf16[128,256,128]{2,1,0:T(8,128)(2,1)}), bf16[128,256,128]{2,1,0:T(8,128)(2,1)}, u32[]{:S(2)}, u32[]{:S(2)}) %all-to-all-start) | async-done | bytes 8388640 | tf_op jit(solution)/shard_map/all_to_all | solution.py:916
  162.9 0.0 copy-start.1
  162.9 0.7 copy-done.1
  163.5 0.0 copy-start
  163.5 0.0 copy-start.2
  163.5 2.3 shard_map.58
  165.8 99.4 %shard_map.59 = (bf16[2048,1024]{1,0:T(8,128)(2,1)S(1)}, bf16[1024,1024]{1,0:T(8,128)(2,1)S(1)}, f32[16,128,128]{2,1,0:T(8,128)S(1)}) custom-call(bf16[8,2,128,128]{3,2,1,0:T(8,128)(2,1)S(1)} %bitcast.14, f32[24]{0:T(128)S(1)} %pad_maximum_fusion.keep_ref), custom_call_target="tpu_custom_call" | custom-call | tf_op jit(solution)/shard_map/pallas_call | solution.py:853
  265.2 0.0 copy-done
  265.2 0.0 copy-done.2
  265.2 14.0 %shard_map.60 = f32[16,128,8,128]{3,2,1,0:T(8,128)} custom-call(s32[96]{0:T(128)S(1)} %copy-done.2, bf16[16,128,8,128]{3,2,1,0:T(8,128)(2,1)S(1)} %bitcast.12, bf16[256,128,128]{2,1,0:T(8,128)(2,1)} %bitcast.3.arrived, bf16[2048,1024]{1,0:T(8,128)(2,1)S(1)} %get-tuple-element.12.below, bf16[1024,1024]{1,0:T(8,128)(2,1)S(1)} %get-tuple-element.13.panel, ...), custom_call_target="tpu_custom_call" | custom-call | tf_op jit(solution)/shard_map/pallas_call | solution.py:892
  (1 shorter events, 0.0 us)
Async XLA Ops:
  51.3 21.2 %copy-start.3 = (s32[120]{0:T(128)S(1)}, s32[120]{0:T(128)}, u32[]{:S(2)}) copy-start(s32[120]{0:T(128)} %param.8) | copy-start | bytes 1444
  51.4 111.5 %all-to-all-start = ((bf16[128,256,128]{2,1,0:T(8,128)(2,1)}), bf16[128,256,128]{2,1,0:T(8,128)(2,1)}, u32[]{:S(2)}, u32[]{:S(2)}) async-start(bf16[128,256,128]{2,1,0:T(8,128)(2,1)} %shard_map.56), calls=%async_computation | async-start | bytes 16777216 | tf_op jit(solution)/shard_map/all_to_all | solution.py:916
  162.9 0.7 copy-start.1
  163.5 101.7 %copy-start = (bf16[1,16,128,1,8,128]{5,4,3,2,1,0:T(8,128)(2,1)S(1)}, bf16[1,16,128,1,8,128]{5,4,3,2,1,0:T(8,128)(2,1)}, u32[]{:S(2)}) copy-start(bf16[1,16,128,1,8,128]{5,4,3,2,1,0:T(8,128)(2,1)} %param.9) | copy-start | bytes 12582916
  163.5 101.7 %copy-start.2 = (s32[96]{0:T(128)S(1)}, s32[96]{0:T(128)}, u32[]{:S(2)}) copy-start(s32[96]{0:T(128)} %shard_map.57.tab) | copy-start | bytes 1156

commit v5 on v4

--- a/solution.py
+++ b/solution.py
@@ -23,36 +23,13 @@
     return pltpu.CompilerParams(vmem_limit_bytes=mib * MIB, **kw)
 
 
-OUT_ROW, OUT_COL = 0, 16
 AT_RSRC, AT_RCH, AT_CSRC, AT_CCH = 0, 32, 64, 80
-
-
-def clear(count):
-    def one(i, _):
-        count[i] = 0
-        return 0
-
-    lax.fori_loop(0, 16, one, 0)
-
-
-def outgoing_kernel(map_ref, tab_ref, count):
-    my_row, my_col = lax.axis_index("row"), lax.axis_index("col")
-    row_rank, col_rank = my_row % 4, my_col % 8
-    child = 2 * (my_row // 4) + my_col // 8
-    clear(count)
-    for l in range(16):
-        owner = map_ref[child, l * 4 + row_rank] % 8
-        tab_ref[OUT_ROW + owner * 2 + count[owner]] = l
-        count[owner] = count[owner] + 1
-    for c in range(16):
-        tab_ref[OUT_COL + c] = 0
-    for m in range(8):
-        tab_ref[OUT_COL + map_ref[child, m * 8 + col_rank] % 16] = m
 
 
 def incoming_kernel(map_ref, tab_ref, count):
     my_row, my_col = lax.axis_index("row"), lax.axis_index("col")
-    clear(count)
+    for i in range(16):
+        count[i] = 0
 
     def arrive(q, _):
         h, g = q // 2, q % 2
@@ -99,7 +76,7 @@
     )
 
 
-def contribution_kernel(tab, p_ref, u_hbm, out_hbm, row_ref, col_ref, total, u_ref, block, slots, local, s_chip, s_sib, s_col, r_row, r_col):
+def contribution_kernel(map_ref, p_ref, u_hbm, out_hbm, row_ref, col_ref, total, u_ref, block, slots, goes, local, s_chip, s_sib, s_col, r_row, r_col):
     my_row, my_col = lax.axis_index("row"), lax.axis_index("col")
     base, y = my_row // 4 * 4, my_row % 4
     half, cc = my_col // 8 * 8, my_col % 8
@@ -210,6 +187,13 @@
                 col_send(0, 1).start()
 
     row_ref[cc] = p_ref[...]
+    child = 2 * (my_row // 4) + my_col // 8
+    targets = [map_ref[child, m * 8 + cc] % 16 for m in range(8)]
+    for c in range(16):
+        at = 0
+        for m in range(1, 8):
+            at = jnp.where(targets[m] == c, m, at)
+        goes[c] = at
     for e in range(1, 8):
         row_wait(e, 0)
         if 2 <= e < 5:
@@ -247,10 +231,13 @@
         def _():
             emit(owner - 2, slot).wait()
 
-        for s in range(2):
-            l = tab[OUT_ROW + owner * 2 + s]
+        pair = [0, 0]
+        for l in range(15, -1, -1):
+            here = map_ref[child, l * 4 + y] % 8 == owner
+            pair = [jnp.where(here, l, pair[0]), jnp.where(here, pair[0], pair[1])]
+        for s, l in enumerate(pair):
             for c in range(16):
-                slots[slot, c, s * B : (s + 1) * B, :] = block[tab[OUT_COL + c], l]
+                slots[slot, c, s * B : (s + 1) * B, :] = block[goes[c], l]
         emit(owner, slot).start()
         return 0
 
@@ -275,7 +262,7 @@
             pass_on(e).wait_send()
 
 
-def contributions(tab, piece, update):
+def contributions(child_map, piece, update):
     dma = pltpu.SemaphoreType.DMA
     return pl.pallas_call(
         contribution_kernel,
@@ -289,6 +276,7 @@
             pltpu.VMEM((16, B, 8, B), BF),
             pltpu.VMEM((8, 16, B, B), BF),
             pltpu.VMEM((2, 16, 2 * B, B), BF),
+            pltpu.SMEM((16,), jnp.int32),
             dma((3,)),
             dma((3, 2)),
             dma((4, 2)),
@@ -297,7 +285,7 @@
             dma((8,)),
         ],
         compiler_params=params(56, collective_id=1, has_side_effects=True),
-    )(tab, piece, update)
+    )(child_map, piece, update)
 
 
 def pivot_kernel(tab, arrived, front, out_ref, block, sem):
@@ -561,13 +549,13 @@
         def _():
             self.px_send().start()
 
-        for step, i in ((3, 0), (3, 1), (3, 2), (3, 3)):
+        for step, i in ((4, 0), (4, 1), (4, 2), (4, 3)):
 
             @pl.when(kb == step)
             def _():
                 self.turn(i)
 
-        for step, i in ((4, 0), (5, 1), (6, 2), (7, 3)):
+        for step, i in ((5, 0), (6, 1), (7, 2)):
 
             @pl.when((kb == step) & turned)
             def _():
@@ -591,9 +579,7 @@
             self.spread(3)
 
     def after(self):
-        @pl.when(self.straight)
-        def _():
-            self.relay(3)
+        self.relay(3)
 
     def end(self):
         @pl.when(jnp.logical_not(self.is_source | self.is_relay))
@@ -653,7 +639,10 @@
     return lax.dot_general(left, right, (dims, ((), ())), preferred_element_type=F32)
 
 
-def diagonal_factor(square):
+POS = 3
+
+
+def diagonal_factor(square, beside):
     group = 16
     lane = lax.broadcasted_iota(jnp.int32, (8, B), 1)
     sub = lax.broadcasted_iota(jnp.int32, (8, B), 0)
@@ -665,6 +654,8 @@
         column = [[jnp.broadcast_to(p[v][:, r0 + j : r0 + j + 1], (8, B)) for v in range(2)] for j in range(group)]
         root = [jnp.zeros((8, B), F32) for _ in range(2)]
         for k in range(group):
+            if k % 8 == POS and beside:
+                beside.pop(0)()
             at, s = divmod(k, 8)
             r = lax.rsqrt(spread(column[k][at], s))
             root[at] = jnp.where(sub == s, r, root[at])
@@ -697,7 +688,7 @@
     return jnp.concatenate(upper, axis=0), jnp.concatenate(lower, axis=0)
 
 
-def factor_start(sq_ref, lower_ref, work):
+def factor_start(sq_ref, lower_ref, work, left, right):
     for i in range(NB):
         for j in range(NB):
             at = (slice(i * B, (i + 1) * B), slice(j * B, (j + 1) * B))
@@ -707,43 +698,64 @@
                 block = lambda r, c: sq_ref[c // 4, c // 2 % 2, c % 2, r // 4, r % 4].astype(F32)
                 work[at] = 0.5 * (block(i, j) + block(j, i).T)
     lower_ref[...] = jnp.zeros((B, B), F32)
+    left[...] = jnp.zeros_like(left)
+    right[...] = jnp.zeros_like(right)
+
+
+def trailing(i, k0, work, left, right, half=None):
+    cols = slice(0, N) if half is None else slice(half * N // 2, (half + 1) * N // 2)
+    i0 = pl.multiple_of(jnp.minimum(i, NB) * B, B)
+    part = left[:, pl.ds(pl.multiple_of(jnp.minimum(i, NB - 1) * B, B), B)]
+    if not half:
+        work[pl.ds(i0, B), pl.ds(k0, B)] = jnp.zeros((B, B), F32)
+    work[pl.ds(i0, B), cols] = work[pl.ds(i0, B), cols] - lax.dot_general(
+        part, right[:, cols], (((0,), (0,)), ((), ())), preferred_element_type=F32
+    )
 
 
 def factor_step(kb, my_row, my_col, inv_ref, lower_ref, work, left, right):
     lane = lax.broadcasted_iota(jnp.int32, (B, B), 1)
     sub = lax.broadcasted_iota(jnp.int32, (B, B), 0)
     d0 = pl.multiple_of(kb * B, B)
-    upper, lower = diagonal_factor(work[pl.ds(d0, B), pl.ds(d0, B)])
+    before = pl.multiple_of(jnp.maximum(kb - 1, 0) * B, B)
+    beside = [
+        functools.partial(trailing, kb + t, before, work, left, right, half) for t in range(1, NB - 1) for half in range(2)
+    ]
+    upper, lower = diagonal_factor(work[pl.ds(d0, B), pl.ds(d0, B)], beside)
+    for piece in beside:
+        piece()
     work[pl.ds(d0, B), pl.ds(d0, B)] = jnp.where(lane == sub, 1.0, 0.0)
     panel = dot_f32(lower, work[pl.ds(d0, B), :], ((1,), (0,)), 2)
     col = lax.broadcasted_iota(jnp.int32, (B, N), 1)
     inv_ref[pl.ds(d0, B), :] = jnp.where(col < d0 + B, panel, 0.0).astype(BF)
-
-    @pl.when(kb == my_col)
-    def _():
-        @pl.when(kb == my_row)
-        def _():
-            lower_ref[...] = jnp.where(lane >= sub, upper, 0.0).T
-
-        @pl.when(kb < my_row)
-        def _():
-            work[pl.ds(d0, B), :] = panel
-            lower_ref[...] = work[pl.ds(d0, B), pl.ds(pl.multiple_of(my_row * B, B), B)].T
-
     parts = splits(panel, 2)
     for t in range(3):
         left[t * B : (t + 1) * B, :] = parts[LEFT[2][t]]
         right[t * B : (t + 1) * B, :] = parts[RIGHT[2][t]]
-
-    def trailing(i, _):
-        i0 = pl.multiple_of(i * B, B)
-        work[pl.ds(i0, B), pl.ds(d0, B)] = jnp.zeros((B, B), F32)
-        work[pl.ds(i0, B), :] = work[pl.ds(i0, B), :] - lax.dot_general(
-            left[:, pl.ds(i0, B)], right[...], (((0,), (0,)), ((), ())), preferred_element_type=F32
+    trailing(kb + 1, d0, work, left, right)
+
+    @pl.when(kb == my_col)
+    def _():
+        @pl.when(kb == my_row)
+        def _():
+            lower_ref[...] = jnp.where(lane >= sub, upper, 0.0).T
+
+        @pl.when(kb < my_row)
+        def _():
+            work[pl.ds(d0, B), :] = panel
+            lower_ref[...] = work[pl.ds(d0, B), pl.ds(pl.multiple_of(my_row * B, B), B)].T
+
+
+def below_tiles(a, inv_ref):
+    tiles = []
+    for c in range(0, N, 2 * B):
+        end = c + 2 * B
+        tiles.append(
+            lax.dot_general(
+                a[:, :end], inv_ref[c:end, :end], (((1,), (1,)), ((), ())), preferred_element_type=F32
+            )
         )
-        return 0
-
-    lax.fori_loop(kb + 1, NB, trailing, 0)
+    return tiles
 
 
 def below_rows(portion, inv_ref, lower_ref, keep_ref, my_col, below_ref, first_ref, wide, write):
@@ -757,12 +769,13 @@
             ],
             axis=0,
         )
-        out = lax.dot_general(a, inv_ref[...], (((1,), (1,)), ((), ())), preferred_element_type=F32)
-        for t in range(4):
-            l = 4 * i + t
-            kept = out[t * B : (t + 1) * B, :] * keep_ref[l]
-            wide[t * B : (t + 1) * B, :] = kept
-            below_ref[pl.ds(pl.multiple_of(l * B, B), B), :] = kept.astype(BF)
+        for c, out in enumerate(below_tiles(a, inv_ref)):
+            cols = slice(2 * B * c, 2 * B * (c + 1))
+            for t in range(4):
+                l = 4 * i + t
+                kept = out[t * B : (t + 1) * B, :] * keep_ref[l]
+                wide[t * B : (t + 1) * B, cols] = kept
+                below_ref[pl.ds(pl.multiple_of(l * B, B), B), cols] = kept.astype(BF)
         for t in range(4):
             first_ref[4 * i + t] = wide[t * B : (t + 1) * B, pl.ds(pl.multiple_of(safe * B, B), B)]
         write(i).start()
@@ -781,11 +794,11 @@
             ],
             axis=0,
         )
-        out = lax.dot_general(a, inv_ref[...], (((1,), (1,)), ((), ())), preferred_element_type=F32)
-        for t in range(4):
-            m = 4 * i + t
-            kept = out[t * B : (t + 1) * B, :] * keep_ref[16 + m]
-            panel_ref[pl.ds(pl.multiple_of(m * B, B), B), :] = kept.astype(BF)
+        for c, out in enumerate(below_tiles(a, inv_ref)):
+            for t in range(4):
+                m = 4 * i + t
+                kept = out[t * B : (t + 1) * B, :] * keep_ref[16 + m]
+                panel_ref[pl.ds(pl.multiple_of(m * B, B), B), 2 * B * c : 2 * B * (c + 1)] = kept.astype(BF)
         write(i).start()
         return 0
 
@@ -810,7 +823,7 @@
     gather.enter()
     gather.square()
     gather.begin()
-    factor_start(sq, lower_ref, work)
+    factor_start(sq, lower_ref, work, left, right)
 
     def step(kb, _):
         gather.during(kb)
@@ -842,7 +855,7 @@
     ((2, 2, 2, 8, B, B), BF),
     ((N, N), BF),
     ((B, B), F32),
-    ((N, N), F32),
+    ((N + B, N), F32),
     ((3 * B, N), BF),
     ((3 * B, N), BF),
     ((4 * B, N), F32),
@@ -911,8 +924,7 @@
 def per_device(child_update_blocks, child_pivot_panel, child_map, coupled, parent_front):
     my_row, my_col = lax.axis_index("row"), lax.axis_index("col")
     front = parent_front.reshape(16, B, 8, B)
-    out_tab = table(outgoing_kernel, 32, child_map)
-    outgoing = contributions(out_tab, child_pivot_panel.reshape(8, 2, B, B), child_update_blocks.reshape(16, B, 8, B))
+    outgoing = contributions(child_map, child_pivot_panel.reshape(8, 2, B, B), child_update_blocks.reshape(16, B, 8, B))
     incoming = lax.all_to_all(outgoing, ("row", "col"), split_axis=0, concat_axis=0, tiled=True)
     arrived = incoming.reshape(256, B, B)
     later_map, later_coupled, _ = lax.optimization_barrier((child_map, coupled, outgoing))

time: 280 us -> 277 us (0.989)
  the two profiles are of different devices: /device:TPU:114 before, /device:TPU:112 now
where the time goes in v5:
time: 277 us; the launch traced here: 276 us
  Pallas kernels  171 us (62%)
  waiting for transfers between devices  87.7 us (32%)
  starting transfers between devices  12.5 us (5%)
  local copies, waits for them, and re-layouts  4.46 us (2%)
    pallas_call x1, Pallas kernels, factor(): pl.pallas_call(factor_kernel, out_shape=FACTOR_OUT, in_specs=[VM, SM], ou...  96.1 us
    all_to_all x1, waiting for transfers between devices, per_device(): lax.all_to_all(outgoing, ('row', 'col'), split_axis=0, concat_axis=0, til...  87.7 us
    pallas_call x1, Pallas kernels, contributions(): pl.pallas_call(contribution_kernel, out_shape=jax.ShapeDtypeStruct((128,...  49.9 us
    pallas_call x1, Pallas kernels, schur(): pl.pallas_call(schur_kernel, out_shape=jax.ShapeDtypeStruct((16, B, 8, B)...  14 us
    all_to_all x1, starting transfers between devices, per_device(): lax.all_to_all(outgoing, ('row', 'col'), split_axis=0, concat_axis=0, til...  12.5 us
    pallas_call x1, Pallas kernels, table(): pl.pallas_call(kernel, out_shape=jax.ShapeDtypeStruct((size,), jnp.int32)...  8.52 us
  transfers between devices with their start and end apart: 1, of which 1 were waited for; matrix products, arithmetic and copies ran while one was open for 1% of the time, Pallas kernels for 3%

profile of v5, /device:TPU:112, one launch (start us, length us, event | category | flops | bytes accessed | tf_op | source)
XLA Modules:
  0.0 275.6 jit_solution(12428090177609798368)
XLA Ops:
  0.0 49.9 %shard_map.55 = bf16[128,256,128]{2,1,0:T(8,128)(2,1)} custom-call(s32[4,64]{1,0:T(4,128)} %map_ref.2, bf16[8,2,128,128]{3,2,1,0:T(8,128)(2,1)} %bitcast.16, bf16[16,128,8,128]{3,2,1,0:T(8,128)(2,1)} %bitcast.15), custom_call_target="tpu_custom_call" | custom-call | tf_op jit(solution)/shard_map/pallas_call | solution.py:267
  49.9 0.0 copy-start.3
  49.9 12.5 %all-to-all-start = ((bf16[128,256,128]{2,1,0:T(8,128)(2,1)}), bf16[128,256,128]{2,1,0:T(8,128)(2,1)}, u32[]{:S(2)}, u32[]{:S(2)}) async-start(bf16[128,256,128]{2,1,0:T(8,128)(2,1)} %shard_map.55), calls=%async_computation | async-start | bytes 16777216 | tf_op jit(solution)/shard_map/all_to_all | solution.py:928
  62.4 8.5 %shard_map.56.tab = s32[96]{0:T(128)} custom-call(s32[4,64]{1,0:T(4,128)} %map_ref.2), custom_call_target="tpu_custom_call" | custom-call | flops 20000 | bytes 2048 | tf_op jit(solution)/shard_map/pallas_call | solution.py:63
  71.0 0.0 copy-done.3
  71.0 0.1 concatenate.6
  71.0 0.1 reshape.30
  71.1 0.1 reshape.29
  71.2 3.1 %slice.4 = bf16[16,128,1,128]{3,2,1,0:T(2,128)(2,1)S(1)} slice(bf16[16,128,8,128]{3,2,1,0:T(8,128)(2,1)} %bitcast.11), slice={[0:16], [0:128], [0:1], [0:128]} | slice | bytes 1048576 | tf_op jit(solution)/shard_map/slice | solution.py:939
  74.3 0.1 copy.10
  74.4 0.2 dynamic-slice_reduce_fusion.1
  74.6 0.2 dynamic-slice_reduce_fusion
  74.8 0.1 pad_maximum_fusion.keep_ref
  74.9 87.7 %all-to-all-done = bf16[128,256,128]{2,1,0:T(8,128)(2,1)} async-done(((bf16[128,256,128]{2,1,0:T(8,128)(2,1)}), bf16[128,256,128]{2,1,0:T(8,128)(2,1)}, u32[]{:S(2)}, u32[]{:S(2)}) %all-to-all-start) | async-done | bytes 8388640 | tf_op jit(solution)/shard_map/all_to_all | solution.py:928
  162.5 0.0 copy-start.1
  162.5 0.7 copy-done.1
  163.2 0.0 copy-start
  163.2 0.0 copy-start.2
  163.2 2.3 shard_map.57
  165.5 96.1 %shard_map.58 = (bf16[2048,1024]{1,0:T(8,128)(2,1)S(1)}, bf16[1024,1024]{1,0:T(8,128)(2,1)S(1)}, f32[16,128,128]{2,1,0:T(8,128)S(1)}) custom-call(bf16[8,2,128,128]{3,2,1,0:T(8,128)(2,1)S(1)} %bitcast.14, f32[24]{0:T(128)S(1)} %pad_maximum_fusion.keep_ref), custom_call_target="tpu_custom_call" | custom-call | tf_op jit(solution)/shard_map/pallas_call | solution.py:866
  261.6 0.0 copy-done
  261.6 0.0 copy-done.2
  261.6 14.0 %shard_map.59 = f32[16,128,8,128]{3,2,1,0:T(8,128)} custom-call(s32[96]{0:T(128)S(1)} %copy-done.2, bf16[16,128,8,128]{3,2,1,0:T(8,128)(2,1)S(1)} %bitcast.12, bf16[256,128,128]{2,1,0:T(8,128)(2,1)} %bitcast.3.arrived, bf16[2048,1024]{1,0:T(8,128)(2,1)S(1)} %get-tuple-element.12.below, bf16[1024,1024]{1,0:T(8,128)(2,1)S(1)} %get-tuple-element.13.panel, ...), custom_call_target="tpu_custom_call" | custom-call | tf_op jit(solution)/shard_map/pallas_call | solution.py:905
  (1 shorter events, 0.0 us)
Async XLA Ops:
  49.9 21.1 %copy-start.3 = (s32[120]{0:T(128)S(1)}, s32[120]{0:T(128)}, u32[]{:S(2)}) copy-start(s32[120]{0:T(128)} %param.8) | copy-start | bytes 1444
  49.9 112.6 %all-to-all-start = ((bf16[128,256,128]{2,1,0:T(8,128)(2,1)}), bf16[128,256,128]{2,1,0:T(8,128)(2,1)}, u32[]{:S(2)}, u32[]{:S(2)}) async-start(bf16[128,256,128]{2,1,0:T(8,128)(2,1)} %shard_map.55), calls=%async_computation | async-start | bytes 16777216 | tf_op jit(solution)/shard_map/all_to_all | solution.py:928
  162.5 0.7 copy-start.1
  163.2 98.4 %copy-start = (bf16[1,16,128,1,8,128]{5,4,3,2,1,0:T(8,128)(2,1)S(1)}, bf16[1,16,128,1,8,128]{5,4,3,2,1,0:T(8,128)(2,1)}, u32[]{:S(2)}) copy-start(bf16[1,16,128,1,8,128]{5,4,3,2,1,0:T(8,128)(2,1)} %param.9) | copy-start | bytes 12582916
  163.2 98.4 %copy-start.2 = (s32[96]{0:T(128)S(1)}, s32[96]{0:T(128)}, u32[]{:S(2)}) copy-start(s32[96]{0:T(128)} %shard_map.56.tab) | copy-start | bytes 1156

commit v6 on v5

--- a/solution.py
+++ b/solution.py
@@ -466,6 +466,7 @@
             self.bx_send(xl, xh).start()
             self.arrived(self.along_x(y, self.k), self.r_y3.at[y])
             self.by_send(y).start()
+        self.early()
         for i in range(4):
             self.arrived(self.along_y(i % 2, i // 2, 1 - self.k), self.r_bx.at[i])
             self.arrived(self.along_x(i, 1 - self.k), self.r_by.at[i])
@@ -523,7 +524,7 @@
             self.arrived(self.group(i), self.r_c.at[i])
             self.pass_send(i).start()
 
-    def begin(self):
+    def early(self):
         for zp in range(2):
 
             @pl.when(self.z != zp)
@@ -534,6 +535,7 @@
         def _():
             self.f_send().start()
 
+    def begin(self):
         self.ps_send(0).start()
         self.spread(0)
 
@@ -542,12 +544,9 @@
 
         @pl.when(kb == 1)
         def _():
+            self.px_send().start()
             self.arrived(self.two(self.xh, 1 - self.k), self.r_ps.at[0])
             self.spread(1)
-
-        @pl.when(kb == 2)
-        def _():
-            self.px_send().start()
 
         for step, i in ((4, 0), (4, 1), (4, 2), (4, 3)):
 

time: 277 us -> 277 us (level)
  no operation moved by 1% of the time
where the time goes in v6:
time: 277 us; the launch traced here: 276 us
  Pallas kernels  171 us (62%)
  waiting for transfers between devices  87.7 us (32%)
  starting transfers between devices  12.5 us (5%)
  local copies, waits for them, and re-layouts  4.46 us (2%)
    pallas_call x1, Pallas kernels, factor(): pl.pallas_call(factor_kernel, out_shape=FACTOR_OUT, in_specs=[VM, SM], ou...  96.1 us
    all_to_all x1, waiting for transfers between devices, per_device(): lax.all_to_all(outgoing, ('row', 'col'), split_axis=0, concat_axis=0, til...  87.7 us
    pallas_call x1, Pallas kernels, contributions(): pl.pallas_call(contribution_kernel, out_shape=jax.ShapeDtypeStruct((128,...  49.9 us
    pallas_call x1, Pallas kernels, schur(): pl.pallas_call(schur_kernel, out_shape=jax.ShapeDtypeStruct((16, B, 8, B)...  14 us
    all_to_all x1, starting transfers between devices, per_device(): lax.all_to_all(outgoing, ('row', 'col'), split_axis=0, concat_axis=0, til...  12.5 us
    pallas_call x1, Pallas kernels, table(): pl.pallas_call(kernel, out_shape=jax.ShapeDtypeStruct((size,), jnp.int32)...  8.52 us
  transfers between devices with their start and end apart: 1, of which 1 were waited for; matrix products, arithmetic and copies ran while one was open for 1% of the time, Pallas kernels for 3%

profile of v6, /device:TPU:112, one launch (start us, length us, event | category | flops | bytes accessed | tf_op | source)
XLA Modules:
  0.0 275.7 jit_solution(6466824805164081394)
XLA Ops:
  0.0 49.9 %shard_map.55 = bf16[128,256,128]{2,1,0:T(8,128)(2,1)} custom-call(s32[4,64]{1,0:T(4,128)} %map_ref.2, bf16[8,2,128,128]{3,2,1,0:T(8,128)(2,1)} %bitcast.16, bf16[16,128,8,128]{3,2,1,0:T(8,128)(2,1)} %bitcast.15), custom_call_target="tpu_custom_call" | custom-call | tf_op jit(solution)/shard_map/pallas_call | solution.py:267
  49.9 0.0 copy-start.3
  49.9 12.5 %all-to-all-start = ((bf16[128,256,128]{2,1,0:T(8,128)(2,1)}), bf16[128,256,128]{2,1,0:T(8,128)(2,1)}, u32[]{:S(2)}, u32[]{:S(2)}) async-start(bf16[128,256,128]{2,1,0:T(8,128)(2,1)} %shard_map.55), calls=%async_computation | async-start | bytes 16777216 | tf_op jit(solution)/shard_map/all_to_all | solution.py:927
  62.4 8.5 %shard_map.56.tab = s32[96]{0:T(128)} custom-call(s32[4,64]{1,0:T(4,128)} %map_ref.2), custom_call_target="tpu_custom_call" | custom-call | flops 20000 | bytes 2048 | tf_op jit(solution)/shard_map/pallas_call | solution.py:63
  71.0 0.0 copy-done.3
  71.0 0.1 concatenate.6
  71.0 0.1 reshape.30
  71.1 0.1 reshape.29
  71.2 3.1 %slice.4 = bf16[16,128,1,128]{3,2,1,0:T(2,128)(2,1)S(1)} slice(bf16[16,128,8,128]{3,2,1,0:T(8,128)(2,1)} %bitcast.11), slice={[0:16], [0:128], [0:1], [0:128]} | slice | bytes 1048576 | tf_op jit(solution)/shard_map/slice | solution.py:938
  74.3 0.1 copy.10
  74.4 0.2 dynamic-slice_reduce_fusion.1
  74.6 0.2 dynamic-slice_reduce_fusion
  74.8 0.1 pad_maximum_fusion.keep_ref
  74.9 87.7 %all-to-all-done = bf16[128,256,128]{2,1,0:T(8,128)(2,1)} async-done(((bf16[128,256,128]{2,1,0:T(8,128)(2,1)}), bf16[128,256,128]{2,1,0:T(8,128)(2,1)}, u32[]{:S(2)}, u32[]{:S(2)}) %all-to-all-start) | async-done | bytes 8388640 | tf_op jit(solution)/shard_map/all_to_all | solution.py:927
  162.5 0.0 copy-start.1
  162.5 0.7 copy-done.1
  163.2 0.0 copy-start
  163.2 0.0 copy-start.2
  163.2 2.3 shard_map.57
  165.5 96.1 %shard_map.58 = (bf16[2048,1024]{1,0:T(8,128)(2,1)S(1)}, bf16[1024,1024]{1,0:T(8,128)(2,1)S(1)}, f32[16,128,128]{2,1,0:T(8,128)S(1)}) custom-call(bf16[8,2,128,128]{3,2,1,0:T(8,128)(2,1)S(1)} %bitcast.14, f32[24]{0:T(128)S(1)} %pad_maximum_fusion.keep_ref), custom_call_target="tpu_custom_call" | custom-call | tf_op jit(solution)/shard_map/pallas_call | solution.py:865
  261.6 0.0 copy-done
  261.6 0.0 copy-done.2
  261.6 14.0 %shard_map.59 = f32[16,128,8,128]{3,2,1,0:T(8,128)} custom-call(s32[96]{0:T(128)S(1)} %copy-done.2, bf16[16,128,8,128]{3,2,1,0:T(8,128)(2,1)S(1)} %bitcast.12, bf16[256,128,128]{2,1,0:T(8,128)(2,1)} %bitcast.3.arrived, bf16[2048,1024]{1,0:T(8,128)(2,1)S(1)} %get-tuple-element.12.below, bf16[1024,1024]{1,0:T(8,128)(2,1)S(1)} %get-tuple-element.13.panel, ...), custom_call_target="tpu_custom_call" | custom-call | tf_op jit(solution)/shard_map/pallas_call | solution.py:904
  (1 shorter events, 0.0 us)
Async XLA Ops:
  49.9 21.1 %copy-start.3 = (s32[120]{0:T(128)S(1)}, s32[120]{0:T(128)}, u32[]{:S(2)}) copy-start(s32[120]{0:T(128)} %param.8) | copy-start | bytes 1444
  49.9 112.6 %all-to-all-start = ((bf16[128,256,128]{2,1,0:T(8,128)(2,1)}), bf16[128,256,128]{2,1,0:T(8,128)(2,1)}, u32[]{:S(2)}, u32[]{:S(2)}) async-start(bf16[128,256,128]{2,1,0:T(8,128)(2,1)} %shard_map.55), calls=%async_computation | async-start | bytes 16777216 | tf_op jit(solution)/shard_map/all_to_all | solution.py:927
  162.5 0.7 copy-start.1
  163.2 98.4 %copy-start = (bf16[1,16,128,1,8,128]{5,4,3,2,1,0:T(8,128)(2,1)S(1)}, bf16[1,16,128,1,8,128]{5,4,3,2,1,0:T(8,128)(2,1)}, u32[]{:S(2)}) copy-start(bf16[1,16,128,1,8,128]{5,4,3,2,1,0:T(8,128)(2,1)} %param.9) | copy-start | bytes 12582916
  163.2 98.4 %copy-start.2 = (s32[96]{0:T(128)S(1)}, s32[96]{0:T(128)}, u32[]{:S(2)}) copy-start(s32[96]{0:T(128)} %shard_map.56.tab) | copy-start | bytes 1156
